TPU v7x, 32 devices: a whole 2x2x4 slice. The times are simulated.
32 devices in a mesh: dp: 8 (over y, x, core), tensor: 4 (over z).
Axes of the slice: x: 2, y: 2, z: 4, core: 2. Of those that a mesh axis runs over, the one named last changes fastest.
Arguments:
- inputs: bfloat16 [2, 8, 1024, 1024], P(None, 'dp', 'tensor'), may hold values from -6 to 6
- segment_ids: int32 [2, 8, 1024], P(None, 'dp'), may hold values from 0 to 2, never falling along the last dimension, each value on 1 to 512 neighbouring positions
- norm1_gain: bfloat16 [2, 1024], P(None, 'dp'), may hold values from 0.099609375 to 1.8984375
- norm1_shift: bfloat16 [2, 1024], P(None, 'dp'), may hold values from -1.25 to 1.25
- w_query: bfloat16 [2, 1024, 1024], P(None, 'dp', 'tensor'), may hold values from -0.1875 to 0.1875
- w_key: bfloat16 [2, 1024, 1024], P(None, 'dp', 'tensor'), may hold values from -0.1875 to 0.1875
- w_value: bfloat16 [2, 1024, 1024], P(None, 'dp', 'tensor'), may hold values from -0.1875 to 0.1875
- w_output: bfloat16 [2, 1024, 1024], P(None, 'tensor', 'dp'), may hold values from -2.5 to 2.5
- norm2_gain: bfloat16 [2, 1024], P(None, 'dp'), may hold values from 0.099609375 to 1.8984375
- norm2_shift: bfloat16 [2, 1024], P(None, 'dp'), may hold values from -1.25 to 1.25
- w_fc_in: bfloat16 [2, 1024, 4096], P(None, 'dp', 'tensor'), may hold values from -0.1875 to 0.1875
- w_fc_out: bfloat16 [2, 4096, 1024], P(None, 'tensor', 'dp'), may hold values from -0.09375 to 0.09375
- cotangent: bfloat16 [2, 8, 1024, 1024], P(None, 'dp', 'tensor'), may hold values from -6 to 6
Outputs:
- block_output: float32 [2, 8, 1024, 1024], P(None, 'dp', 'tensor')
- input_grad: float32 [2, 8, 1024, 1024], P(None, 'dp', 'tensor')
- grad_norm1_gain: float32 [2, 1024], P(None, 'dp')
- grad_norm1_shift: float32 [2, 1024], P(None, 'dp')
- grad_w_query: float32 [2, 1024, 1024], P(None, 'dp', 'tensor')
- grad_w_key: float32 [2, 1024, 1024], P(None, 'dp', 'tensor')
- grad_w_value: float32 [2, 1024, 1024], P(None, 'dp', 'tensor')
- grad_w_output: float32 [2, 1024, 1024], P(None, 'tensor', 'dp')
- grad_norm2_gain: float32 [2, 1024], P(None, 'dp')
- grad_norm2_shift: float32 [2, 1024], P(None, 'dp')
- grad_w_fc_in: float32 [2, 1024, 4096], P(None, 'dp', 'tensor')
- grad_w_fc_out: float32 [2, 4096, 1024], P(None, 'tensor', 'dp')
Inputs may be any that keep to these rules, and one draw needn't show every extreme that they name: `segment_ids`: along each sequence the ids never fall; each of the three scenes of a sequence is one run of 1 to 512 tokens.
All inputs are finite; a program needn't handle non-finite values.
Results may differ from a plain program's by a relative error of at most 0.023.
Values may be sent and summed in bfloat16 or wider, within the bound.
A program may use at most 320 MiB of HBM per device.

v0:
```python
from functools import partial
import math

import jax
import jax.numpy as jnp
from jax import lax
from jax.sharding import PartitionSpec as P

D = 1024
HEADS = 16


float_type = jnp.float32
brain_type = jnp.bfloat16


def layer_norm(token_rows, gain_vec, shift_vec):
    center = token_rows - jnp.mean(token_rows, axis=-1, keepdims=True)
    spread = jnp.mean(center * center, axis=-1, keepdims=True)
    return center * lax.rsqrt(spread + 1e-05) * gain_vec + shift_vec


def normed_local(token_rows, gain_vec, shift_vec):
    return layer_norm(token_rows, gain_vec.astype(float_type), shift_vec.astype(float_type)).astype(
        brain_type
    )


def normed_send(token_rows, gain_vec, shift_vec):
    return lax.all_gather(
        normed_local(token_rows, gain_vec, shift_vec), "tensor", axis=0, tiled=True
    )


def normed_resend(token_rows, gain_vec, shift_vec):
    return lax.all_gather(
        normed_local(token_rows, gain_vec, shift_vec), "tensor", axis=0, tiled=True
    )


def branch_total(partial_sum):
    return lax.psum_scatter(
        partial_sum.astype(jnp.bfloat16), "tensor", scatter_dimension=0, tiled=True
    ).astype(jnp.float32)


def branch_cotangent(grad_rows):
    return lax.all_gather(grad_rows.astype(brain_type), "tensor", axis=0, tiled=True)


def input_total(partial_sum):
    return lax.psum_scatter(
        partial_sum.astype(jnp.bfloat16), "tensor", scatter_dimension=0, tiled=True
    ).astype(jnp.float32)


def norm_backward(token_rows, gain_vec, shift_vec, grad_normed):
    _, norm_pull = jax.vjp(
        layer_norm, token_rows, gain_vec.astype(float_type), shift_vec.astype(float_type)
    )
    return norm_pull(grad_normed)


def masked_scores(query_part, segment_part, key_heads, segment, score_scale):
    raw_scores = jnp.einsum(
        "qhd,khd->hqk", query_part, key_heads, preferred_element_type=float_type
    )
    same_scene = segment_part[:, None] == segment[None, :]
    return jnp.where(same_scene[None], raw_scores * score_scale, -1e30)


def attend_forward(queries, key_heads, values, segment, block_rows):
    seq_len, head_count, head_width = queries.shape
    score_scale = 1.0 / math.sqrt(head_width)
    block_count = seq_len // block_rows

    def one_block(block_pair):
        query_part, segment_part = block_pair
        scores = masked_scores(query_part, segment_part, key_heads, segment, score_scale)
        row_max = jnp.max(scores, axis=-1, keepdims=True)
        exp_scores = jnp.exp(scores - row_max)
        row_total = jnp.sum(exp_scores, axis=-1, keepdims=True)
        probabilities = (exp_scores / row_total).astype(brain_type)
        block_out = jnp.einsum(
            "hqk,khd->qhd", probabilities, values, preferred_element_type=float_type
        )
        log_total = (row_max + jnp.log(row_total))[..., 0]
        return (block_out.astype(brain_type), log_total)

    query_blocks = queries.reshape(block_count, block_rows, head_count, head_width)
    segment_blocks = segment.reshape(block_count, block_rows)
    outputs, log_totals = lax.map(one_block, (query_blocks, segment_blocks))
    return (outputs.reshape(seq_len, head_count * head_width), log_totals)


def attend_backward(queries, key_heads, values, segment, log_totals, grad_out, block_rows):
    seq_len, head_count, head_width = queries.shape
    score_scale = 1.0 / math.sqrt(head_width)
    block_count = seq_len // block_rows

    def one_block(carry_pair, block_items):
        grad_keys, grad_values = carry_pair
        query_part, segment_part, log_part, grad_part = block_items
        scores = masked_scores(query_part, segment_part, key_heads, segment, score_scale)
        probabilities = jnp.exp(scores - log_part[..., None])
        grad_probs = jnp.einsum(
            "qhd,khd->hqk", grad_part, values, preferred_element_type=float_type
        )
        row_inner = jnp.sum(probabilities * grad_probs, axis=-1, keepdims=True)
        grad_raw = (probabilities * (grad_probs - row_inner) * score_scale).astype(brain_type)
        grad_query = jnp.einsum(
            "hqk,khd->qhd", grad_raw, key_heads, preferred_element_type=float_type
        )
        grad_keys = grad_keys + jnp.einsum(
            "hqk,qhd->khd", grad_raw, query_part, preferred_element_type=float_type
        )
        grad_values = grad_values + jnp.einsum(
            "hqk,qhd->khd",
            probabilities.astype(brain_type),
            grad_part,
            preferred_element_type=float_type,
        )
        return ((grad_keys, grad_values), grad_query.astype(brain_type))

    zero_heads = jnp.zeros((seq_len, head_count, head_width), float_type)
    block_items = (
        queries.reshape(block_count, block_rows, head_count, head_width),
        segment.reshape(block_count, block_rows),
        log_totals,
        grad_out.reshape(block_count, block_rows, head_count, head_width),
    )
    (grad_keys, grad_values), grad_queries = lax.scan(
        one_block, (zero_heads, zero_heads), block_items
    )
    flat_shape = (seq_len, head_count * head_width)
    return (
        grad_queries.reshape(flat_shape),
        grad_keys.astype(brain_type).reshape(flat_shape),
        grad_values.astype(brain_type).reshape(flat_shape),
    )


def fresh_totals(layers, attn_width, hidden_width):
    vector_zero = jnp.zeros((layers, D), float_type)
    column_zero = jnp.zeros((layers, D, attn_width), float_type)
    return [
        vector_zero,
        vector_zero,
        column_zero,
        column_zero,
        column_zero,
        jnp.zeros((layers, attn_width, D), float_type),
        vector_zero,
        vector_zero,
        jnp.zeros((layers, D, hidden_width), float_type),
        jnp.zeros((layers, hidden_width, D), float_type),
    ]


def add_into(grad_totals, position, layer_index, term):
    grad_totals[position] = grad_totals[position].at[layer_index].add(term)


def per_device(
    inputs,
    segment_ids,
    norm1_gain,
    norm1_shift,
    w_query,
    w_key,
    w_value,
    w_output,
    norm2_gain,
    norm2_shift,
    w_fc_in,
    w_fc_out,
    cotangent,
):
    micro_count = inputs.shape[0]
    layers = norm1_gain.shape[0]
    seq_len = segment_ids.shape[2]
    block_rows = min(512, seq_len)
    head_width = D // HEADS
    attn_width = w_query.shape[2]
    hidden_width = w_fc_in.shape[2]
    grad_totals = fresh_totals(layers, attn_width, hidden_width)
    reduced = None
    output_list = []
    input_grad_list = []
    for micro_index in range(micro_count):
        token_rows = inputs[micro_index, 0].astype(float_type)
        segment = segment_ids[micro_index, 0]
        saved_state = []
        for layer_index in range(layers):
            weights = (
                lax.all_gather(norm1_gain[layer_index], "dp", axis=0, tiled=True),
                lax.all_gather(norm1_shift[layer_index], "dp", axis=0, tiled=True),
                lax.all_gather(w_query[layer_index], "dp", axis=0, tiled=True),
                lax.all_gather(w_key[layer_index], "dp", axis=0, tiled=True),
                lax.all_gather(w_value[layer_index], "dp", axis=0, tiled=True),
                lax.all_gather(w_output[layer_index], "dp", axis=1, tiled=True),
                lax.all_gather(norm2_gain[layer_index], "dp", axis=0, tiled=True),
                lax.all_gather(norm2_shift[layer_index], "dp", axis=0, tiled=True),
                lax.all_gather(w_fc_in[layer_index], "dp", axis=0, tiled=True),
                lax.all_gather(w_fc_out[layer_index], "dp", axis=1, tiled=True),
            )
            (
                gain_one,
                shift_one,
                query_w,
                key_w,
                value_w,
                output_w,
                gain_two,
                shift_two,
                fc_in_w,
                fc_out_w,
            ) = weights
            whole_weights = None
            normed = normed_send(token_rows, gain_one, shift_one)
            queries = jnp.dot(normed, query_w, preferred_element_type=float_type).astype(brain_type)
            key_heads = jnp.dot(normed, key_w, preferred_element_type=float_type).astype(brain_type)
            values = jnp.dot(normed, value_w, preferred_element_type=float_type).astype(brain_type)
            attended, log_totals = attend_forward(
                queries.reshape(seq_len, -1, head_width),
                key_heads.reshape(seq_len, -1, head_width),
                values.reshape(seq_len, -1, head_width),
                segment,
                block_rows,
            )
            mid_rows = token_rows + branch_total(
                jnp.dot(attended, output_w, preferred_element_type=float_type)
            )
            normed_two = normed_send(mid_rows, gain_two, shift_two)
            pre_act = jnp.dot(normed_two, fc_in_w, preferred_element_type=float_type)
            hidden = jax.nn.gelu(pre_act, approximate=False).astype(brain_type)
            next_rows = mid_rows + branch_total(
                jnp.dot(hidden, fc_out_w, preferred_element_type=float_type)
            )
            saved_state.append(
                (
                    token_rows,
                    mid_rows,
                    weights,
                    normed,
                    normed_two,
                    queries,
                    key_heads,
                    values,
                    attended,
                    log_totals,
                    pre_act,
                    hidden,
                    whole_weights,
                )
            )
            token_rows = next_rows
        output_list.append(token_rows)
        grad_rows = cotangent[micro_index, 0].astype(float_type)
        for layer_index in reversed(range(layers)):
            (
                layer_rows,
                mid_rows,
                weights,
                normed,
                normed_two,
                queries,
                key_heads,
                values,
                attended,
                log_totals,
                pre_act,
                hidden,
                whole_weights,
            ) = saved_state[layer_index]
            weights = (
                lax.all_gather(norm1_gain[layer_index], "dp", axis=0, tiled=True),
                lax.all_gather(norm1_shift[layer_index], "dp", axis=0, tiled=True),
                lax.all_gather(w_query[layer_index], "dp", axis=0, tiled=True),
                lax.all_gather(w_key[layer_index], "dp", axis=0, tiled=True),
                lax.all_gather(w_value[layer_index], "dp", axis=0, tiled=True),
                lax.all_gather(w_output[layer_index], "dp", axis=1, tiled=True),
                lax.all_gather(norm2_gain[layer_index], "dp", axis=0, tiled=True),
                lax.all_gather(norm2_shift[layer_index], "dp", axis=0, tiled=True),
                lax.all_gather(w_fc_in[layer_index], "dp", axis=0, tiled=True),
                lax.all_gather(w_fc_out[layer_index], "dp", axis=1, tiled=True),
            )
            (
                gain_one,
                shift_one,
                query_w,
                key_w,
                value_w,
                output_w,
                gain_two,
                shift_two,
                fc_in_w,
                fc_out_w,
            ) = weights
            normed = normed_resend(layer_rows, gain_one, shift_one)
            normed_two = normed_resend(mid_rows, gain_two, shift_two)
            grad_branch = branch_cotangent(grad_rows)
            add_into(
                grad_totals,
                9,
                layer_index,
                jnp.einsum("sf,sd->fd", hidden, grad_branch, preferred_element_type=float_type),
            )
            grad_hidden = jnp.einsum(
                "sd,fd->sf", grad_branch, fc_out_w, preferred_element_type=float_type
            )
            _, gelu_pull = jax.vjp(partial(jax.nn.gelu, approximate=False), pre_act)
            grad_pre = gelu_pull(grad_hidden)[0].astype(brain_type)
            add_into(
                grad_totals,
                8,
                layer_index,
                jnp.einsum("sd,sf->df", normed_two, grad_pre, preferred_element_type=float_type),
            )
            grad_normed = input_total(
                jnp.einsum("sf,df->sd", grad_pre, fc_in_w, preferred_element_type=float_type)
            )
            grad_mid_part, grad_gain, grad_shift = norm_backward(
                mid_rows, gain_two, shift_two, grad_normed
            )
            add_into(grad_totals, 6, layer_index, grad_gain)
            add_into(grad_totals, 7, layer_index, grad_shift)
            grad_mid = grad_rows + grad_mid_part
            grad_branch = branch_cotangent(grad_mid)
            add_into(
                grad_totals,
                5,
                layer_index,
                jnp.einsum("sa,sd->ad", attended, grad_branch, preferred_element_type=float_type),
            )
            grad_attended = jnp.einsum(
                "sd,ad->sa", grad_branch, output_w, preferred_element_type=float_type
            ).astype(brain_type)
            grad_queries, grad_keys, grad_values = attend_backward(
                queries.reshape(seq_len, -1, head_width),
                key_heads.reshape(seq_len, -1, head_width),
                values.reshape(seq_len, -1, head_width),
                segment,
                log_totals,
                grad_attended.reshape(seq_len, -1, head_width),
                block_rows,
            )
            add_into(
                grad_totals,
                2,
                layer_index,
                jnp.einsum("sd,sa->da", normed, grad_queries, preferred_element_type=float_type),
            )
            add_into(
                grad_totals,
                3,
                layer_index,
                jnp.einsum("sd,sa->da", normed, grad_keys, preferred_element_type=float_type),
            )
            add_into(
                grad_totals,
                4,
                layer_index,
                jnp.einsum("sd,sa->da", normed, grad_values, preferred_element_type=float_type),
            )
            grad_input_part = jnp.einsum(
                "sa,da->sd", grad_queries, query_w, preferred_element_type=float_type
            )
            grad_input_part = grad_input_part + jnp.einsum(
                "sa,da->sd", grad_keys, key_w, preferred_element_type=float_type
            )
            grad_input_part = grad_input_part + jnp.einsum(
                "sa,da->sd", grad_values, value_w, preferred_element_type=float_type
            )
            grad_normed = input_total(grad_input_part)
            grad_below, grad_gain, grad_shift = norm_backward(
                layer_rows, gain_one, shift_one, grad_normed
            )
            add_into(grad_totals, 0, layer_index, grad_gain)
            add_into(grad_totals, 1, layer_index, grad_shift)
            grad_rows = grad_mid + grad_below
        input_grad_list.append(grad_rows)
    reduced = (
        lax.psum_scatter(
            grad_totals[0].astype(jnp.bfloat16), "dp", scatter_dimension=1, tiled=True
        ).astype(jnp.float32),
        lax.psum_scatter(
            grad_totals[1].astype(jnp.bfloat16), "dp", scatter_dimension=1, tiled=True
        ).astype(jnp.float32),
        lax.psum_scatter(
            grad_totals[2].astype(jnp.bfloat16), "dp", scatter_dimension=1, tiled=True
        ).astype(jnp.float32),
        lax.psum_scatter(
            grad_totals[3].astype(jnp.bfloat16), "dp", scatter_dimension=1, tiled=True
        ).astype(jnp.float32),
        lax.psum_scatter(
            grad_totals[4].astype(jnp.bfloat16), "dp", scatter_dimension=1, tiled=True
        ).astype(jnp.float32),
        lax.psum_scatter(
            grad_totals[5].astype(jnp.bfloat16), "dp", scatter_dimension=2, tiled=True
        ).astype(jnp.float32),
        lax.psum_scatter(
            grad_totals[6].astype(jnp.bfloat16), "dp", scatter_dimension=1, tiled=True
        ).astype(jnp.float32),
        lax.psum_scatter(
            grad_totals[7].astype(jnp.bfloat16), "dp", scatter_dimension=1, tiled=True
        ).astype(jnp.float32),
        lax.psum_scatter(
            grad_totals[8].astype(jnp.bfloat16), "dp", scatter_dimension=1, tiled=True
        ).astype(jnp.float32),
        lax.psum_scatter(
            grad_totals[9].astype(jnp.bfloat16), "dp", scatter_dimension=2, tiled=True
        ).astype(jnp.float32),
    )
    norm_sums = lax.psum((reduced[0], reduced[1], reduced[6], reduced[7]), "tensor")
    block_output = jnp.stack(output_list)[:, None]
    input_grad = jnp.stack(input_grad_list)[:, None]
    return (
        block_output,
        input_grad,
        norm_sums[0],
        norm_sums[1],
        reduced[2],
        reduced[3],
        reduced[4],
        reduced[5],
        norm_sums[2],
        norm_sums[3],
        reduced[8],
        reduced[9],
    )


def solution(mesh):
    placed = (
        P(None, "dp", "tensor", None),
        P(None, "dp", None),
        P(None, "dp"),
        P(None, "dp"),
        P(None, "dp", "tensor"),
        P(None, "dp", "tensor"),
        P(None, "dp", "tensor"),
        P(None, "tensor", "dp"),
        P(None, "dp"),
        P(None, "dp"),
        P(None, "dp", "tensor"),
        P(None, "tensor", "dp"),
        P(None, "dp", "tensor", None),
    )
    return jax.shard_map(
        per_device,
        mesh=mesh,
        in_specs=placed,
        out_specs=(
            P(None, "dp", "tensor", None),
            P(None, "dp", "tensor", None),
            P(None, "dp"),
            P(None, "dp"),
            P(None, "dp", "tensor"),
            P(None, "dp", "tensor"),
            P(None, "dp", "tensor"),
            P(None, "tensor", "dp"),
            P(None, "dp"),
            P(None, "dp"),
            P(None, "dp", "tensor"),
            P(None, "tensor", "dp"),
        ),
        check_vma=False,
    )
```

profile of v0, /device:TPU:0, one launch (start us, length us, event | category | flops | bytes accessed | tf_op | source)
XLA Modules:
  0.0 2246.7 jit_solution(188920313976740745)
XLA Ops:
  115.5 42.7 %reduce-scatter.39.cloned.1.call-done = bf16[256,1024]{1,0:T(8,128)(2,1)} async-done(((bf16[1024,1024]{1,0:T(8,128)(2,1)}), bf16[256,1024]{1,0:T(8,128)(2,1)}) %reduce-scatter.39.cloned.1.call-update) | async-done | bytes 524304 | tf_op jit(solution)/shard_map/reduce_scatter | solution.py:42
  161.5 45.1 %all-gather.51.cloned.1.call-done = bf16[1024,1024]{1,0:T(8,128)(2,1)} async-done(((bf16[256,1024]{1,0:T(8,128)(2,1)}), bf16[1024,1024]{1,0:T(8,128)(2,1)}) %all-gather.51.cloned.1.call-update) | async-done | bytes 2097168 | tf_op jit(solution)/shard_map/all_gather | solution.py:30
  289.6 42.8 %all-gather.45.cloned.1.call-done = bf16[1024,1024]{1,0:T(8,128)(2,1)} async-done(((bf16[256,1024]{1,0:T(8,128)(2,1)}), bf16[1024,1024]{1,0:T(8,128)(2,1)}) %all-gather.45.cloned.1.call-update) | async-done | bytes 2097168 | tf_op jit(solution)/shard_map/all_gather | solution.py:30
  367.6 41.8 %all-gather.53.cloned.1.call-done = bf16[1024,1024]{1,0:T(8,128)(2,1)} async-done(((bf16[256,1024]{1,0:T(8,128)(2,1)}), bf16[1024,1024]{1,0:T(8,128)(2,1)}) %all-gather.53.cloned.1.call-update) | async-done | bytes 2097168 | tf_op jit(solution)/shard_map/all_gather | solution.py:30
  454.6 45.1 %reduce-scatter.49.cloned.1.call-done = bf16[256,1024]{1,0:T(8,128)(2,1)} async-done(((bf16[1024,1024]{1,0:T(8,128)(2,1)}), bf16[256,1024]{1,0:T(8,128)(2,1)}) %reduce-scatter.49.cloned.1.call-update) | async-done | bytes 524304 | tf_op jit(solution)/shard_map/reduce_scatter | solution.py:42
  650.1 37.0 %reduce-scatter.43.cloned.1.call-done = bf16[256,1024]{1,0:T(8,128)(2,1)} async-done(((bf16[1024,1024]{1,0:T(8,128)(2,1)}), bf16[256,1024]{1,0:T(8,128)(2,1)}) %reduce-scatter.43.cloned.1.call-update) | async-done | bytes 524304 | tf_op jit(solution)/shard_map/reduce_scatter | solution.py:42
  695.6 40.1 %all-gather.57.cloned.1.call-done = bf16[1024,1024]{1,0:T(8,128)(2,1)} async-done(((bf16[256,1024]{1,0:T(8,128)(2,1)}), bf16[1024,1024]{1,0:T(8,128)(2,1)}) %all-gather.57.cloned.1.call-update) | async-done | bytes 2097168 | tf_op jit(solution)/shard_map/all_gather | solution.py:30
  824.4 57.0 %all-gather.49.cloned.1.call-done = bf16[1024,1024]{1,0:T(8,128)(2,1)} async-done(((bf16[256,1024]{1,0:T(8,128)(2,1)}), bf16[1024,1024]{1,0:T(8,128)(2,1)}) %all-gather.49.cloned.1.call-update) | async-done | bytes 2097168 | tf_op jit(solution)/shard_map/all_gather | solution.py:30
  986.2 42.9 %reduce-scatter.53.cloned.1.call-done = bf16[256,1024]{1,0:T(8,128)(2,1)} async-done(((bf16[1024,1024]{1,0:T(8,128)(2,1)}), bf16[256,1024]{1,0:T(8,128)(2,1)}) %reduce-scatter.53.cloned.1.call-update) | async-done | bytes 524304 | tf_op jit(solution)/shard_map/reduce_scatter | solution.py:42
  1029.1 45.5 %reduce-scatter.45.cloned.1.call-done = bf16[256,1024]{1,0:T(8,128)(2,1)} async-done(((bf16[1024,1024]{1,0:T(8,128)(2,1)}), bf16[256,1024]{1,0:T(8,128)(2,1)}) %reduce-scatter.45.cloned.1.call-update) | async-done | bytes 524304 | tf_op jit(solution)/shard_map/reduce_scatter | solution.py:42
  1082.6 44.2 %all-gather.65.cloned.1.call-done = bf16[1024,1024]{1,0:T(8,128)(2,1)} async-done(((bf16[256,1024]{1,0:T(8,128)(2,1)}), bf16[1024,1024]{1,0:T(8,128)(2,1)}) %all-gather.65.cloned.1.call-update) | async-done | bytes 2097168 | tf_op jit(solution)/shard_map/all_gather | solution.py:48
  1132.2 111.8 %while.154 = (s32[]{:T(128)}, f32[1024,4,64]{0,2,1:T(8,128)}, f32[1024,4,64]{0,2,1:T(8,128)}, bf16[2,512,4,64]{1,3,2,0:T(8,128)(2,1)S(1)}, bf16[2,512,4,64]{1,3,...) while((s32[]{:T(128)}, f32[1024,4,64]{0,2,1:T(8,128)}, ...), condition=%wide.region_63.64_spmd.clone, body=%wide.region_61.63_spmd.clone.sunk | while | flops 1398413312 | bytes 102567064 | solution.py:132
  1256.6 114.5 %while.152 = (s32[]{:T(128)}, f32[1024,4,64]{0,2,1:T(8,128)}, f32[1024,4,64]{0,2,1:T(8,128)}, bf16[2,512,4,64]{1,3,2,0:T(8,128)(2,1)}, bf16[2,512,4,64]{1,3,2,0:...) while((s32[]{:T(128)}, f32[1024,4,64]{0,2,1:T(8,128)}, ...), condition=%wide.region_45.46_spmd.clone, body=%wide.region_43.45_spmd.clone.sunk | while | flops 1398413312 | bytes 102567064 | solution.py:132
  1378.4 42.7 %reduce-scatter.57.cloned.1.call-done = bf16[256,1024]{1,0:T(8,128)(2,1)} async-done(((bf16[1024,1024]{1,0:T(8,128)(2,1)}), bf16[256,1024]{1,0:T(8,128)(2,1)}) %reduce-scatter.57.cloned.1.call-update) | async-done | bytes 524304 | tf_op jit(solution)/shard_map/reduce_scatter | solution.py:52
  1429.8 44.2 %all-gather.67.cloned.1.call-done = bf16[1024,1024]{1,0:T(8,128)(2,1)} async-done(((bf16[256,1024]{1,0:T(8,128)(2,1)}), bf16[1024,1024]{1,0:T(8,128)(2,1)}) %all-gather.67.cloned.1.call-update) | async-done | bytes 2097168 | tf_op jit(solution)/shard_map/all_gather | solution.py:48
  1487.7 55.7 %all-gather.61.cloned.1.call-done = bf16[1024,1024]{1,0:T(8,128)(2,1)} async-done(((bf16[256,1024]{1,0:T(8,128)(2,1)}), bf16[1024,1024]{1,0:T(8,128)(2,1)}) %all-gather.61.cloned.1.call-update) | async-done | bytes 2097168 | tf_op jit(solution)/shard_map/all_gather | solution.py:48
  1556.2 43.9 %reduce-scatter.59.cloned.1.call-done = bf16[256,1024]{1,0:T(8,128)(2,1)} async-done(((bf16[1024,1024]{1,0:T(8,128)(2,1)}), bf16[256,1024]{1,0:T(8,128)(2,1)}) %reduce-scatter.59.cloned.1.call-update) | async-done | bytes 524304 | tf_op jit(solution)/shard_map/reduce_scatter | solution.py:52
  1713.8 112.9 %while.153 = (s32[]{:T(128)}, f32[1024,4,64]{0,2,1:T(8,128)}, f32[1024,4,64]{0,2,1:T(8,128)}, bf16[2,512,4,64]{1,3,2,0:T(8,128)(2,1)}, bf16[2,512,4,64]{1,3,2,0:...) while((s32[]{:T(128)}, f32[1024,4,64]{0,2,1:T(8,128)}, ...), condition=%wide.region_54.55_spmd.clone, body=%wide.region_52.54_spmd.clone.sunk | while | flops 1398413312 | bytes 102567576 | solution.py:132
  1826.9 112.5 %while.155 = (s32[]{:T(128)}, f32[1024,4,64]{0,2,1:T(8,128)}, f32[1024,4,64]{0,2,1:T(8,128)}, bf16[2,512,4,64]{1,3,2,0:T(8,128)(2,1)S(1)}, bf16[2,512,4,64]{1,3,...) while((s32[]{:T(128)}, f32[1024,4,64]{0,2,1:T(8,128)}, ...), condition=%wide.region_72.73_spmd.clone, body=%wide.region_70.72_spmd.clone.sunk | while | flops 1398413312 | bytes 102567064 | solution.py:132
  1985.4 37.4 %reduce-scatter.73.cloned.1.call-done = bf16[2,128,256]{2,1,0:T(8,128)(2,1)} async-done(((bf16[2,1024,256]{2,1,0:T(8,128)(2,1)}), bf16[2,128,256]{2,1,0:T(8,128)(2,1)}) %reduce-scatter.73.cloned.1.call-update) | async-done | bytes 131088 | tf_op jit(solution)/shard_map/reduce_scatter | solution.py:393
  2024.4 37.5 %reduce-scatter.71.cloned.1.call-done = bf16[2,128,256]{2,1,0:T(8,128)(2,1)} async-done(((bf16[2,1024,256]{2,1,0:T(8,128)(2,1)}), bf16[2,128,256]{2,1,0:T(8,128)(2,1)}) %reduce-scatter.71.cloned.1.call-update) | async-done | bytes 131088 | tf_op jit(solution)/shard_map/reduce_scatter | solution.py:390
  2063.6 44.2 %reduce-scatter.69.cloned.1.call-done = bf16[256,1024]{1,0:T(8,128)(2,1)} async-done(((bf16[1024,1024]{1,0:T(8,128)(2,1)}), bf16[256,1024]{1,0:T(8,128)(2,1)}) %reduce-scatter.69.cloned.1.call-update) | async-done | bytes 524304 | tf_op jit(solution)/shard_map/reduce_scatter | solution.py:52
  2107.8 45.6 %reduce-scatter.61.cloned.1.call-done = bf16[256,1024]{1,0:T(8,128)(2,1)} async-done(((bf16[1024,1024]{1,0:T(8,128)(2,1)}), bf16[256,1024]{1,0:T(8,128)(2,1)}) %reduce-scatter.61.cloned.1.call-update) | async-done | bytes 524304 | tf_op jit(solution)/shard_map/reduce_scatter | solution.py:52
  2190.1 36.2 %reduce-scatter.79.cloned.1.call-done = bf16[128,2]{1,0:T(8,128)(2,1)} async-done(((bf16[1024,2]{1,0:T(8,128)(2,1)}), bf16[128,2]{1,0:T(8,128)(2,1)}) %reduce-scatter.79.cloned.1.call-update) | async-done | bytes 528
  (974 shorter events, 1420.9 us)
Async XLA Ops:
  34.5 123.7 %reduce-scatter.39.cloned.1.call-start = ((), (), s32[]{:S(2)}) async-start(), calls=%async_computation.27 | async-start | bytes 2621440 | tf_op jit(solution)/shard_map/reduce_scatter | solution.py:42
  288.4 121.0 %all-gather.53.cloned.1.call-start = ((), (), s32[]{:S(2)}) async-start(), calls=%async_computation.36 | async-start | bytes 2621440 | tf_op jit(solution)/shard_map/all_gather | solution.py:30
  289.2 165.4 %reduce-scatter.41.cloned.1.call-start = ((), (), s32[]{:S(2)}) async-start(), calls=%async_computation.29 | async-start | bytes 2621440 | tf_op jit(solution)/shard_map/reduce_scatter | solution.py:42
  367.5 132.2 %reduce-scatter.49.cloned.1.call-start = ((), (), s32[]{:S(2)}) async-start(), calls=%async_computation.37 | async-start | bytes 2621440 | tf_op jit(solution)/shard_map/reduce_scatter | solution.py:42
  693.8 187.6 %all-gather.49.cloned.1.call-start = ((), (), s32[]{:S(2)}) async-start(), calls=%async_computation.32 | async-start | bytes 2621440 | tf_op jit(solution)/shard_map/all_gather | solution.py:30
  694.4 233.1 %all-gather.79.cloned.1.call-start = ((), (), s32[]{:S(2)}) async-start(), calls=%async_computation.64 | async-start | bytes 2621440 | tf_op jit(solution)/shard_map/all_gather | solution.py:48
  695.1 258.1 %reduce-scatter.63.cloned.1.call-start = ((), (), s32[]{:S(2)}) async-start(), calls=%async_computation.49 | async-start | bytes 2621440 | tf_op jit(solution)/shard_map/reduce_scatter | solution.py:52
  824.2 159.4 %reduce-scatter.55.cloned.1.call-start = ((), (), s32[]{:S(2)}) async-start(), calls=%async_computation.42 | async-start | bytes 2621440 | tf_op jit(solution)/shard_map/reduce_scatter | solution.py:52
  946.7 127.8 %reduce-scatter.45.cloned.1.call-start = ((), (), s32[]{:S(2)}) async-start(), calls=%async_computation.33 | async-start | bytes 2621440 | tf_op jit(solution)/shard_map/reduce_scatter | solution.py:42
  952.8 174.0 %all-gather.65.cloned.1.call-start = ((), (), s32[]{:S(2)}) async-start(), calls=%async_computation.50 | async-start | bytes 2621440 | tf_op jit(solution)/shard_map/all_gather | solution.py:48
  1081.8 168.5 %all-gather.59.cloned.1.call-start = ((), (), s32[]{:S(2)}) async-start(), calls=%async_computation.43 | async-start | bytes 2621440 | tf_op jit(solution)/shard_map/all_gather | solution.py:48
  1082.6 295.9 %reduce-scatter.65.cloned.1.call-start = ((), (), s32[]{:S(2)}) async-start(), calls=%async_computation.51 | async-start | bytes 2621440 | tf_op jit(solution)/shard_map/reduce_scatter | solution.py:52
  1250.2 171.0 %reduce-scatter.57.cloned.1.call-start = ((), (), s32[]{:S(2)}) async-start(), calls=%async_computation.44 | async-start | bytes 2621440 | tf_op jit(solution)/shard_map/reduce_scatter | solution.py:52
  1429.7 126.5 %reduce-scatter.67.cloned.1.call-start = ((), (), s32[]{:S(2)}) async-start(), calls=%async_computation.53 | async-start | bytes 2621440 | tf_op jit(solution)/shard_map/reduce_scatter | solution.py:52
  1556.1 124.9 %all-gather.63.cloned.1.call-start = ((), (), s32[]{:S(2)}) async-start(), calls=%async_computation.47 | async-start | bytes 2621440 | tf_op jit(solution)/shard_map/all_gather | solution.py:48
  1610.0 363.8 %reduce-scatter.87.cloned.1.call-start = ((), (), s32[]{:S(2)}) async-start(), calls=%async_computation.70 | async-start | bytes 294912
  1627.5 347.2 %reduce-scatter.85.cloned.1.call-start = ((), (), s32[]{:S(2)}) async-start(), calls=%async_computation.69 | async-start | bytes 294912
  1628.6 346.9 %reduce-scatter.89.cloned.1.call-start = ((), (), s32[]{:S(2)}) async-start(), calls=%async_computation.71 | async-start | bytes 4718592
  1659.7 318.9 %reduce-scatter.77.cloned.1.call-start = ((), (), s32[]{:S(2)}) async-start(), calls=%async_computation.59 | async-start | bytes 4718592 | tf_op jit(solution)/shard_map/reduce_scatter | solution.py:408
  1680.7 300.2 %reduce-scatter.83.cloned.1.call-start = ((), (), s32[]{:S(2)}) async-start(), calls=%async_computation.68 | async-start | bytes 1179648
  1826.8 157.0 %reduce-scatter.75.cloned.1.call-start = ((), (), s32[]{:S(2)}) async-start(), calls=%async_computation.58 | async-start | bytes 1179648 | tf_op jit(solution)/shard_map/reduce_scatter | solution.py:396
  1964.3 143.6 %reduce-scatter.69.cloned.1.call-start = ((), (), s32[]{:S(2)}) async-start(), calls=%async_computation.55 | async-start | bytes 2621440 | tf_op jit(solution)/shard_map/reduce_scatter | solution.py:52
  1968.2 185.2 %reduce-scatter.61.cloned.1.call-start = ((), (), s32[]{:S(2)}) async-start(), calls=%async_computation.48 | async-start | bytes 2621440 | tf_op jit(solution)/shard_map/reduce_scatter | solution.py:52
  1972.1 217.1 %reduce-scatter.81.cloned.1.call-start = ((), (), s32[]{:S(2)}) async-start(), calls=%async_computation.67 | async-start | bytes 294912
  (246 other events, 9209.9 us)
Sparse Core Ops, SparseCore 0:
  34.6 46.2 all-gather.42
  115.6 42.5 reduce-scatter.38
  161.3 45.2 all-gather.50
  239.4 42.5 reduce-scatter.46
  504.1 45.1 all-gather.54
  551.3 44.6 all-gather.46
  598.3 42.5 reduce-scatter.50
  643.9 43.1 reduce-scatter.42
  824.3 68.4 reduce-scatter.62
  940.9 42.6 reduce-scatter.54
  985.9 43.1 reduce-scatter.52
  1031.4 43.1 reduce-scatter.44
  1250.2 42.6 reduce-scatter.64
  1378.5 42.6 reduce-scatter.56
  1487.3 67.2 reduce-scatter.66
  1556.9 43.0 reduce-scatter.58
Sparse Core Ops, SparseCore 1:
  287.6 44.8 all-gather.44
  363.8 45.5 all-gather.52
  412.3 42.3 reduce-scatter.40
  457.0 42.7 reduce-scatter.48
  690.8 44.8 all-gather.56
  737.2 44.4 all-gather.80
  813.0 68.3 all-gather.48
  883.1 44.4 all-gather.78
  1081.9 44.9 all-gather.64
  1128.4 44.3 all-gather.58
  1429.0 44.9 all-gather.66
  1476.1 67.1 all-gather.60
  1607.8 44.9 all-gather.62
  1654.3 44.3 all-gather.68
  1738.6 33.7 reduce-scatter.84
  1775.6 51.3 reduce-scatter.88
  1830.6 51.3 reduce-scatter.76
  1885.0 35.9 reduce-scatter.82
  1949.0 34.8 reduce-scatter.74
  1986.9 35.9 reduce-scatter.72
  2026.0 35.9 reduce-scatter.70
  2064.3 43.5 reduce-scatter.68
  2110.6 42.7 reduce-scatter.60
  2192.6 33.6 reduce-scatter.78
  (6 shorter events, 171.6 us)
where the time goes:
time: 2250 us
  waiting for transfers between devices  1110 us (49%)
  matrix products  730 us (32%)
  blocking collectives  163 us (7%)
  other arithmetic  117 us (5%)
  local copies, waits for them, and re-layouts  103 us (5%)
    all_gather x8, waiting for transfers between devices, normed_send(): lax.all_gather(normed_local(token_rows, gain_vec, shift_vec), 'tensor', a...  251 us
    reduce_scatter x8, waiting for transfers between devices, branch_total(): lax.psum_scatter(partial_sum.astype(jnp.bfloat16), 'tensor', scatter_dime...  243 us
    all_gather x8, waiting for transfers between devices, branch_cotangent(): lax.all_gather(grad_rows.astype(brain_type), 'tensor', axis=0, tiled=True)  219 us
    reduce_scatter x8, waiting for transfers between devices, input_total(): lax.psum_scatter(partial_sum.astype(jnp.bfloat16), 'tensor', scatter_dime...  207 us
    dot_general x8, matrix products, one_block(): jnp.einsum('hqk,qhd->khd', grad_raw, query_part, preferred_element_type=f...  178 us
    dot_general x8, matrix products, one_block(): jnp.einsum('hqk,khd->qhd', grad_raw, key_heads, preferred_element_type=fl...  140 us
    unnamed x52, waiting for transfers between devices  66.7 us
    unnamed x468, local copies, waits for them, and re-layouts  59 us
  transfers between devices with their start and end apart: 46, of which 33 were waited for; matrix products, arithmetic and copies ran while one was open for 37% of the time, Pallas kernels for 0%

commit v1 on v0

--- a/solution.py
+++ b/solution.py
@@ -4,14 +4,781 @@
 import jax
 import jax.numpy as jnp
 from jax import lax
+from jax.experimental import pallas as pl
+from jax.experimental.pallas import tpu as pltpu
 from jax.sharding import PartitionSpec as P
 
 D = 1024
 HEADS = 16
-
-
 float_type = jnp.float32
 brain_type = jnp.bfloat16
+CORE, XBIT, YBIT = 1, 2, 4
+ZLOW, ZHIGH = 1, 2
+
+
+def swap(block, axis_name, bit):
+    size = lax.axis_size(axis_name)
+    return lax.ppermute(block, axis_name, [(i, i ^ bit) for i in range(size)])
+
+
+def after(block, earlier):
+    return lax.optimization_barrier((block, earlier))[0]
+
+
+def pick(flag, when_zero, when_one):
+    return jnp.where(flag == 0, when_zero, when_one)
+
+
+def tn_low(left, right):
+    return tn(left, right).astype(brain_type)
+
+
+def nt(left, right):
+    return lax.dot_general(left, right, (((1,), (1,)), ((), ())), preferred_element_type=float_type)
+
+
+def nn(left, right):
+    return lax.dot_general(left, right, (((1,), (0,)), ((), ())), preferred_element_type=float_type)
+
+
+def tn(left, right):
+    return lax.dot_general(left, right, (((0,), (0,)), ((), ())), preferred_element_type=float_type)
+
+
+def attend_kernel(score_scale, qkv_ref, seg_col_ref, seg_row_ref, out_ref):
+    seq_len = qkv_ref.shape[0]
+    rows = 256
+    keys = qkv_ref[:, 128:256]
+    values = qkv_ref[:, 256:384]
+    low_lane = lax.broadcasted_iota(jnp.int32, (rows, 128), 1) < 64
+    for part in range(seq_len // rows):
+        span = slice(part * rows, (part + 1) * rows)
+        query = qkv_ref[span, :128]
+        same = seg_col_ref[span, :] == seg_row_ref[...]
+        outs = []
+        for head in range(2):
+            mine = low_lane if head == 0 else jnp.logical_not(low_lane)
+            masked = jnp.where(mine, query, jnp.zeros_like(query))
+            scores = jnp.where(same, nt(masked, keys) * score_scale, -1e30)
+            top = jnp.max(scores, axis=1, keepdims=True)
+            weight = jnp.exp(scores - top)
+            total = jnp.sum(weight, axis=1, keepdims=True)
+            probs = (weight * (1.0 / total)).astype(brain_type)
+            outs.append(nn(probs, values))
+        out_ref[span, :] = jnp.where(low_lane, outs[0], outs[1]).astype(brain_type)
+
+
+def attend(qkv, segment, score_scale):
+    seq_len, width = qkv.shape
+    blocks = width // 384
+    return pl.pallas_call(
+        partial(attend_kernel, score_scale),
+        grid=(blocks,),
+        in_specs=[
+            pl.BlockSpec((seq_len, 384), lambda i: (0, i)),
+            pl.BlockSpec((seq_len, 1), lambda i: (0, 0)),
+            pl.BlockSpec((1, seq_len), lambda i: (0, 0)),
+        ],
+        out_specs=pl.BlockSpec((seq_len, 128), lambda i: (0, i)),
+        out_shape=jax.ShapeDtypeStruct((seq_len, blocks * 128), brain_type),
+        compiler_params=pltpu.CompilerParams(vmem_limit_bytes=48 * 1024 * 1024),
+        cost_estimate=pl.CostEstimate(
+            flops=blocks * 2 * 2 * 4 * seq_len * seq_len * 64 * 2,
+            bytes_accessed=seq_len * width * 2,
+            transcendentals=blocks * 2 * seq_len * seq_len,
+        ),
+        name="attend",
+    )(qkv, segment[:, None], segment[None, :])
+
+
+def attend_back_kernel(score_scale, qkv_ref, grad_ref, seg_col_ref, seg_row_ref, out_ref, gk_ref, gv_ref):
+    seq_len = qkv_ref.shape[0]
+    rows = 256
+    keys = qkv_ref[:, 128:256]
+    values = qkv_ref[:, 256:384]
+    low_lane = lax.broadcasted_iota(jnp.int32, (rows, 128), 1) < 64
+    for part in range(seq_len // rows):
+        span = slice(part * rows, (part + 1) * rows)
+        query = qkv_ref[span, :128]
+        grad = grad_ref[span, :]
+        same = seg_col_ref[...] == seg_row_ref[:, span]
+        grad_queries = []
+        for head in range(2):
+            mine = low_lane if head == 0 else jnp.logical_not(low_lane)
+            masked = jnp.where(mine, query, jnp.zeros_like(query))
+            grad_masked = jnp.where(mine, grad, jnp.zeros_like(grad))
+            scores = jnp.where(same, nt(keys, masked) * score_scale, -1e30)
+            top = jnp.max(scores, axis=0, keepdims=True)
+            weight = jnp.exp(scores - top)
+            total = jnp.sum(weight, axis=0, keepdims=True)
+            probs = weight * (1.0 / total)
+            grad_probs = nt(values, grad_masked)
+            inner = jnp.sum(probs * grad_probs, axis=0, keepdims=True)
+            grad_raw = (probs * (grad_probs - inner) * score_scale).astype(brain_type)
+            gv_part = nn(probs.astype(brain_type), grad_masked)
+            gk_part = nn(grad_raw, masked)
+            if part == 0 and head == 0:
+                gv_ref[...] = gv_part
+                gk_ref[...] = gk_part
+            else:
+                gv_ref[...] += gv_part
+                gk_ref[...] += gk_part
+            grad_queries.append(tn(grad_raw, keys))
+        out_ref[span, :128] = jnp.where(low_lane, grad_queries[0], grad_queries[1]).astype(brain_type)
+    out_ref[:, 128:256] = gk_ref[...].astype(brain_type)
+    out_ref[:, 256:384] = gv_ref[...].astype(brain_type)
+
+
+def attend_back(qkv, grad, segment, score_scale):
+    seq_len, width = qkv.shape
+    blocks = width // 384
+    return pl.pallas_call(
+        partial(attend_back_kernel, score_scale),
+        grid=(blocks,),
+        in_specs=[
+            pl.BlockSpec((seq_len, 384), lambda i: (0, i)),
+            pl.BlockSpec((seq_len, 128), lambda i: (0, i)),
+            pl.BlockSpec((seq_len, 1), lambda i: (0, 0)),
+            pl.BlockSpec((1, seq_len), lambda i: (0, 0)),
+        ],
+        out_specs=pl.BlockSpec((seq_len, 384), lambda i: (0, i)),
+        out_shape=jax.ShapeDtypeStruct((seq_len, width), brain_type),
+        scratch_shapes=[
+            pltpu.VMEM((seq_len, 128), float_type),
+            pltpu.VMEM((seq_len, 128), float_type),
+        ],
+        compiler_params=pltpu.CompilerParams(vmem_limit_bytes=48 * 1024 * 1024),
+        cost_estimate=pl.CostEstimate(
+            flops=blocks * 2 * 5 * 4 * seq_len * seq_len * 64 * 2,
+            bytes_accessed=seq_len * width * 5,
+            transcendentals=blocks * 2 * seq_len * seq_len,
+        ),
+        name="attend_back",
+    )(qkv, grad, segment[:, None], segment[None, :])
+
+
+def center_of(rows):
+    center = rows - jnp.mean(rows, axis=-1, keepdims=True)
+    scale = lax.rsqrt(jnp.mean(center * center, axis=-1, keepdims=True) + 1e-05)
+    return center * scale, scale
+
+
+def normed(rows, gain, shift):
+    return (center_of(rows)[0] * gain + shift).astype(brain_type)
+
+
+def normed_back(rows, gain, grad):
+    unit, scale = center_of(rows)
+    grad_unit = grad * gain
+    below = scale * (
+        grad_unit
+        - jnp.mean(grad_unit, axis=-1, keepdims=True)
+        - unit * jnp.mean(grad_unit * unit, axis=-1, keepdims=True)
+    )
+    return below, jnp.sum(grad * unit, axis=0), jnp.sum(grad, axis=0)
+
+
+def gelu_pair(pre):
+    cdf = 0.5 * (1.0 + lax.erf(pre * math.sqrt(0.5)))
+    density = jnp.exp(-0.5 * pre * pre) * (1.0 / math.sqrt(2.0 * math.pi))
+    return (pre * cdf).astype(brain_type), (cdf + pre * density).astype(brain_type)
+
+
+class Mover:
+    def __init__(self, send_sems, recv_sems, local_sems):
+        self.send_sems, self.recv_sems, self.local_sems = send_sems, recv_sems, local_sems
+        self.remote, self.local = 0, 0
+        self.place = lax.axis_index("dp")
+        self.height = lax.axis_index("tensor")
+        self.core = lax.rem(self.place, 2)
+        self.x_bit = lax.rem(self.place // 2, 2)
+        self.y_bit = lax.rem(self.place // 4, 2)
+        self.z_low = lax.rem(self.height, 2)
+        self.z_high = self.height // 2
+        self.sibling = {"dp": self.place + 1 - 2 * self.core}
+        self.x_side = {"dp": self.place + 2 - 4 * self.x_bit}
+        self.y_side = {"dp": self.place + 4 - 8 * self.y_bit}
+        self.z_near = {"tensor": self.height + 1 - 2 * self.z_low}
+        self.z_far = {"tensor": self.height + 2 - 4 * self.z_high}
+
+    def make(self, source, target, device, send_index, recv_index):
+        return pltpu.make_async_remote_copy(
+            src_ref=source,
+            dst_ref=target,
+            send_sem=self.send_sems.at[send_index],
+            recv_sem=self.recv_sems.at[recv_index],
+            device_id=device,
+            device_id_type=pl.DeviceIdType.MESH,
+        )
+
+    def send(self, source, target, device):
+        copy = self.make(source, target, device, self.remote, self.remote)
+        self.remote += 1
+        copy.start()
+        return copy
+
+    def keep(self, source, target):
+        copy = pltpu.make_async_copy(source, target, self.local_sems.at[self.local])
+        self.local += 1
+        copy.start()
+        return copy
+
+    def greet(self):
+        barrier = pltpu.get_barrier_semaphore()
+        plane = self.place - self.core
+        devices = [self.x_side, self.y_side]
+        for step in range(1, 8):
+            other = lax.rem(self.core * 4 + self.height + step, 8)
+            devices.append({"dp": plane + other // 4, "tensor": lax.rem(other, 4)})
+        for device in devices:
+            pl.semaphore_signal(
+                barrier, inc=1, device_id=device, device_id_type=pl.DeviceIdType.MESH
+            )
+        pl.semaphore_wait(barrier, len(devices))
+
+    def column(self, y, x, half):
+        y_off = lax.rem(y + self.y_bit, 2)
+        x_off = lax.rem(x + self.x_bit, 2)
+        spot = 2 * y_off + x_off if half == 0 else y_off + 2 * x_off
+        return pl.multiple_of((half * 4 + spot) * 128, 128)
+
+
+BLOCKS = [(y, x, half) for y in range(2) for x in range(2) for half in range(2)]
+
+
+def move_tokens(move, ways, origins):
+    base, local = move.remote, move.local
+    move.remote += 2
+    move.local += 2
+    closing = []
+    for i, (to_core, to_z, copies, whole, slot) in enumerate(ways):
+        stays = jnp.logical_and(to_core == move.core, to_z == move.height)
+        device = {"dp": move.place - move.core + to_core, "tensor": to_z}
+
+        @pl.when(stays)
+        def _():
+            for source, target in copies:
+                pltpu.make_async_copy(source, target, move.local_sems.at[local + i]).start()
+
+        @pl.when(jnp.logical_not(stays))
+        def _():
+            for source, target in copies:
+                move.make(source, target, device, base + i, base + slot).start()
+
+        closing.append((stays, device, whole, i))
+
+    def finish():
+        for stays, device, (source, target), i in closing:
+            @pl.when(stays)
+            def _():
+                pltpu.make_async_copy(source, target, move.local_sems.at[local + i]).wait()
+
+            @pl.when(jnp.logical_not(stays))
+            def _():
+                move.make(source, target, device, base + i, base + i).wait_send()
+
+        for slot, (from_core, from_z, (source, target)) in enumerate(origins):
+            comes = jnp.logical_not(
+                jnp.logical_and(from_core == move.core, from_z == move.height)
+            )
+
+            @pl.when(comes)
+            def _():
+                move.make(source, target, move.sibling, base + slot, base + slot).wait_recv()
+
+    return finish
+
+
+def fetch_tokens(move, source, target):
+    rows = source.shape[1]
+    here = pl.ds(pl.multiple_of(move.z_low * rows, rows), rows)
+    ways, origins = [], []
+    for micro in range(2):
+        copies = [
+            (
+                source.at[micro, :, pl.ds(i * 128, 128)],
+                target.at[here, pl.ds(move.column(*block), 128)],
+            )
+            for i, block in enumerate(BLOCKS)
+        ]
+        whole = (source.at[micro], target.at[here])
+        ways.append((move.z_high, 2 * micro + move.core, copies, whole, move.z_low))
+    for slot in range(2):
+        whole = (source.at[slot], target.at[pl.ds(slot * rows, rows)])
+        origins.append((move.z_low, 2 * move.core + slot, whole))
+    return move_tokens(move, ways, origins)
+
+
+def return_tokens(move, source, target):
+    rows = target.shape[1]
+    ways, origins = [], []
+    for slot in range(2):
+        copies = [
+            (
+                source.at[pl.ds(slot * rows, rows), pl.ds(move.column(*block), 128)],
+                target.at[move.z_high, :, pl.ds(i * 128, 128)],
+            )
+            for i, block in enumerate(BLOCKS)
+        ]
+        whole = (source.at[pl.ds(slot * rows, rows)], target.at[move.z_high])
+        ways.append((move.z_low, 2 * move.core + slot, copies, whole, move.z_high))
+    for micro in range(2):
+        whole = (source.at[pl.ds(micro * rows, rows)], target.at[micro])
+        origins.append((move.z_high, 2 * micro + move.core, whole))
+    return move_tokens(move, ways, origins)
+
+
+def spread_stages(move, mine, other, whole, start=None):
+    rows, units = mine.shape
+    half = whole.shape[0] // 2
+    own = pl.ds(pl.multiple_of(move.core * half, half), rows)
+
+    def part(first, spot, lane, lanes):
+        return whole.at[pl.ds(first * half + spot * rows, rows), pl.ds(lane * units, lanes * units)]
+
+    copies = [
+        move.send(other, whole.at[own, pl.ds(0, units)], move.sibling),
+        move.keep(mine, whole.at[own, pl.ds(0, units)]),
+    ]
+    done = []
+
+    def go(first, spot, lane, lanes, to_spot, to_lane, device):
+        copy = move.send(part(first, spot, lane, lanes), part(first, to_spot, to_lane, lanes), device)
+        done.append(copy)
+        return copy
+
+    def plane(lane, lanes):
+        one = go(0, 0, lane, lanes, 1, lane, move.x_side)
+        two = go(1, 0, lane, lanes, 1, lane, move.y_side)
+        last = [
+            go(0, 0, lane, lanes, 2, lane, move.y_side),
+            go(1, 0, lane, lanes, 2, lane, move.x_side),
+        ]
+        return one, two, last, lane, lanes
+
+    def relay(one, two, last, lane, lanes):
+        one.wait_recv()
+        last.append(go(0, 1, lane, lanes, 3, lane, move.y_side))
+        two.wait_recv()
+        last.append(go(1, 1, lane, lanes, 3, lane, move.x_side))
+        return last
+
+    yield
+    copies[0].wait_send()
+    copies[0].wait_recv()
+    copies[1].wait()
+    near = [go(first, 0, 0, 1, 0, 1, move.z_near) for first in range(2)]
+    far = [go(first, 0, 0, 1, 0, 2, move.z_far) for first in range(2)]
+    planes = [plane(0, 1)]
+    yield
+    for copy in near:
+        copy.wait_recv()
+    far += [go(first, 0, 1, 1, 0, 3, move.z_far) for first in range(2)]
+    planes.append(plane(1, 1))
+    yield
+    lasts = relay(*planes[0])
+    for copy in far:
+        copy.wait_recv()
+    planes.append(plane(2, 2))
+    yield
+    lasts += relay(*planes[1])
+    yield
+    lasts += relay(*planes[2])
+    yield
+    for copy in lasts:
+        copy.wait_recv()
+    for copy in done:
+        copy.wait_send()
+
+
+SPREAD_STEPS = 6
+
+
+def vector_stages(move, vectors, out):
+    own = move.core * 4
+    keep = move.keep(vectors, out.at[own])
+    copy = move.send(vectors, out.at[own], move.sibling)
+    yield
+    keep.wait()
+    copy.wait()
+    over_x = [move.send(out.at[i], out.at[j], move.x_side) for i, j in ((0, 1), (4, 6))]
+    yield
+    for copy in over_x:
+        copy.wait()
+    over_y = [
+        move.send(out.at[i], out.at[j], move.y_side) for i, j in ((0, 2), (1, 3), (4, 5), (6, 7))
+    ]
+    yield
+    for copy in over_y:
+        copy.wait()
+
+
+def spread_kernel(groups, *refs):
+    count = 2 * groups
+    inputs, cotangent, vectors, ids = refs[:4]
+    pieces = refs[4 : 4 + count]
+    rows_out, grad_out, vectors_out, ids_out = refs[4 + count : 8 + count]
+    wholes = refs[8 + count : 8 + count + groups]
+    move = Mover(*refs[8 + count + groups :])
+    move.greet()
+    tasks = [
+        spread_stages(move, pieces[2 * i], pieces[2 * i + 1], wholes[i]) for i in range(groups)
+    ]
+    for task in tasks:
+        next(task)
+    finish_rows = fetch_tokens(move, inputs, rows_out)
+    small = vector_stages(move, vectors, vectors_out)
+    next(small)
+    ids_copy = move.send(ids, ids_out, move.sibling)
+    finish_grad = None
+    for tick in range(groups + SPREAD_STEPS - 1):
+        for i in range(groups - 1, -1, -1):
+            if 0 <= tick - i < SPREAD_STEPS:
+                next(tasks[i], None)
+        next(small, None)
+        if tick == 2:
+            finish_grad = fetch_tokens(move, cotangent, grad_out)
+    ids_copy.wait()
+    finish_rows()
+    finish_grad()
+
+
+def hbm(count):
+    return [pl.BlockSpec(memory_space=pl.ANY)] * count
+
+
+def spread_all(inputs, cotangent, vectors, ids, pieces):
+    groups = len(pieces)
+    tokens = 2 * inputs.shape[1]
+    width = inputs.shape[2]
+    flat = [block for piece in pieces for block in piece]
+    remote = 27 * groups + 16
+    outs = pl.pallas_call(
+        partial(spread_kernel, groups),
+        out_shape=[
+            jax.ShapeDtypeStruct((tokens, width), inputs.dtype),
+            jax.ShapeDtypeStruct((tokens, width), inputs.dtype),
+            jax.ShapeDtypeStruct((8, *vectors.shape), vectors.dtype),
+            jax.ShapeDtypeStruct(ids.shape, ids.dtype),
+        ]
+        + [jax.ShapeDtypeStruct((8 * p.shape[0], 4 * p.shape[1]), p.dtype) for p, _ in pieces],
+        in_specs=hbm(4 + 2 * groups),
+        out_specs=hbm(4 + groups),
+        scratch_shapes=[
+            pltpu.SemaphoreType.DMA((remote,)),
+            pltpu.SemaphoreType.DMA((remote,)),
+            pltpu.SemaphoreType.DMA((groups + 5,)),
+        ],
+        compiler_params=pltpu.CompilerParams(collective_id=0, has_side_effects=True),
+        name="spread",
+    )(inputs, cotangent, vectors, ids, *flat)
+    return outs[0], outs[1], outs[2], outs[3], outs[4:]
+
+
+def collect_stages(move, grads, out, loaded, first_got, second_got, far_got, near_got):
+    quarter = grads.shape[0] // 4
+    rows, units = quarter // 2, grads.shape[1] // 4
+    sides = ((move.y_side, move.x_side), (move.x_side, move.y_side))
+    done = []
+
+    def go(source, target, device):
+        copy = move.send(source, target, device)
+        done.append(copy)
+        return copy
+
+    def total(target, source, height, width):
+        step = 32
+
+        def body(i, carry):
+            span = (pl.ds(pl.multiple_of(i * step, step), step), pl.ds(0, width))
+            target[span] = (
+                target[span].astype(float_type) + source[span].astype(float_type)
+            ).astype(brain_type)
+            return carry
+
+        lax.fori_loop(0, height // step, body, 0)
+
+    first = [
+        go(grads.at[pl.ds((2 * i + 1) * quarter, quarter)], first_got.at[i], sides[i][0])
+        for i in range(2)
+    ]
+    loads = [
+        move.keep(grads.at[pl.ds(2 * i * quarter, quarter)], loaded.at[i]) for i in range(2)
+    ]
+    yield
+    second = []
+    for i in range(2):
+        loads[i].wait()
+        first[i].wait_recv()
+        total(loaded.at[i], first_got.at[i], quarter, 4 * units)
+        second.append(go(loaded.at[i, pl.ds(rows, rows)], second_got.at[i], sides[i][1]))
+    yield
+    far = []
+    for i in range(2):
+        second[i].wait_recv()
+        total(loaded.at[i], second_got.at[i], rows, 4 * units)
+        far.append(
+            go(loaded.at[i, pl.ds(0, rows), pl.ds(2 * units, 2 * units)], far_got.at[i], move.z_far)
+        )
+    yield
+    near = []
+    for i in range(2):
+        far[i].wait_recv()
+        total(loaded.at[i], far_got.at[i], rows, 2 * units)
+        near.append(
+            go(loaded.at[i, pl.ds(0, rows), pl.ds(units, units)], near_got.at[i], move.z_near)
+        )
+    yield
+    for i in range(2):
+        near[i].wait_recv()
+        total(loaded.at[i], near_got.at[i], rows, units)
+    ready = pl.ds(0, rows), pl.ds(0, units)
+    last = go(loaded.at[(1 - move.core, *ready)], out.at[1], move.sibling)
+    stay = move.keep(loaded.at[(move.core, *ready)], out.at[0])
+    yield
+    last.wait_recv()
+    stay.wait()
+    for copy in done:
+        copy.wait_send()
+
+
+COLLECT_STEPS = 6
+
+
+def vector_sum_stages(move, vectors, out, sums, by_core, by_y, by_x, by_near, by_far):
+    keep = move.keep(vectors.at[move.core], sums)
+    copy = move.send(vectors.at[1 - move.core], by_core, move.sibling)
+    yield
+    keep.wait()
+    copy.wait()
+    sums[...] += by_core[...]
+    copy = move.send(sums.at[pl.ds(2, 2)], by_y, move.y_side)
+    yield
+    copy.wait()
+    sums[:2] += by_y[...]
+    copy = move.send(sums.at[1], by_x, move.x_side)
+    yield
+    copy.wait()
+    sums[0] += by_x[...]
+    copy = move.send(sums.at[0], by_near, move.z_near)
+    yield
+    copy.wait()
+    sums[1] = sums[0] + by_near[...]
+    copy = move.send(sums.at[1], by_far, move.z_far)
+    yield
+    copy.wait()
+    out[...] = sums[1] + by_far[...]
+
+
+def collect_kernel(groups, *refs):
+    above, below, vectors = refs[:3]
+    grads = refs[3 : 3 + groups]
+    above_out, below_out, vectors_out = refs[3 + groups : 6 + groups]
+    outs = refs[6 + groups : 6 + 2 * groups]
+    buffers = refs[6 + 2 * groups : 6 + 7 * groups]
+    small_buffers = refs[6 + 7 * groups : 12 + 7 * groups]
+    move = Mover(*refs[12 + 7 * groups :])
+    move.greet()
+    tasks = [
+        collect_stages(move, grads[i], outs[i], *buffers[5 * i : 5 * i + 5]) for i in range(groups)
+    ]
+    for task in tasks:
+        next(task)
+    finish_above = return_tokens(move, above, above_out)
+    finish_below = return_tokens(move, below, below_out)
+    small = vector_sum_stages(move, vectors, vectors_out, *small_buffers)
+    next(small)
+    for tick in range(groups + COLLECT_STEPS - 1):
+        for i in range(groups):
+            if 0 <= tick - i < COLLECT_STEPS:
+                next(tasks[i], None)
+        next(small, None)
+    finish_above()
+    finish_below()
+
+
+def collect_all(tokens, vectors, grads):
+    groups = len(grads)
+    width = tokens[0].shape[1]
+    buffers = []
+    for grad in grads:
+        rows, units = grad.shape[0] // 8, grad.shape[1] // 4
+        for height, lanes in ((2 * rows, 4), (2 * rows, 4), (rows, 4), (rows, 2), (rows, 1)):
+            buffers.append(pltpu.VMEM((2, height, lanes * units), grad.dtype))
+    for shape in ((4, 8, 128), (4, 8, 128), (2, 8, 128), (8, 128), (8, 128), (8, 128)):
+        buffers.append(pltpu.VMEM(shape, vectors.dtype))
+    remote = 9 * groups + 9
+    outs = pl.pallas_call(
+        partial(collect_kernel, groups),
+        out_shape=[
+            jax.ShapeDtypeStruct((2, tokens[0].shape[0] // 2, width), tokens[0].dtype)
+            for _ in tokens
+        ]
+        + [
+            jax.ShapeDtypeStruct(vectors.shape[2:], vectors.dtype),
+        ]
+        + [
+            jax.ShapeDtypeStruct((2, g.shape[0] // 8, g.shape[1] // 4), g.dtype) for g in grads
+        ],
+        in_specs=hbm(3 + groups),
+        out_specs=hbm(2) + [pl.BlockSpec(memory_space=pltpu.VMEM)] + hbm(groups),
+        scratch_shapes=buffers
+        + [
+            pltpu.SemaphoreType.DMA((remote,)),
+            pltpu.SemaphoreType.DMA((remote,)),
+            pltpu.SemaphoreType.DMA((3 * groups + 5,)),
+        ],
+        compiler_params=pltpu.CompilerParams(
+            collective_id=1, has_side_effects=True, vmem_limit_bytes=60 * 1024 * 1024
+        ),
+        name="collect",
+    )(*tokens, vectors, *grads)
+    return outs[:2], outs[2], outs[3:]
+
+
+def per_chip(
+    inputs,
+    segment_ids,
+    norm1_gain,
+    norm1_shift,
+    w_query,
+    w_key,
+    w_value,
+    w_output,
+    norm2_gain,
+    norm2_shift,
+    w_fc_in,
+    w_fc_out,
+    cotangent,
+):
+    layers = norm1_gain.shape[0]
+    head_width = inputs.shape[3] // HEADS
+    score_scale = 1.0 / math.sqrt(head_width)
+    place = lax.axis_index("dp")
+    height = lax.axis_index("tensor")
+    core, x_bit, y_bit = place & 1, (place >> 1) & 1, (place >> 2) & 1
+    z_low, z_high = height & 1, (height >> 1) & 1
+
+    def halves(columns):
+        wide = columns.shape[1] // 2
+        low, high = columns[:, :wide], columns[:, wide:]
+        return pick(core, low, high), pick(core, high, low)
+
+    pieces = []
+    for layer in range(layers):
+        both = [halves(w[layer]) for w in (w_query, w_key, w_value)]
+        pieces += [
+            tuple(jnp.concatenate([b[side] for b in both], axis=1) for side in range(2)),
+            halves(w_output[layer].T),
+            halves(w_fc_in[layer]),
+            halves(w_fc_out[layer].T),
+        ]
+    vectors = jnp.concatenate([norm1_gain, norm1_shift, norm2_gain, norm2_shift], axis=0)
+    rows, grad, vectors, other_ids, weights = spread_all(
+        inputs[:, 0], cotangent[:, 0], vectors.astype(float_type), segment_ids, pieces
+    )
+    rows, grad = rows.astype(float_type), grad.astype(float_type)
+    vectors = vectors.transpose(1, 0, 2).reshape(4 * layers, -1)
+
+    ids = pick(z_low ^ core, segment_ids, other_ids)
+    ids = pick(z_high, ids[0, 0], ids[1, 0])
+    half_len = ids.shape[0] // 2
+    ids = pick(core, ids, jnp.concatenate([ids[half_len:], ids[:half_len]]))
+
+    def whole_tokens(half):
+        return jnp.concatenate([half, swap(half, "dp", CORE)], axis=0)
+
+    def summed(product, left):
+        rows_here = left.shape[0] // 2
+        got = swap(product(left[rows_here:]).astype(brain_type), "dp", CORE)
+        return product(left[:rows_here]) + got.astype(float_type)
+
+    saved = []
+    for layer in range(layers):
+        qkv_w, output_w, fc_in_w, fc_out_w = weights[4 * layer : 4 * layer + 4]
+        gain_one, shift_one, gain_two, shift_two = (vectors[i * layers + layer] for i in range(4))
+        normed_one = whole_tokens(normed(rows, gain_one, shift_one))
+        qkv = nn(normed_one, qkv_w).astype(brain_type)
+        attended = attend(qkv, ids, score_scale)
+        mid = rows + summed(lambda left: nt(left, output_w), attended)
+        normed_two = whole_tokens(normed(mid, gain_two, shift_two))
+        hidden, slope = gelu_pair(nn(normed_two, fc_in_w))
+        above = mid + summed(lambda left: nt(left, fc_out_w), hidden)
+        saved.append((rows, normed_one, qkv, attended, mid, normed_two, hidden, slope))
+        rows = above
+    block_output = rows
+
+    totals = [None] * (4 * layers)
+    vector_grads = [None] * (4 * layers)
+    for layer in reversed(range(layers)):
+        rows, normed_one, qkv, attended, mid, normed_two, hidden, slope = saved[layer]
+        qkv_w, output_w, fc_in_w, fc_out_w = weights[4 * layer : 4 * layer + 4]
+        gain_one, shift_one, gain_two, shift_two = (vectors[i * layers + layer] for i in range(4))
+        branch = whole_tokens(grad.astype(brain_type))
+        totals[4 * layer + 3] = tn_low(branch, hidden)
+        grad_pre = (nn(branch, fc_out_w) * slope.astype(float_type)).astype(brain_type)
+        totals[4 * layer + 2] = tn_low(normed_two, grad_pre)
+        grad_normed = summed(lambda left: nt(left, fc_in_w), grad_pre)
+        below, vector_grads[2 * layers + layer], vector_grads[3 * layers + layer] = normed_back(
+            mid, gain_two, grad_normed
+        )
+        grad = grad + below
+        branch = whole_tokens(grad.astype(brain_type))
+        totals[4 * layer + 1] = tn_low(branch, attended)
+        grad_attended = nn(branch, output_w).astype(brain_type)
+        grad_qkv = attend_back(qkv, grad_attended, ids, score_scale)
+        totals[4 * layer] = tn_low(normed_one, grad_qkv)
+        grad_normed = summed(lambda left: nt(left, qkv_w), grad_qkv)
+        below, vector_grads[layer], vector_grads[layers + layer] = normed_back(
+            rows, gain_one, grad_normed
+        )
+        grad = grad + below
+    vector_grads = jnp.stack(vector_grads).reshape(4 * layers, 2, 4, -1)
+    second = vector_grads[:, 1]
+    second = jnp.stack([second[:, i] for i in (0, 2, 1, 3)], axis=1)
+    vector_grads = jnp.stack([vector_grads[:, 0], second])
+    order = [4 * layer + kind for layer in reversed(range(layers)) for kind in (3, 2, 1, 0)]
+    block_output, vector_grads, outs = collect_all(
+        (block_output.astype(brain_type), grad.astype(brain_type)),
+        vector_grads.transpose(0, 2, 1, 3),
+        [totals[i] for i in order],
+    )
+    outs = [(pick(core, out[0], out[1]), pick(core, out[1], out[0])) for out in outs]
+    outs = [outs[order.index(i)] for i in range(4 * layers)]
+    block_output, input_grad = (tokens.astype(float_type) for tokens in block_output)
+
+    def joined(kind, columns=None):
+        per_layer = []
+        for layer in range(layers):
+            low, high = outs[4 * layer + kind]
+            if columns is not None:
+                low, high = low[:, columns], high[:, columns]
+            per_layer.append(jnp.concatenate([low, high], axis=1))
+        return jnp.stack(per_layer)
+
+    width = w_query.shape[2] // 2
+    grad_query, grad_key, grad_value = (joined(0, slice(i * width, (i + 1) * width)) for i in range(3))
+    grad_output = joined(1).transpose(0, 2, 1)
+    grad_fc_in = joined(2)
+    grad_fc_out = joined(3).transpose(0, 2, 1)
+
+    gain_one, shift_one, gain_two, shift_two = (
+        vector_grads[i * layers : (i + 1) * layers] for i in range(4)
+    )
+    return (
+        block_output[:, None],
+        input_grad[:, None],
+        gain_one,
+        shift_one,
+        grad_query.astype(float_type),
+        grad_key.astype(float_type),
+        grad_value.astype(float_type),
+        grad_output.astype(float_type),
+        gain_two,
+        shift_two,
+        grad_fc_in.astype(float_type),
+        grad_fc_out.astype(float_type),
+    )
 
 
 def layer_norm(token_rows, gain_vec, shift_vec):
@@ -447,8 +1214,10 @@
         P(None, "tensor", "dp"),
         P(None, "dp", "tensor", None),
     )
+    line, plane = mesh.shape["tensor"], mesh.shape["dp"]
+    fits = line == 4 and plane == 8 and 2 * line == plane
     return jax.shard_map(
-        per_device,
+        per_chip if fits else per_device,
         mesh=mesh,
         in_specs=placed,
         out_specs=(

time: 2250 us -> 907 us (0.40)
  waiting for transfers between devices: 1110 us -> 21.7 us
  Pallas kernels: 0 us -> 693 us
  matrix products: 730 us -> 138 us
  blocking collectives: 163 us -> 0 us
  other arithmetic: 117 us -> 26.9 us
  local copies, waits for them, and re-layouts: 103 us -> 13.6 us
    pallas_call x0 -> x6, Pallas kernels: none -> 693 us  [the longest x1 296 us: collect_all(): pl.pallas_call(partial(collect_kernel, groups), out_shape=[jax.ShapeDtype...]
    dot_general x128 -> x32, matrix products: 730 us -> 138 us  [the longest x8 51.6 us: nn(): lax.dot_general(left, right, (((1,), (0,)), ((), ())), preferred_element_...]
    reduce_scatter x20 -> x0, waiting for transfers between devices: 526 us -> none  [the longest x8 243 us: branch_total(): lax.psum_scatter(partial_sum.astype(jnp.bfloat16), 'tensor', scatter_dime...]
    all_gather x20 -> x0, waiting for transfers between devices: 514 us -> none  [the longest x8 251 us: normed_send(): lax.all_gather(normed_local(token_rows, gain_vec, shift_vec), 'tensor', a...]
    all_gather x16 -> x0, blocking collectives: 151 us -> none  [the longest x2 21.9 us: per_device(): lax.all_gather(w_output[layer_index], 'dp', axis=1, tiled=True)]
    unnamed x52 -> x0, waiting for transfers between devices: 66.7 us -> none
    unnamed x468 -> x141, local copies, waits for them, and re-layouts: 59 us -> 6.73 us
    reduce_sum x28 -> x5, other arithmetic: 50.9 us -> 4.13 us  [the longest x4 2.69 us: center_of(): scale = lax.rsqrt(jnp.mean(center * center, axis=-1, keepdims=True) + 1e-05)]
  transfers between devices with their start and end apart: 46 -> 16, of which waited for: 33 -> 9; matrix products, arithmetic and copies ran while one was open for 37% -> 6% of each run, Pallas kernels for 0% -> 0%
where the time goes in v1:
time: 907 us; the launch traced here: 900 us
  Pallas kernels  693 us (76%)
  matrix products  138 us (15%)
  other arithmetic  26.9 us (3%)
  waiting for transfers between devices  21.7 us (2%)
  local copies, waits for them, and re-layouts  13.6 us (1%)
    pallas_call x1, Pallas kernels, collect_all(): pl.pallas_call(partial(collect_kernel, groups), out_shape=[jax.ShapeDtype...  296 us
    pallas_call x1, Pallas kernels, spread_all(): pl.pallas_call(partial(spread_kernel, groups), out_shape=[jax.ShapeDtypeS...  270 us
    pallas_call x2, Pallas kernels, attend_back(): pl.pallas_call(partial(attend_back_kernel, score_scale), grid=(blocks,),...  83.9 us
    dot_general x8, matrix products, nn(): lax.dot_general(left, right, (((1,), (0,)), ((), ())), preferred_element_...  51.6 us
    dot_general x16, matrix products, nt(): lax.dot_general(left, right, (((1,), (1,)), ((), ())), preferred_element_...  45.5 us
    pallas_call x2, Pallas kernels, attend(): pl.pallas_call(partial(attend_kernel, score_scale), grid=(blocks,), in_sp...  43.2 us
    dot_general x8, matrix products, tn(): lax.dot_general(left, right, (((0,), (0,)), ((), ())), preferred_element_...  41.2 us
    ppermute x16, waiting for transfers between devices, swap(): return lax.ppermute(block, axis_name, [(i, i ^ bit) for i in range(size)])  21.7 us
  transfers between devices with their start and end apart: 16, of which 9 were waited for; matrix products, arithmetic and copies ran while one was open for 6% of the time, Pallas kernels for 0%

profile of v1, /device:TPU:0, one launch (start us, length us, event | category | flops | bytes accessed | tf_op | source)
XLA Modules:
  0.0 900.0 jit_solution(2059928315907957758)
XLA Ops:
  12.4 270.1 %spread.1 = (bf16[512,1024]{1,0:T(8,128)(2,1)}, bf16[512,1024]{1,0:T(8,128)(2,1)}, f32[8,8,128]{2,1,0:T(8,128)}, s32[2,1,1024]{2,1,0:T(1,128)}, bf16[1024,1536]{...) custom-call(bf16[2,256,1024]{2,1,0:T(8,128)(2,1)} %bitcast.175, ...), custom_call_target="tpu_custom_call" | custom-call | tf_op jit(solution)/shard_map/spread/pallas_call | solution.py:456
  290.2 5.6 convolution_convert_fusion.3.qkv_ref
  295.8 21.6 %attend.2 = bf16[1024,512]{1,0:T(8,128)(2,1)S(1)} custom-call(bf16[1024,1536]{1,0:T(8,128)(2,1)S(1)} %convolution_convert_fusion.3.qkv_ref, s32[1024,1]{1,0:T(8,128)S(1)} %broadcast_select_fusion.seg_col_ref, s32[1,1024]{1,0:T(1,128)S(1)} %broadcast_select_fusion.26.seg_row_ref), custom_call_target="tpu_custom_call" | custom-call | flops 8589934592 | bytes 3145728 | tf_op jit(solution)/shard_map/attend/pallas_call | solution.py:74
  325.5 8.4 multiply_convert_fusion.3
  345.1 4.5 convolution_convert_fusion.2.qkv_ref
  349.6 21.6 %attend.3 = bf16[1024,512]{1,0:T(8,128)(2,1)S(1)} custom-call(bf16[1024,1536]{1,0:T(8,128)(2,1)S(1)} %convolution_convert_fusion.2.qkv_ref, s32[1024,1]{1,0:T(8,128)S(1)} %broadcast_select_fusion.seg_col_ref, s32[1,1024]{1,0:T(1,128)S(1)} %broadcast_select_fusion.26.seg_row_ref), custom_call_target="tpu_custom_call" | custom-call | flops 8589934592 | bytes 3145728 | tf_op jit(solution)/shard_map/attend/pallas_call | solution.py:74
  379.4 8.0 multiply_convert_fusion.2
  387.4 11.5 %multiply_convert_fusion.1 = bf16[1024,2048]{1,0:T(8,128)(2,1)} fusion(bf16[1024,1024]{1,0:T(8,128)(2,1)S(1)} %constant_dynamic-update-slice_fusion, bf16[1024,2048]{1,0:T(8,128)(2,1)S(1)} %copy-done.48, f32[1024,2048]{1,0:T(8,128)} %get-tuple-element.213), kind=kOutput, calls=%fused_computation.13 | convolution fusion | flops 4320133120 | bytes 18874368 | tf_op jit(solution)/shard_map/dot_general | solution.py:41
  398.8 4.0 fusion.65
  405.8 6.4 multiply_reduce_fusion
  412.3 5.5 fusion.101
  422.7 42.0 %attend_back.2 = bf16[1024,1536]{1,0:T(8,128)(2,1)S(1)} custom-call(bf16[1024,1536]{1,0:T(8,128)(2,1)} %copy-done.3, bf16[1024,512]{1,0:T(8,128)(2,1)S(1)} %convolution_convert_fusion.11.grad_ref, s32[1024,1]{1,0:T(8,128)S(1)} %broadcast_select_fusion.seg_col_ref, s32[1,1024]{1,0:T(1,128)S(1)} %broadcast_select_fusion.26.seg_row_ref), custom_call_target="tpu_custom_call" | custom-call | flops 21474836480 | bytes 7864320 | tf_op jit(solution)/shard_map/attend_back/pallas_call | solution.py:135
  464.6 3.9 fusion.53
  476.2 6.4 convolution_convert_fusion.6.refs_4_
  482.6 6.2 convolution_convert_fusion.7.refs_3_
  488.9 11.0 %multiply_convert_fusion = bf16[1024,2048]{1,0:T(8,128)(2,1)} fusion(bf16[1024,2048]{1,0:T(8,128)(2,1)S(1)} %copy-done.47, f32[1024,2048]{1,0:T(8,128)} %get-tuple-element.208, bf16[512,1024]{1,0:T(8,128)(2,1)S(1)} %collective-permute-done.12, bf16[512,1024]{1,0:T(8,128)(2,1)S(1)} %get-tuple-element.112), kind=kOutput, calls=%fused_computation.12 | convolution fusion | flops 4324327424 | bytes 18874368 | tf_op jit(solution)/shard_map/dot_general | solution.py:41
  499.9 4.1 fusion.68
  506.6 4.9 convolution_convert_fusion.1.refs_6_
  516.8 6.3 convolution_convert_fusion.5.refs_7_
  523.1 6.5 convolution_convert_fusion.4.refs_8_
  530.9 41.9 %attend_back.3 = bf16[1024,1536]{1,0:T(8,128)(2,1)S(1)} custom-call(bf16[1024,1536]{1,0:T(8,128)(2,1)} %copy-done.2, bf16[1024,512]{1,0:T(8,128)(2,1)S(1)} %convolution_convert_fusion.10.grad_ref, s32[1024,1]{1,0:T(8,128)S(1)} %broadcast_select_fusion.seg_col_ref, s32[1,1024]{1,0:T(1,128)S(1)} %broadcast_select_fusion.26.seg_row_ref), custom_call_target="tpu_custom_call" | custom-call | flops 21474836480 | bytes 7864320 | tf_op jit(solution)/shard_map/attend_back/pallas_call | solution.py:135
  577.5 6.3 convolution_convert_fusion.refs_10_
  583.8 3.6 fusion.23
  591.5 296.3 %collect.1 = (bf16[2,256,1024]{2,1,0:T(8,128)(2,1)}, bf16[2,256,1024]{2,1,0:T(8,128)(2,1)}, f32[8,128]{1,0:T(8,128)}, bf16[2,128,512]{2,1,0:T(8,128)(2,1)}, bf16...) custom-call(bf16[512,1024]{1,0:T(8,128)(2,1)} %get-tuple-element.118, ...), custom_call_target="tpu_custom_call" | custom-call | tf_op jit(solution)/shard_map/collect/pallas_call | solution.py:611
  (282 shorter events, 90.9 us)
Async XLA Ops:
  283.7 38.6 %copy-start.24 = (f32[1,8,128]{2,0,1:T(1,128)}, f32[1,8,128]{2,0,1:T(1,128)S(1)}, u32[]{:S(2)}) copy-start(f32[1,8,128]{2,0,1:T(1,128)S(1)} %get-tuple-element.190) | copy-start | bytes 12292
  287.3 2.9 collective-permute-start
  295.8 21.6 %copy-start.2 = (bf16[1024,1536]{1,0:T(8,128)(2,1)}, bf16[1024,1536]{1,0:T(8,128)(2,1)S(1)}, u32[]{:S(2)}) copy-start(bf16[1024,1536]{1,0:T(8,128)(2,1)S(1)} %convolution_convert_fusion.3.qkv_ref) | copy-start | bytes 9437188
  295.8 21.6 %copy-start.12 = (bf16[1024,512]{1,0:T(8,128)(2,1)S(1)}, bf16[1024,512]{1,0:T(8,128)(2,1)}, u32[]{:S(2)}) copy-start(bf16[1024,512]{1,0:T(8,128)(2,1)} %get-tuple-element.39) | copy-start | bytes 3145732
  318.2 2.7 collective-permute-start.1
  322.3 11.6 %copy-start.35 = (f32[512]{0:T(512)}, f32[512]{0:T(512)S(1)}, u32[]{:S(2)}) copy-start(f32[512]{0:T(512)S(1)} %add_rsqrt_fusion.2) | copy-start | bytes 6148
  322.7 2.7 collective-permute-start.2
  336.3 2.7 collective-permute-start.3
  342.4 2.7 collective-permute-start.4
  349.6 21.6 %copy-start.3 = (bf16[1024,1536]{1,0:T(8,128)(2,1)}, bf16[1024,1536]{1,0:T(8,128)(2,1)S(1)}, u32[]{:S(2)}) copy-start(bf16[1024,1536]{1,0:T(8,128)(2,1)S(1)} %convolution_convert_fusion.2.qkv_ref) | copy-start | bytes 9437188
  349.6 21.6 %copy-start.6 = (bf16[1024,512]{1,0:T(8,128)(2,1)S(1)}, bf16[1024,512]{1,0:T(8,128)(2,1)}, u32[]{:S(2)}) copy-start(bf16[1024,512]{1,0:T(8,128)(2,1)} %get-tuple-element.43) | copy-start | bytes 3145732
  372.0 2.7 collective-permute-start.5
  372.5 4.3 collective-permute-start.8
  376.4 2.7 collective-permute-start.6
  387.4 24.9 %copy-start.61 = (bf16[1024,2048]{1,0:T(8,128)(2,1)}, bf16[1024,2048]{1,0:T(8,128)(2,1)S(1)}, u32[]{:S(2)}) copy-start(bf16[1024,2048]{1,0:T(8,128)(2,1)S(1)} %get-tuple-element.212) | copy-start | bytes 12582916
  402.8 3.0 collective-permute-start.9
  405.4 6.9 collective-permute-start.7
  417.8 2.7 collective-permute-start.10
  468.5 2.7 collective-permute-start.11
  474.5 14.3 %collective-permute-start.12 = (bf16[512,1024]{1,0:T(8,128)(2,1)S(1)}, bf16[512,1024]{1,0:T(8,128)(2,1)S(1)}, u32[]{:S(2)}, u32[]{:S(2)}) collective-permute-start(bf16[512,1024]{1,0:T(8,128)(2,1)S(1)} %get-tuple-element.112), channel_id=1, source_target_pairs={{0,4},{4,0},{8,12},{12,8},{16,20},{20,16},{24,28},{28,24},{1,5},{5... | collective-permute-start | bytes 3145736 | tf_op jit(solution)/shard_map/ppermute | solution.py:21
  504.1 7.4 collective-permute-start.13
  515.5 14.2 %collective-permute-start.14 = (bf16[512,1024]{1,0:T(8,128)(2,1)S(1)}, bf16[512,1024]{1,0:T(8,128)(2,1)S(1)}, u32[]{:S(2)}, u32[]{:S(2)}) collective-permute-start(bf16[512,1024]{1,0:T(8,128)(2,1)S(1)} %get-tuple-element.110), channel_id=1, source_target_pairs={{0,4},{4,0},{8,12},{12,8},{16,20},{20,16},{24,28},{28,24},{1,5},{5... | collective-permute-start | bytes 3145736 | tf_op jit(solution)/shard_map/ppermute | solution.py:21
  530.9 42.0 %copy-start.50 = (bf16[1024,1536]{1,0:T(8,128)(2,1)S(1)}, bf16[1024,1536]{1,0:T(8,128)(2,1)}, u32[]{:S(2)}) copy-start(bf16[1024,1536]{1,0:T(8,128)(2,1)} %get-tuple-element.37) | copy-start | bytes 9437188
  574.8 9.0 %collective-permute-start.15 = (bf16[512,1024]{1,0:T(8,128)(2,1)S(1)}, bf16[512,1024]{1,0:T(8,128)(2,1)S(1)}, u32[]{:S(2)}, u32[]{:S(2)}) collective-permute-start(bf16[512,1024]{1,0:T(8,128)(2,1)S(1)} %fusion.56), channel_id=1, source_target_pairs={{0,4},{4,0},{8,12},{12,8},{16,20},{20,16},{24,28},{28,24},{1,5},{5... | collective-permute-start | bytes 3145736 | tf_op jit(solution)/shard_map/ppermute | solution.py:21
  (59 other events, 289.1 us)

commit v2 on v1

--- a/solution.py
+++ b/solution.py
@@ -43,52 +43,6 @@
 
 def tn(left, right):
     return lax.dot_general(left, right, (((0,), (0,)), ((), ())), preferred_element_type=float_type)
-
-
-def attend_kernel(score_scale, qkv_ref, seg_col_ref, seg_row_ref, out_ref):
-    seq_len = qkv_ref.shape[0]
-    rows = 256
-    keys = qkv_ref[:, 128:256]
-    values = qkv_ref[:, 256:384]
-    low_lane = lax.broadcasted_iota(jnp.int32, (rows, 128), 1) < 64
-    for part in range(seq_len // rows):
-        span = slice(part * rows, (part + 1) * rows)
-        query = qkv_ref[span, :128]
-        same = seg_col_ref[span, :] == seg_row_ref[...]
-        outs = []
-        for head in range(2):
-            mine = low_lane if head == 0 else jnp.logical_not(low_lane)
-            masked = jnp.where(mine, query, jnp.zeros_like(query))
-            scores = jnp.where(same, nt(masked, keys) * score_scale, -1e30)
-            top = jnp.max(scores, axis=1, keepdims=True)
-            weight = jnp.exp(scores - top)
-            total = jnp.sum(weight, axis=1, keepdims=True)
-            probs = (weight * (1.0 / total)).astype(brain_type)
-            outs.append(nn(probs, values))
-        out_ref[span, :] = jnp.where(low_lane, outs[0], outs[1]).astype(brain_type)
-
-
-def attend(qkv, segment, score_scale):
-    seq_len, width = qkv.shape
-    blocks = width // 384
-    return pl.pallas_call(
-        partial(attend_kernel, score_scale),
-        grid=(blocks,),
-        in_specs=[
-            pl.BlockSpec((seq_len, 384), lambda i: (0, i)),
-            pl.BlockSpec((seq_len, 1), lambda i: (0, 0)),
-            pl.BlockSpec((1, seq_len), lambda i: (0, 0)),
-        ],
-        out_specs=pl.BlockSpec((seq_len, 128), lambda i: (0, i)),
-        out_shape=jax.ShapeDtypeStruct((seq_len, blocks * 128), brain_type),
-        compiler_params=pltpu.CompilerParams(vmem_limit_bytes=48 * 1024 * 1024),
-        cost_estimate=pl.CostEstimate(
-            flops=blocks * 2 * 2 * 4 * seq_len * seq_len * 64 * 2,
-            bytes_accessed=seq_len * width * 2,
-            transcendentals=blocks * 2 * seq_len * seq_len,
-        ),
-        name="attend",
-    )(qkv, segment[:, None], segment[None, :])
 
 
 def attend_back_kernel(score_scale, qkv_ref, grad_ref, seg_col_ref, seg_row_ref, out_ref, gk_ref, gv_ref):
@@ -163,10 +117,6 @@
     return center * scale, scale
 
 
-def normed(rows, gain, shift):
-    return (center_of(rows)[0] * gain + shift).astype(brain_type)
-
-
 def normed_back(rows, gain, grad):
     unit, scale = center_of(rows)
     grad_unit = grad * gain
@@ -176,12 +126,6 @@
         - unit * jnp.mean(grad_unit * unit, axis=-1, keepdims=True)
     )
     return below, jnp.sum(grad * unit, axis=0), jnp.sum(grad, axis=0)
-
-
-def gelu_pair(pre):
-    cdf = 0.5 * (1.0 + lax.erf(pre * math.sqrt(0.5)))
-    density = jnp.exp(-0.5 * pre * pre) * (1.0 / math.sqrt(2.0 * math.pi))
-    return (pre * cdf).astype(brain_type), (cdf + pre * density).astype(brain_type)
 
 
 class Mover:
@@ -413,66 +357,337 @@
         copy.wait()
 
 
-def spread_kernel(groups, *refs):
-    count = 2 * groups
-    inputs, cotangent, vectors, ids = refs[:4]
-    pieces = refs[4 : 4 + count]
-    rows_out, grad_out, vectors_out, ids_out = refs[4 + count : 8 + count]
-    wholes = refs[8 + count : 8 + count + groups]
-    move = Mover(*refs[8 + count + groups :])
+def hbm(count):
+    return [pl.BlockSpec(memory_space=pl.ANY)] * count
+
+
+def loop(count, body):
+    def step(i, carry):
+        body(i)
+        return carry
+
+    lax.fori_loop(0, count, step, 0)
+
+
+def at(i, size):
+    return pl.ds(pl.multiple_of(i * size, size), size)
+
+
+def vector_row(vectors, index):
+    return jnp.concatenate([vectors[spot, index : index + 1, :] for spot in range(8)], axis=1)
+
+
+def segment_rows(move, own_ids, other_ids, seg_row, seg_col):
+    own, other = own_ids[move.z_high], other_ids[move.z_high]
+    ids = jnp.where(move.z_low == move.core, own, other).astype(float_type)
+    half = ids.shape[1] // 2
+    turned = jnp.concatenate([ids[:, half:], ids[:, :half]], axis=1)
+    ids = jnp.where(move.core == 0, ids, turned)
+    seg_row[...] = ids
+    seg_col[...] = jnp.transpose(jnp.broadcast_to(ids, (128, 2 * half)))
+
+
+def forward_steps(move, score_scale, layers, box):
+    half = box["x"].shape[0]
+    tile = 256
+    vectors = box["vectors"]
+    send, got = box["send"], box["got"]
+    saves = {}
+
+    def save(name, layer):
+        source = box[name]
+        copy = move.keep(source, box["saved"][layer][name])
+        saves[name] = copy
+
+    def before(*names):
+        for name in names:
+            if name in saves:
+                saves.pop(name).wait()
+
+    def norm(source, target, gain, shift):
+        gain_row, shift_row = vector_row(vectors, gain), vector_row(vectors, shift)
+
+        def body(i):
+            rows = at(i, 64)
+            target[rows, :] = (center_of(source[rows, :])[0] * gain_row + shift_row).astype(
+                brain_type
+            )
+
+        loop(half // 64, body)
+        return move.send(target.at[pl.ds(0, half)], target.at[pl.ds(half, half)], move.sibling)
+
+    def partial_sums(left, weight, first):
+        def body(i):
+            columns = at(i, tile)
+            send[:, columns] = nt(left[pl.ds(half, half), :], weight[columns, :]).astype(brain_type)
+
+        loop(weight.shape[0] // tile, body)
+        return move.send(send, got, move.sibling)
+
+    def whole_sums(left, weight, base, target, copy):
+        copy.wait()
+
+        def body(i):
+            columns = at(i, tile)
+            target[:, columns] = (
+                base[:, columns]
+                + nt(left[pl.ds(0, half), :], weight[columns, :])
+                + got[:, columns].astype(float_type)
+            )
+
+        loop(weight.shape[0] // tile, body)
+
+    for layer in range(layers):
+        x, mid, n1, n2 = box["x"], box["mid"], box["n1"], box["n2"]
+        qkv, att, hid, slope = box["qkv"], box["att"], box["hid"], box["slope"]
+        base = 4 * layer
+        before("n1", "qkv")
+        sent = norm(x, n1, layer, layers + layer)
+        yield base
+        box["load"](base)
+
+        def project(first):
+            def body(i):
+                columns = at(i, tile)
+                rows = pl.ds(first * half, half)
+                qkv[rows, columns] = nn(n1[rows, :], box["w0"][:, columns]).astype(brain_type)
+
+            loop(qkv.shape[1] // tile, body)
+
+        project(0)
+        yield None
+        sent.wait()
+        project(1)
+        save("n1", layer)
+        save("qkv", layer)
+        before("att")
+        yield None
+        for pair in range(qkv.shape[1] // 384):
+
+            def body(part, pair=pair):
+                rows = at(part, tile)
+                low_lane = lax.broadcasted_iota(jnp.int32, (tile, 128), 1) < 64
+                query = qkv[rows, pl.ds(pair * 384, 128)] * jnp.asarray(score_scale, brain_type)
+                keys = qkv[:, pl.ds(pair * 384 + 128, 128)]
+                values = qkv[:, pl.ds(pair * 384 + 256, 128)]
+                same = box["seg_col"][rows, :1] == box["seg_row"][...]
+                outs = []
+                for head in range(2):
+                    mine = low_lane if head == 0 else jnp.logical_not(low_lane)
+                    scores = nt(jnp.where(mine, query, jnp.zeros_like(query)), keys)
+                    scores = jnp.where(same, scores, -1e30)
+                    weight = jnp.exp(scores - jnp.max(scores, axis=1, keepdims=True))
+                    inverse = 1.0 / jnp.sum(weight, axis=1, keepdims=True)
+                    outs.append(nn((weight * inverse).astype(brain_type), values))
+                att[rows, pl.ds(pair * 128, 128)] = jnp.where(low_lane, outs[0], outs[1]).astype(
+                    brain_type
+                )
+
+            loop(2 * half // tile, body)
+            yield None
+        yield base + 1
+        box["load"](base + 1)
+        sent = partial_sums(att, box["w1"], half)
+        save("att", layer)
+        yield None
+        before("mid", "n2")
+        whole_sums(att, box["w1"], x, mid, sent)
+        sent = norm(mid, n2, 2 * layers + layer, 3 * layers + layer)
+        save("mid", layer)
+        before("hid", "slope")
+        yield base + 2
+        box["load"](base + 2)
+        for first in range(2):
+            if first == 1:
+                sent.wait()
+                save("n2", layer)
+            rows = pl.ds(first * half, half)
+            count = hid.shape[1] // tile
+            for part in range(2):
+
+                def body(i, rows=rows, part=part):
+                    columns = at(part * (count // 2) + i, tile)
+                    pre = nn(n2[rows, :], box["w2"][:, columns])
+                    cdf = 0.5 * (1.0 + lax.erf(pre * math.sqrt(0.5)))
+                    density = jnp.exp(-0.5 * pre * pre) * (1.0 / math.sqrt(2.0 * math.pi))
+                    hid[rows, columns] = (pre * cdf).astype(brain_type)
+                    slope[rows, columns] = (cdf + pre * density).astype(brain_type)
+
+                loop(count // 2, body)
+                yield None
+        save("slope", layer)
+        yield base + 3
+        box["load"](base + 3)
+        before("n1", "qkv", "att", "n2")
+        sent = partial_sums(hid, box["w3"], half)
+        save("hid", layer)
+        yield None
+        before("x")
+        whole_sums(hid, box["w3"], mid, x, sent)
+        save("x", layer)
+    before(*list(saves))
+
+
+def forward_kernel(groups, layers, score_scale, *refs):
+    refs = list(refs)
+
+    def take(count):
+        taken, refs[:count] = refs[:count], []
+        return taken
+
+    inputs, cotangent, vectors, ids = take(4)
+    pieces = take(2 * groups)
+    rows_out, grad_out, vectors_out, ids_out = take(4)
+    wholes = take(groups)
+    names = ("n1", "qkv", "att", "mid", "n2", "hid", "slope", "x")
+    saved = [dict(zip(names, take(8))) for _ in range(layers)]
+    box = dict(zip(names, take(8)))
+    box["saved"] = saved
+    weights = take(4)
+    for i in range(4):
+        box[f"w{i}"] = weights[i]
+    box["send"], box["got"], x_in, box["vectors"] = take(4)
+    own_ids, other_ids, box["seg_row"], box["seg_col"] = take(4)
+    move = Mover(*refs)
     move.greet()
+    finish_rows = fetch_tokens(move, inputs, rows_out)
     tasks = [
         spread_stages(move, pieces[2 * i], pieces[2 * i + 1], wholes[i]) for i in range(groups)
     ]
     for task in tasks:
         next(task)
-    finish_rows = fetch_tokens(move, inputs, rows_out)
     small = vector_stages(move, vectors, vectors_out)
     next(small)
-    ids_copy = move.send(ids, ids_out, move.sibling)
-    finish_grad = None
+    ids_copy = move.send(ids, other_ids, move.sibling)
+    ids_here = move.keep(ids, own_ids)
+
+    loads = {}
+    complete = set()
+
+    def load(group):
+        loads.pop(group).wait()
+
+    def start_load(group):
+        loads[group] = move.keep(wholes[group], weights[group % 4])
+
+    box["load"] = load
+    compute = forward_steps(move, score_scale, layers, box)
+    state = {"need": None, "begun": False, "over": False, "loaded": -1}
+
+    def ready():
+        return state["need"] is None or state["need"] in complete
+
+    def prefetch():
+        group = state["loaded"] + 1
+        while group < groups and group in complete and (group < 4 or state["used"] > group - 4):
+            start_load(group)
+            state["loaded"] = group
+            group += 1
+
+    state["used"] = 0
+
+    def advance(count):
+        for _ in range(count):
+            if state["over"] or not ready():
+                return
+            if state["need"] is not None:
+                state["used"] = state["need"]
+                prefetch()
+            if state["need"] is not None and state["need"] not in loads:
+                return
+            try:
+                state["need"] = next(compute)
+            except StopIteration:
+                state["over"] = True
+
     for tick in range(groups + SPREAD_STEPS - 1):
         for i in range(groups - 1, -1, -1):
             if 0 <= tick - i < SPREAD_STEPS:
                 next(tasks[i], None)
+                if tick - i == SPREAD_STEPS - 1:
+                    complete.add(i)
+                    prefetch()
+                if state["begun"]:
+                    advance(PACE)
         next(small, None)
         if tick == 2:
+            ids_copy.wait()
+            ids_here.wait()
+            ids_kept = move.keep(other_ids, ids_out)
+            segment_rows(move, own_ids, other_ids, box["seg_row"], box["seg_col"])
             finish_grad = fetch_tokens(move, cotangent, grad_out)
-    ids_copy.wait()
-    finish_rows()
+        if tick == 3:
+            finish_rows()
+            copies = [move.keep(rows_out, x_in), move.keep(vectors_out, box["vectors"])]
+            for copy in copies:
+                copy.wait()
+
+            def body(i):
+                rows = at(i, 64)
+                box["x"][rows, :] = x_in[rows, :].astype(float_type)
+
+            loop(x_in.shape[0] // 64, body)
+            state["begun"] = True
+            state["need"] = None
+    while not state["over"]:
+        advance(1)
+    ids_kept.wait()
     finish_grad()
 
 
-def hbm(count):
-    return [pl.BlockSpec(memory_space=pl.ANY)] * count
-
-
-def spread_all(inputs, cotangent, vectors, ids, pieces):
+PACE = 1
+
+
+def forward_all(inputs, cotangent, vectors, ids, pieces, layers, score_scale):
     groups = len(pieces)
-    tokens = 2 * inputs.shape[1]
-    width = inputs.shape[2]
+    tokens, width = 2 * inputs.shape[1], inputs.shape[2]
+    units = [p.shape[1] for p, _ in pieces[:4]]
     flat = [block for piece in pieces for block in piece]
-    remote = 27 * groups + 16
+    remote = 27 * groups + 16 + 4 * layers
+    kept = [
+        ((2 * tokens, width), brain_type),
+        ((2 * tokens, 4 * units[0]), brain_type),
+        ((2 * tokens, 4 * units[1]), brain_type),
+        ((tokens, width), float_type),
+        ((2 * tokens, width), brain_type),
+        ((2 * tokens, 4 * units[2]), brain_type),
+        ((2 * tokens, 4 * units[2]), brain_type),
+        ((tokens, width), float_type),
+    ]
     outs = pl.pallas_call(
-        partial(spread_kernel, groups),
+        partial(forward_kernel, groups, layers, score_scale),
         out_shape=[
             jax.ShapeDtypeStruct((tokens, width), inputs.dtype),
             jax.ShapeDtypeStruct((tokens, width), inputs.dtype),
             jax.ShapeDtypeStruct((8, *vectors.shape), vectors.dtype),
             jax.ShapeDtypeStruct(ids.shape, ids.dtype),
         ]
-        + [jax.ShapeDtypeStruct((8 * p.shape[0], 4 * p.shape[1]), p.dtype) for p, _ in pieces],
+        + [jax.ShapeDtypeStruct((8 * p.shape[0], 4 * p.shape[1]), p.dtype) for p, _ in pieces]
+        + [jax.ShapeDtypeStruct(*shape) for _ in range(layers) for shape in kept],
         in_specs=hbm(4 + 2 * groups),
-        out_specs=hbm(4 + groups),
-        scratch_shapes=[
+        out_specs=hbm(4 + groups + 8 * layers),
+        scratch_shapes=[pltpu.VMEM(*shape) for shape in kept]
+        + [pltpu.VMEM((8 * p.shape[0], 4 * p.shape[1]), p.dtype) for p, _ in pieces[:4]]
+        + [
+            pltpu.VMEM((tokens, width), brain_type),
+            pltpu.VMEM((tokens, width), brain_type),
+            pltpu.VMEM((tokens, width), brain_type),
+            pltpu.VMEM((8, *vectors.shape), vectors.dtype),
+            pltpu.VMEM(ids.shape, ids.dtype),
+            pltpu.VMEM(ids.shape, ids.dtype),
+            pltpu.VMEM((1, 2 * tokens), float_type),
+            pltpu.VMEM((2 * tokens, 128), float_type),
             pltpu.SemaphoreType.DMA((remote,)),
             pltpu.SemaphoreType.DMA((remote,)),
-            pltpu.SemaphoreType.DMA((groups + 5,)),
+            pltpu.SemaphoreType.DMA((2 * groups + 10 + 8 * layers,)),
         ],
-        compiler_params=pltpu.CompilerParams(collective_id=0, has_side_effects=True),
-        name="spread",
+        compiler_params=pltpu.CompilerParams(
+            collective_id=0, has_side_effects=True, vmem_limit_bytes=60 * 1024 * 1024
+        ),
+        name="forward",
     )(inputs, cotangent, vectors, ids, *flat)
-    return outs[0], outs[1], outs[2], outs[3], outs[4:]
+    saved = [outs[4 + groups + 8 * i : 12 + groups + 8 * i] for i in range(layers)]
+    return outs[0], outs[1], outs[2], outs[3], outs[4 : 4 + groups], saved
 
 
 def collect_stages(move, grads, out, loaded, first_got, second_got, far_got, near_got):
@@ -674,10 +889,17 @@
             halves(w_fc_out[layer].T),
         ]
     vectors = jnp.concatenate([norm1_gain, norm1_shift, norm2_gain, norm2_shift], axis=0)
-    rows, grad, vectors, other_ids, weights = spread_all(
-        inputs[:, 0], cotangent[:, 0], vectors.astype(float_type), segment_ids, pieces
-    )
-    rows, grad = rows.astype(float_type), grad.astype(float_type)
+    rows, grad, vectors, other_ids, weights, saved = forward_all(
+        inputs[:, 0],
+        cotangent[:, 0],
+        vectors.astype(float_type),
+        segment_ids,
+        pieces,
+        layers,
+        score_scale,
+    )
+    below_rows = [rows.astype(float_type)] + [kept[7] for kept in saved]
+    grad = grad.astype(float_type)
     vectors = vectors.transpose(1, 0, 2).reshape(4 * layers, -1)
 
     ids = pick(z_low ^ core, segment_ids, other_ids)
@@ -693,25 +915,13 @@
         got = swap(product(left[rows_here:]).astype(brain_type), "dp", CORE)
         return product(left[:rows_here]) + got.astype(float_type)
 
-    saved = []
-    for layer in range(layers):
-        qkv_w, output_w, fc_in_w, fc_out_w = weights[4 * layer : 4 * layer + 4]
-        gain_one, shift_one, gain_two, shift_two = (vectors[i * layers + layer] for i in range(4))
-        normed_one = whole_tokens(normed(rows, gain_one, shift_one))
-        qkv = nn(normed_one, qkv_w).astype(brain_type)
-        attended = attend(qkv, ids, score_scale)
-        mid = rows + summed(lambda left: nt(left, output_w), attended)
-        normed_two = whole_tokens(normed(mid, gain_two, shift_two))
-        hidden, slope = gelu_pair(nn(normed_two, fc_in_w))
-        above = mid + summed(lambda left: nt(left, fc_out_w), hidden)
-        saved.append((rows, normed_one, qkv, attended, mid, normed_two, hidden, slope))
-        rows = above
-    block_output = rows
+    block_output = below_rows[layers]
 
     totals = [None] * (4 * layers)
     vector_grads = [None] * (4 * layers)
     for layer in reversed(range(layers)):
-        rows, normed_one, qkv, attended, mid, normed_two, hidden, slope = saved[layer]
+        normed_one, qkv, attended, mid, normed_two, hidden, slope, _ = saved[layer]
+        rows = below_rows[layer]
         qkv_w, output_w, fc_in_w, fc_out_w = weights[4 * layer : 4 * layer + 4]
         gain_one, shift_one, gain_two, shift_two = (vectors[i * layers + layer] for i in range(4))
         branch = whole_tokens(grad.astype(brain_type))

time: 907 us -> 831 us (0.916)
  matrix products: 138 us -> 80.7 us
  waiting for transfers between devices: 21.7 us -> 4.77 us
  Pallas kernels: 693 us -> 683 us
    dot_general x8 -> x4, matrix products: 51.6 us -> 18.5 us  [nn(): lax.dot_general(left, right, (((1,), (0,)), ((), ())), preferred_element_...]
    dot_general x16 -> x8, matrix products: 45.5 us -> 22.3 us  [nt(): lax.dot_general(left, right, (((1,), (1,)), ((), ())), preferred_element_...]
    ppermute x16 -> x8, waiting for transfers between devices: 21.7 us -> 4.77 us  [swap(): return lax.ppermute(block, axis_name, [(i, i ^ bit) for i in range(size)])]
    pallas_call x3 -> x1, Pallas kernels: 313 us -> 302 us  [forward_all(): pl.pallas_call(partial(forward_kernel, groups, layers, score_scale), out_...]
  transfers between devices with their start and end apart: 16 -> 8, of which waited for: 9 -> 3; matrix products, arithmetic and copies ran while one was open for 6% -> 6% of each run, Pallas kernels for 0% -> 0%
where the time goes in v2:
time: 831 us; the launch traced here: 820 us
  Pallas kernels  683 us (82%)
  matrix products  80.7 us (10%)
  other arithmetic  30.3 us (4%)
  local copies, waits for them, and re-layouts  17 us (2%)
    pallas_call x1, Pallas kernels, forward_all(): pl.pallas_call(partial(forward_kernel, groups, layers, score_scale), out_...  302 us
    pallas_call x1, Pallas kernels, collect_all(): pl.pallas_call(partial(collect_kernel, groups), out_shape=[jax.ShapeDtype...  297 us
    pallas_call x2, Pallas kernels, attend_back(): pl.pallas_call(partial(attend_back_kernel, score_scale), grid=(blocks,),...  84 us
    dot_general x8, matrix products, tn(): lax.dot_general(left, right, (((0,), (0,)), ((), ())), preferred_element_...  39.8 us
    dot_general x8, matrix products, nt(): lax.dot_general(left, right, (((1,), (1,)), ((), ())), preferred_element_...  22.3 us
    dot_general x4, matrix products, nn(): lax.dot_general(left, right, (((1,), (0,)), ((), ())), preferred_element_...  18.5 us
  transfers between devices with their start and end apart: 8, of which 3 were waited for; matrix products, arithmetic and copies ran while one was open for 6% of the time, Pallas kernels for 0%

profile of v2, /device:TPU:0, one launch (start us, length us, event | category | flops | bytes accessed | tf_op | source)
XLA Modules:
  0.0 820.4 jit_solution(12816466090664836891)
XLA Ops:
  13.4 301.9 %forward.1 = (bf16[512,1024]{1,0:T(8,128)(2,1)}, bf16[512,1024]{1,0:T(8,128)(2,1)}, f32[8,8,128]{2,1,0:T(8,128)}, s32[2,1,1024]{2,1,0:T(1,128)}, bf16[1024,1536]...) custom-call(bf16[2,256,1024]{2,1,0:T(8,128)(2,1)} %bitcast.163, ...), custom_call_target="tpu_custom_call" | custom-call | tf_op jit(solution)/shard_map/forward/pallas_call | solution.py:657
  315.6 2.9 convert_element_type.118.refs_0_
  326.9 6.9 multiply_convert_fusion.1
  333.8 2.4 fusion.38
  339.0 3.1 multiply_reduce_fusion
  343.9 2.0 collective-permute-done.2
  347.1 42.1 %attend_back.2 = bf16[1024,1536]{1,0:T(8,128)(2,1)S(1)} custom-call(bf16[1024,1536]{1,0:T(8,128)(2,1)} %get-tuple-element.59.qkv_ref, bf16[1024,512]{1,0:T(8,128)(2,1)S(1)} %convolution_convert_fusion.9.grad_ref, s32[1024,1]{1,0:T(8,128)S(1)} %broadcast_select_fusion.seg_col_ref, s32[1,1024]{1,0:T(1,128)S(1)} %broadcast_select_fusion.26.seg_row_ref), custom_call_target="tpu_custom_call" | custom-call | flops 21474836480 | bytes 7864320 | tf_op jit(solution)/shard_map/attend_back/pallas_call | solution.py:89
  393.8 2.4 multiply_reduce_fusion.2
  399.1 6.3 convolution_convert_fusion.5.refs_3_
  405.4 6.3 convolution_convert_fusion.4.refs_4_
  411.7 9.1 %multiply_convert_fusion = bf16[1024,2048]{1,0:T(8,128)(2,1)} fusion(bf16[1024,2048]{1,0:T(8,128)(2,1)} %get-tuple-element.65, bf16[1024,2048]{1,0:T(8,128)(2,1)S(1)} %copy-done.26, bf16[512,1024]{1,0:T(8,128)(2,1)S(1)} %collective-permute-done.4, bf16[512,1024]{1,0:T(8,128)(2,1)S(1)} %get-tuple-element.144), kind=kOutput, calls=%fused_computation | convolution fusion | flops 4305453056 | bytes 14680064 | tf_op jit(solution)/shard_map/dot_general | solution.py:41
  420.8 4.1 fusion.41
  425.4 2.3 convolution_convert_fusion.7.refs_5_
  427.6 5.0 convolution_convert_fusion.1.refs_6_
  432.7 3.1 multiply_reduce_fusion.1
  437.9 6.2 convolution_convert_fusion.3.refs_7_
  444.2 6.4 convolution_convert_fusion.2.refs_8_
  451.9 41.9 %attend_back.3 = bf16[1024,1536]{1,0:T(8,128)(2,1)S(1)} custom-call(bf16[1024,1536]{1,0:T(8,128)(2,1)} %get-tuple-element.68.qkv_ref, bf16[1024,512]{1,0:T(8,128)(2,1)S(1)} %convolution_convert_fusion.8.grad_ref, s32[1024,1]{1,0:T(8,128)S(1)} %broadcast_select_fusion.seg_col_ref, s32[1,1024]{1,0:T(1,128)S(1)} %broadcast_select_fusion.26.seg_row_ref), custom_call_target="tpu_custom_call" | custom-call | flops 21474836480 | bytes 7864320 | tf_op jit(solution)/shard_map/attend_back/pallas_call | solution.py:89
  495.9 2.3 convolution_convert_fusion.6.refs_9_
  498.2 5.0 convolution_convert_fusion.refs_10_
  503.2 3.7 fusion.10
  507.6 3.3 fusion.9.refs_1_
  510.9 296.9 %collect.1 = (bf16[2,256,1024]{2,1,0:T(8,128)(2,1)}, bf16[2,256,1024]{2,1,0:T(8,128)(2,1)}, f32[8,128]{1,0:T(8,128)}, bf16[2,128,512]{2,1,0:T(8,128)(2,1)}, bf16...) custom-call(bf16[512,1024]{1,0:T(8,128)(2,1)} %convert_element_type., ...), custom_call_target="tpu_custom_call" | custom-call | tf_op jit(solution)/shard_map/collect/pallas_call | solution.py:826
  814.2 2.5 bitcast_convert_fusion
  (215 shorter events, 50.4 us)
Async XLA Ops:
  0.6 6.2 copy-start.12
  6.9 5.9 copy-start.20
  6.9 5.9 copy-start.21
  6.9 5.9 copy-start.22
  6.9 5.9 copy-start.23
  315.4 9.1 %collective-permute-start = (bf16[512,1024]{1,0:T(8,128)(2,1)}, bf16[512,1024]{1,0:T(8,128)(2,1)}, u32[]{:S(2)}, u32[]{:S(2)}) collective-permute-start(bf16[512,1024]{1,0:T(8,128)(2,1)} %get-tuple-element.52), channel_id=1, source_target_pairs={{0,4},{4,0},{8,12},{12,8},{16,20},{20,16},{24,28},{28,24},{1,5},{5... | collective-permute-start | bytes 3145736 | tf_op jit(solution)/shard_map/ppermute | solution.py:21
  325.9 7.9 copy-start.10
  326.9 6.9 copy-start.28
  333.8 5.2 copy-start.45
  336.2 2.7 collective-permute-start.1
  343.1 2.7 collective-permute-start.2
  347.1 42.1 %copy-start.31 = (bf16[1024,1536]{1,0:T(8,128)(2,1)S(1)}, bf16[1024,1536]{1,0:T(8,128)(2,1)}, u32[]{:S(2)}) copy-start(bf16[1024,1536]{1,0:T(8,128)(2,1)} %get-tuple-element.62) | copy-start | bytes 9437188
  391.0 2.7 collective-permute-start.3
  397.0 14.6 %collective-permute-start.4 = (bf16[512,1024]{1,0:T(8,128)(2,1)S(1)}, bf16[512,1024]{1,0:T(8,128)(2,1)S(1)}, u32[]{:S(2)}, u32[]{:S(2)}) collective-permute-start(bf16[512,1024]{1,0:T(8,128)(2,1)S(1)} %get-tuple-element.144), channel_id=1, source_target_pairs={{0,4},{4,0},{8,12},{12,8},{16,20},{20,16},{24,28},{28,24},{1,5},{5... | collective-permute-start | bytes 3145736 | tf_op jit(solution)/shard_map/ppermute | solution.py:21
  399.1 6.3 copy-start.36
  399.1 6.3 copy-start.46
  405.4 6.3 copy-start.26
  411.7 9.1 %copy-start.25 = (bf16[1024,2048]{1,0:T(8,128)(2,1)S(1)}, bf16[1024,2048]{1,0:T(8,128)(2,1)}, u32[]{:S(2)}) copy-start(bf16[1024,2048]{1,0:T(8,128)(2,1)} %get-tuple-element.66) | copy-start | bytes 12582916
  424.9 7.7 collective-permute-start.5
  436.7 13.9 %collective-permute-start.6 = (bf16[512,1024]{1,0:T(8,128)(2,1)S(1)}, bf16[512,1024]{1,0:T(8,128)(2,1)S(1)}, u32[]{:S(2)}, u32[]{:S(2)}) collective-permute-start(bf16[512,1024]{1,0:T(8,128)(2,1)S(1)} %get-tuple-element.142), channel_id=1, source_target_pairs={{0,4},{4,0},{8,12},{12,8},{16,20},{20,16},{24,28},{28,24},{1,5},{5... | collective-permute-start | bytes 3145736 | tf_op jit(solution)/shard_map/ppermute | solution.py:21
  437.9 6.2 copy-start.34
  444.2 6.4 copy-start.38
  451.9 41.9 %copy-start.30 = (bf16[1024,1536]{1,0:T(8,128)(2,1)S(1)}, bf16[1024,1536]{1,0:T(8,128)(2,1)}, u32[]{:S(2)}) copy-start(bf16[1024,1536]{1,0:T(8,128)(2,1)} %get-tuple-element.70) | copy-start | bytes 9437188
  495.7 7.6 collective-permute-start.7
  (32 other events, 84.3 us)

commit v3 on v2

--- a/solution.py
+++ b/solution.py
@@ -12,27 +12,12 @@
 HEADS = 16
 float_type = jnp.float32
 brain_type = jnp.bfloat16
-CORE, XBIT, YBIT = 1, 2, 4
-ZLOW, ZHIGH = 1, 2
-
-
-def swap(block, axis_name, bit):
-    size = lax.axis_size(axis_name)
-    return lax.ppermute(block, axis_name, [(i, i ^ bit) for i in range(size)])
-
-
-def after(block, earlier):
-    return lax.optimization_barrier((block, earlier))[0]
 
 
 def pick(flag, when_zero, when_one):
     return jnp.where(flag == 0, when_zero, when_one)
 
 
-def tn_low(left, right):
-    return tn(left, right).astype(brain_type)
-
-
 def nt(left, right):
     return lax.dot_general(left, right, (((1,), (1,)), ((), ())), preferred_element_type=float_type)
 
@@ -43,89 +28,12 @@
 
 def tn(left, right):
     return lax.dot_general(left, right, (((0,), (0,)), ((), ())), preferred_element_type=float_type)
-
-
-def attend_back_kernel(score_scale, qkv_ref, grad_ref, seg_col_ref, seg_row_ref, out_ref, gk_ref, gv_ref):
-    seq_len = qkv_ref.shape[0]
-    rows = 256
-    keys = qkv_ref[:, 128:256]
-    values = qkv_ref[:, 256:384]
-    low_lane = lax.broadcasted_iota(jnp.int32, (rows, 128), 1) < 64
-    for part in range(seq_len // rows):
-        span = slice(part * rows, (part + 1) * rows)
-        query = qkv_ref[span, :128]
-        grad = grad_ref[span, :]
-        same = seg_col_ref[...] == seg_row_ref[:, span]
-        grad_queries = []
-        for head in range(2):
-            mine = low_lane if head == 0 else jnp.logical_not(low_lane)
-            masked = jnp.where(mine, query, jnp.zeros_like(query))
-            grad_masked = jnp.where(mine, grad, jnp.zeros_like(grad))
-            scores = jnp.where(same, nt(keys, masked) * score_scale, -1e30)
-            top = jnp.max(scores, axis=0, keepdims=True)
-            weight = jnp.exp(scores - top)
-            total = jnp.sum(weight, axis=0, keepdims=True)
-            probs = weight * (1.0 / total)
-            grad_probs = nt(values, grad_masked)
-            inner = jnp.sum(probs * grad_probs, axis=0, keepdims=True)
-            grad_raw = (probs * (grad_probs - inner) * score_scale).astype(brain_type)
-            gv_part = nn(probs.astype(brain_type), grad_masked)
-            gk_part = nn(grad_raw, masked)
-            if part == 0 and head == 0:
-                gv_ref[...] = gv_part
-                gk_ref[...] = gk_part
-            else:
-                gv_ref[...] += gv_part
-                gk_ref[...] += gk_part
-            grad_queries.append(tn(grad_raw, keys))
-        out_ref[span, :128] = jnp.where(low_lane, grad_queries[0], grad_queries[1]).astype(brain_type)
-    out_ref[:, 128:256] = gk_ref[...].astype(brain_type)
-    out_ref[:, 256:384] = gv_ref[...].astype(brain_type)
-
-
-def attend_back(qkv, grad, segment, score_scale):
-    seq_len, width = qkv.shape
-    blocks = width // 384
-    return pl.pallas_call(
-        partial(attend_back_kernel, score_scale),
-        grid=(blocks,),
-        in_specs=[
-            pl.BlockSpec((seq_len, 384), lambda i: (0, i)),
-            pl.BlockSpec((seq_len, 128), lambda i: (0, i)),
-            pl.BlockSpec((seq_len, 1), lambda i: (0, 0)),
-            pl.BlockSpec((1, seq_len), lambda i: (0, 0)),
-        ],
-        out_specs=pl.BlockSpec((seq_len, 384), lambda i: (0, i)),
-        out_shape=jax.ShapeDtypeStruct((seq_len, width), brain_type),
-        scratch_shapes=[
-            pltpu.VMEM((seq_len, 128), float_type),
-            pltpu.VMEM((seq_len, 128), float_type),
-        ],
-        compiler_params=pltpu.CompilerParams(vmem_limit_bytes=48 * 1024 * 1024),
-        cost_estimate=pl.CostEstimate(
-            flops=blocks * 2 * 5 * 4 * seq_len * seq_len * 64 * 2,
-            bytes_accessed=seq_len * width * 5,
-            transcendentals=blocks * 2 * seq_len * seq_len,
-        ),
-        name="attend_back",
-    )(qkv, grad, segment[:, None], segment[None, :])
 
 
 def center_of(rows):
     center = rows - jnp.mean(rows, axis=-1, keepdims=True)
     scale = lax.rsqrt(jnp.mean(center * center, axis=-1, keepdims=True) + 1e-05)
     return center * scale, scale
-
-
-def normed_back(rows, gain, grad):
-    unit, scale = center_of(rows)
-    grad_unit = grad * gain
-    below = scale * (
-        grad_unit
-        - jnp.mean(grad_unit, axis=-1, keepdims=True)
-        - unit * jnp.mean(grad_unit * unit, axis=-1, keepdims=True)
-    )
-    return below, jnp.sum(grad * unit, axis=0), jnp.sum(grad, axis=0)
 
 
 class Mover:
@@ -272,87 +180,147 @@
     return move_tokens(move, ways, origins)
 
 
-def spread_stages(move, mine, other, whole, start=None):
+class Clock:
+    def __init__(self):
+        self.now = 0.0
+        self.free = {}
+
+    def post(self, size, links):
+        start, end = self.now, self.now
+        for link, share in links:
+            begin = max(self.free.get(link, 0.0), self.now)
+            self.free[link] = begin + share * size * PER_BYTE
+            end = max(end, self.free[link])
+        return end + LATENCY
+
+
+PER_BYTE = 2.0 / 88e3
+LATENCY = 1.5
+OVER_X, OVER_Y = (("x", 1.0),), (("y", 1.0),)
+OVER_NEAR, OVER_FAR = (("z_out", 1.0),), (("z_out", 1.0), ("z_mid", 2.0))
+OVER_CORE = (("core", 0.1),)
+
+
+class Plan:
+    def __init__(self, clock):
+        self.clock, self.tasks = clock, []
+
+    def add(self, task):
+        due = next(task, None)
+        if due is not None:
+            self.tasks.append((due, task))
+
+    def step(self):
+        index = min(range(len(self.tasks)), key=lambda i: self.tasks[i][0])
+        due, task = self.tasks.pop(index)
+        self.clock.now = max(self.clock.now, due)
+        self.add(task)
+
+    def due(self):
+        return min((due for due, _ in self.tasks), default=float("inf"))
+
+    def finish(self, task):
+        while any(task is other for _, other in self.tasks):
+            self.step()
+
+    def run(self, compute, ready):
+        over = False
+        while self.tasks or not over:
+            if self.due() <= self.clock.now:
+                self.step()
+            elif not over and ready():
+                cost = next(compute, None)
+                if cost is None:
+                    over = True
+                else:
+                    self.clock.now += cost
+            elif self.tasks:
+                self.step()
+
+
+def size_of(ref):
+    return math.prod(ref.shape) * jnp.dtype(ref.dtype).itemsize
+
+
+def spread_group(move, plan, mine, other, whole, onward, complete):
+    clock = plan.clock
     rows, units = mine.shape
     half = whole.shape[0] // 2
     own = pl.ds(pl.multiple_of(move.core * half, half), rows)
+    done, planes = [], []
 
     def part(first, spot, lane, lanes):
         return whole.at[pl.ds(first * half + spot * rows, rows), pl.ds(lane * units, lanes * units)]
 
-    copies = [
-        move.send(other, whole.at[own, pl.ds(0, units)], move.sibling),
-        move.keep(mine, whole.at[own, pl.ds(0, units)]),
-    ]
-    done = []
-
-    def go(first, spot, lane, lanes, to_spot, to_lane, device):
-        copy = move.send(part(first, spot, lane, lanes), part(first, to_spot, to_lane, lanes), device)
+    def go(first, spot, lane, lanes, to_spot, to_lane, device, links):
+        source = part(first, spot, lane, lanes)
+        copy = move.send(source, part(first, to_spot, to_lane, lanes), device)
         done.append(copy)
-        return copy
+        return copy, clock.post(size_of(source), links)
+
+    x_way, y_way = (move.x_side, OVER_X), (move.y_side, OVER_Y)
 
     def plane(lane, lanes):
-        one = go(0, 0, lane, lanes, 1, lane, move.x_side)
-        two = go(1, 0, lane, lanes, 1, lane, move.y_side)
-        last = [
-            go(0, 0, lane, lanes, 2, lane, move.y_side),
-            go(1, 0, lane, lanes, 2, lane, move.x_side),
-        ]
-        return one, two, last, lane, lanes
-
-    def relay(one, two, last, lane, lanes):
-        one.wait_recv()
-        last.append(go(0, 1, lane, lanes, 3, lane, move.y_side))
-        two.wait_recv()
-        last.append(go(1, 1, lane, lanes, 3, lane, move.x_side))
-        return last
-
-    yield
-    copies[0].wait_send()
-    copies[0].wait_recv()
-    copies[1].wait()
-    near = [go(first, 0, 0, 1, 0, 1, move.z_near) for first in range(2)]
-    far = [go(first, 0, 0, 1, 0, 2, move.z_far) for first in range(2)]
-    planes = [plane(0, 1)]
-    yield
-    for copy in near:
-        copy.wait_recv()
-    far += [go(first, 0, 1, 1, 0, 3, move.z_far) for first in range(2)]
-    planes.append(plane(1, 1))
-    yield
-    lasts = relay(*planes[0])
-    for copy in far:
-        copy.wait_recv()
-    planes.append(plane(2, 2))
-    yield
-    lasts += relay(*planes[1])
-    yield
-    lasts += relay(*planes[2])
-    yield
-    for copy in lasts:
-        copy.wait_recv()
-    for copy in done:
-        copy.wait_send()
-
-
-SPREAD_STEPS = 6
-
-
-def vector_stages(move, vectors, out):
+        one = go(0, 0, lane, lanes, 1, lane, *x_way)
+        two = go(1, 0, lane, lanes, 1, lane, *y_way)
+        last = [go(0, 0, lane, lanes, 2, lane, *y_way), go(1, 0, lane, lanes, 2, lane, *x_way)]
+
+        def relay():
+            yield one[1]
+            one[0].wait_recv()
+            last.append(go(0, 1, lane, lanes, 3, lane, *y_way))
+            yield two[1]
+            two[0].wait_recv()
+            last.append(go(1, 1, lane, lanes, 3, lane, *x_way))
+            yield max(due for _, due in last)
+            for copy, _ in last:
+                copy.wait_recv()
+            planes.append(lane)
+            if len(planes) == 3:
+                for copy in done:
+                    copy.wait_send()
+                complete()
+
+        plan.add(relay())
+
+    def stages():
+        yield clock.now
+        swapped.wait()
+        kept.wait()
+        near = [go(i, 0, 0, 1, 0, 1, move.z_near, OVER_NEAR) for i in range(2)]
+        far = [go(i, 0, 0, 1, 0, 2, move.z_far, OVER_FAR) for i in range(2)]
+        plane(0, 1)
+        yield near[1][1]
+        for copy, _ in near:
+            copy.wait_recv()
+        far += [go(i, 0, 1, 1, 0, 3, move.z_far, OVER_FAR) for i in range(2)]
+        plane(1, 1)
+        onward()
+        yield far[3][1]
+        for copy, _ in far:
+            copy.wait_recv()
+        plane(2, 2)
+
+    swapped = move.send(other, whole.at[own, pl.ds(0, units)], move.sibling)
+    kept = move.keep(mine, whole.at[own, pl.ds(0, units)])
+    return stages()
+
+
+def vector_stages(move, clock, vectors, out):
     own = move.core * 4
     keep = move.keep(vectors, out.at[own])
     copy = move.send(vectors, out.at[own], move.sibling)
-    yield
+    yield clock.now + 2.0
     keep.wait()
     copy.wait()
     over_x = [move.send(out.at[i], out.at[j], move.x_side) for i, j in ((0, 1), (4, 6))]
-    yield
+    yield clock.now + 4.0
     for copy in over_x:
         copy.wait()
     over_y = [
         move.send(out.at[i], out.at[j], move.y_side) for i, j in ((0, 2), (1, 3), (4, 5), (6, 7))
     ]
-    yield
+    yield clock.now + 4.0
     for copy in over_y:
         copy.wait()
 
@@ -441,9 +409,11 @@
         x, mid, n1, n2 = box["x"], box["mid"], box["n1"], box["n2"]
         qkv, att, hid, slope = box["qkv"], box["att"], box["hid"], box["slope"]
         base = 4 * layer
+        save("x", layer)
         before("n1", "qkv")
         sent = norm(x, n1, layer, layers + layer)
-        yield base
+        box["need"](base)
+        yield 2.0
         box["load"](base)
 
         def project(first):
@@ -455,13 +425,13 @@
             loop(qkv.shape[1] // tile, body)
 
         project(0)
-        yield None
+        yield 3.0
         sent.wait()
         project(1)
         save("n1", layer)
         save("qkv", layer)
         before("att")
-        yield None
+        yield 3.0
         for pair in range(qkv.shape[1] // 384):
 
             def body(part, pair=pair):
@@ -484,18 +454,20 @@
                 )
 
             loop(2 * half // tile, body)
-            yield None
-        yield base + 1
+            if pair == qkv.shape[1] // 384 - 1:
+                box["need"](base + 1)
+            yield 5.5
         box["load"](base + 1)
         sent = partial_sums(att, box["w1"], half)
         save("att", layer)
-        yield None
+        yield 1.5
         before("mid", "n2")
         whole_sums(att, box["w1"], x, mid, sent)
         sent = norm(mid, n2, 2 * layers + layer, 3 * layers + layer)
         save("mid", layer)
         before("hid", "slope")
-        yield base + 2
+        box["need"](base + 2)
+        yield 4.0
         box["load"](base + 2)
         for first in range(2):
             if first == 1:
@@ -514,18 +486,28 @@
                     slope[rows, columns] = (cdf + pre * density).astype(brain_type)
 
                 loop(count // 2, body)
-                yield None
+                if first == 1 and part == 1:
+                    box["need"](base + 3)
+                yield 3.0
         save("slope", layer)
-        yield base + 3
         box["load"](base + 3)
         before("n1", "qkv", "att", "n2")
         sent = partial_sums(hid, box["w3"], half)
         save("hid", layer)
-        yield None
+        yield 3.5
         before("x")
         whole_sums(hid, box["w3"], mid, x, sent)
-        save("x", layer)
+        yield 4.0
+    low = box["low"]
+
+    def body(i):
+        rows = at(i, 64)
+        low[rows, :] = x[rows, :].astype(brain_type)
+
+    loop(half // 64, body)
+    copy = move.keep(low, box["block"])
     before(*list(saves))
+    copy.wait()
 
 
 def forward_kernel(groups, layers, score_scale, *refs):
@@ -537,105 +519,98 @@
 
     inputs, cotangent, vectors, ids = take(4)
     pieces = take(2 * groups)
-    rows_out, grad_out, vectors_out, ids_out = take(4)
+    rows_out, grad_out, vectors_out, ids_out, block_out = take(5)
     wholes = take(groups)
     names = ("n1", "qkv", "att", "mid", "n2", "hid", "slope", "x")
     saved = [dict(zip(names, take(8))) for _ in range(layers)]
     box = dict(zip(names, take(8)))
-    box["saved"] = saved
+    box["saved"], box["block"] = saved, block_out
     weights = take(4)
     for i in range(4):
         box[f"w{i}"] = weights[i]
-    box["send"], box["got"], x_in, box["vectors"] = take(4)
+    box["send"], box["got"], box["low"], box["vectors"] = take(4)
     own_ids, other_ids, box["seg_row"], box["seg_col"] = take(4)
     move = Mover(*refs)
+    clock = Clock()
+    plan = Plan(clock)
     move.greet()
     finish_rows = fetch_tokens(move, inputs, rows_out)
-    tasks = [
-        spread_stages(move, pieces[2 * i], pieces[2 * i + 1], wholes[i]) for i in range(groups)
-    ]
-    for task in tasks:
-        next(task)
-    small = vector_stages(move, vectors, vectors_out)
-    next(small)
-    ids_copy = move.send(ids, other_ids, move.sibling)
-    ids_here = move.keep(ids, own_ids)
-
-    loads = {}
-    complete = set()
-
-    def load(group):
-        loads.pop(group).wait()
-
-    def start_load(group):
-        loads[group] = move.keep(wholes[group], weights[group % 4])
-
-    box["load"] = load
-    compute = forward_steps(move, score_scale, layers, box)
-    state = {"need": None, "begun": False, "over": False, "loaded": -1}
-
-    def ready():
-        return state["need"] is None or state["need"] in complete
+    clock.post(size_of(inputs), OVER_FAR)
+    clock.now = 2.0
+    loads, complete = {}, set()
+    state = {"need": None, "begun": False, "loaded": -1, "used": 0}
 
     def prefetch():
         group = state["loaded"] + 1
         while group < groups and group in complete and (group < 4 or state["used"] > group - 4):
-            start_load(group)
+            loads[group] = move.keep(wholes[group], weights[group % 4])
             state["loaded"] = group
             group += 1
 
-    state["used"] = 0
-
-    def advance(count):
-        for _ in range(count):
-            if state["over"] or not ready():
-                return
-            if state["need"] is not None:
-                state["used"] = state["need"]
-                prefetch()
-            if state["need"] is not None and state["need"] not in loads:
-                return
-            try:
-                state["need"] = next(compute)
-            except StopIteration:
-                state["over"] = True
-
-    for tick in range(groups + SPREAD_STEPS - 1):
-        for i in range(groups - 1, -1, -1):
-            if 0 <= tick - i < SPREAD_STEPS:
-                next(tasks[i], None)
-                if tick - i == SPREAD_STEPS - 1:
-                    complete.add(i)
-                    prefetch()
-                if state["begun"]:
-                    advance(PACE)
-        next(small, None)
-        if tick == 2:
-            ids_copy.wait()
-            ids_here.wait()
-            ids_kept = move.keep(other_ids, ids_out)
-            segment_rows(move, own_ids, other_ids, box["seg_row"], box["seg_col"])
-            finish_grad = fetch_tokens(move, cotangent, grad_out)
-        if tick == 3:
-            finish_rows()
-            copies = [move.keep(rows_out, x_in), move.keep(vectors_out, box["vectors"])]
-            for copy in copies:
-                copy.wait()
-
-            def body(i):
-                rows = at(i, 64)
-                box["x"][rows, :] = x_in[rows, :].astype(float_type)
-
-            loop(x_in.shape[0] // 64, body)
-            state["begun"] = True
-            state["need"] = None
-    while not state["over"]:
-        advance(1)
-    ids_kept.wait()
-    finish_grad()
-
-
-PACE = 1
+    def spread_next(group):
+        if group < groups:
+            plan.add(tasks[group])
+
+    def completed(group):
+        complete.add(group)
+        prefetch()
+
+    tasks = [
+        spread_group(
+            move,
+            plan,
+            pieces[2 * i],
+            pieces[2 * i + 1],
+            wholes[i],
+            partial(spread_next, i + 1),
+            partial(completed, i),
+        )
+        for i in range(groups)
+    ]
+    ids_copy = move.send(ids, other_ids, move.sibling)
+    ids_here = move.keep(ids, own_ids)
+    plan.add(vector_stages(move, clock, vectors, vectors_out))
+    plan.add(tasks[0])
+
+    def need(group):
+        state["need"], state["used"] = group, group
+        prefetch()
+
+    def load(group):
+        loads.pop(group).wait()
+        state["need"] = None
+
+    box["need"], box["load"] = need, load
+    ends = []
+
+    def prepare():
+        yield 35.0
+        ids_copy.wait()
+        ids_here.wait()
+        ends.append(move.keep(other_ids, ids_out).wait)
+        segment_rows(move, own_ids, other_ids, box["seg_row"], box["seg_col"])
+        finish_rows()
+        copies = [move.keep(rows_out, box["low"]), move.keep(vectors_out, box["vectors"])]
+        for copy in copies:
+            copy.wait()
+
+        def body(i):
+            rows = at(i, 64)
+            box["x"][rows, :] = box["low"][rows, :].astype(float_type)
+
+        loop(box["x"].shape[0] // 64, body)
+        state["begun"] = True
+        yield 80.0
+        ends.append(fetch_tokens(move, cotangent, grad_out))
+
+    plan.add(prepare())
+
+    def ready():
+        return state["begun"] and (state["need"] is None or state["need"] in loads)
+
+    plan.run(forward_steps(move, score_scale, layers, box), ready)
+    for finish in ends:
+        finish()
 
 
 def forward_all(inputs, cotangent, vectors, ids, pieces, layers, score_scale):
@@ -661,11 +636,12 @@
             jax.ShapeDtypeStruct((tokens, width), inputs.dtype),
             jax.ShapeDtypeStruct((8, *vectors.shape), vectors.dtype),
             jax.ShapeDtypeStruct(ids.shape, ids.dtype),
+            jax.ShapeDtypeStruct((tokens, width), brain_type),
         ]
         + [jax.ShapeDtypeStruct((8 * p.shape[0], 4 * p.shape[1]), p.dtype) for p, _ in pieces]
         + [jax.ShapeDtypeStruct(*shape) for _ in range(layers) for shape in kept],
         in_specs=hbm(4 + 2 * groups),
-        out_specs=hbm(4 + groups + 8 * layers),
+        out_specs=hbm(5 + groups + 8 * layers),
         scratch_shapes=[pltpu.VMEM(*shape) for shape in kept]
         + [pltpu.VMEM((8 * p.shape[0], 4 * p.shape[1]), p.dtype) for p, _ in pieces[:4]]
         + [
@@ -686,168 +662,472 @@
         ),
         name="forward",
     )(inputs, cotangent, vectors, ids, *flat)
-    saved = [outs[4 + groups + 8 * i : 12 + groups + 8 * i] for i in range(layers)]
-    return outs[0], outs[1], outs[2], outs[3], outs[4 : 4 + groups], saved
-
-
-def collect_stages(move, grads, out, loaded, first_got, second_got, far_got, near_got):
-    quarter = grads.shape[0] // 4
-    rows, units = quarter // 2, grads.shape[1] // 4
-    sides = ((move.y_side, move.x_side), (move.x_side, move.y_side))
-    done = []
-
-    def go(source, target, device):
+    saved = [outs[5 + groups + 8 * i : 13 + groups + 8 * i] for i in range(layers)]
+    return outs[1], outs[2], outs[3], outs[4], outs[5 : 5 + groups], saved
+
+
+def collect_stages(move, clock, first, loaded, got, out, free, release):
+    first_got, second_got, far_got, near_got = got
+    rows, units = loaded.shape[1] // 2, loaded.shape[2] // 4
+    sides = ((move.x_side, OVER_X), (move.y_side, OVER_Y))
+    done = [copy for copy, _ in first]
+
+    def go(source, target, device, links):
         copy = move.send(source, target, device)
         done.append(copy)
-        return copy
+        return copy, clock.post(size_of(source), links)
 
     def total(target, source, height, width):
-        step = 32
-
-        def body(i, carry):
-            span = (pl.ds(pl.multiple_of(i * step, step), step), pl.ds(0, width))
+        def body(i):
+            span = (at(i, 32), pl.ds(0, width))
             target[span] = (
                 target[span].astype(float_type) + source[span].astype(float_type)
             ).astype(brain_type)
-            return carry
-
-        lax.fori_loop(0, height // step, body, 0)
-
-    first = [
-        go(grads.at[pl.ds((2 * i + 1) * quarter, quarter)], first_got.at[i], sides[i][0])
-        for i in range(2)
-    ]
-    loads = [
-        move.keep(grads.at[pl.ds(2 * i * quarter, quarter)], loaded.at[i]) for i in range(2)
-    ]
-    yield
+
+        loop(height // 32, body)
+
     second = []
     for i in range(2):
-        loads[i].wait()
-        first[i].wait_recv()
-        total(loaded.at[i], first_got.at[i], quarter, 4 * units)
-        second.append(go(loaded.at[i, pl.ds(rows, rows)], second_got.at[i], sides[i][1]))
-    yield
+        yield first[i][1]
+        first[i][0].wait_recv()
+        total(loaded.at[i], first_got.at[i], 2 * rows, 4 * units)
+        second.append(go(loaded.at[i, pl.ds(rows, rows)], second_got.at[i], *sides[i]))
     far = []
+    free("far")
     for i in range(2):
-        second[i].wait_recv()
+        yield second[i][1]
+        second[i][0].wait_recv()
         total(loaded.at[i], second_got.at[i], rows, 4 * units)
         far.append(
-            go(loaded.at[i, pl.ds(0, rows), pl.ds(2 * units, 2 * units)], far_got.at[i], move.z_far)
+            go(
+                loaded.at[i, pl.ds(0, rows), pl.ds(2 * units, 2 * units)],
+                far_got.at[i],
+                move.z_far,
+                OVER_FAR,
+            )
         )
-    yield
     near = []
+    free("near")
     for i in range(2):
-        far[i].wait_recv()
+        yield far[i][1]
+        far[i][0].wait_recv()
         total(loaded.at[i], far_got.at[i], rows, 2 * units)
         near.append(
-            go(loaded.at[i, pl.ds(0, rows), pl.ds(units, units)], near_got.at[i], move.z_near)
+            go(
+                loaded.at[i, pl.ds(0, rows), pl.ds(units, units)],
+                near_got.at[i],
+                move.z_near,
+                OVER_NEAR,
+            )
         )
-    yield
+    yield max(near[0][1], near[1][1])
     for i in range(2):
-        near[i].wait_recv()
+        near[i][0].wait_recv()
         total(loaded.at[i], near_got.at[i], rows, units)
+    release()
     ready = pl.ds(0, rows), pl.ds(0, units)
-    last = go(loaded.at[(1 - move.core, *ready)], out.at[1], move.sibling)
+    last, due = go(loaded.at[(1 - move.core, *ready)], out.at[1], move.sibling, OVER_CORE)
     stay = move.keep(loaded.at[(move.core, *ready)], out.at[0])
-    yield
+    yield due + 1.0
     last.wait_recv()
     stay.wait()
     for copy in done:
         copy.wait_send()
 
 
-COLLECT_STEPS = 6
-
-
-def vector_sum_stages(move, vectors, out, sums, by_core, by_y, by_x, by_near, by_far):
-    keep = move.keep(vectors.at[move.core], sums)
-    copy = move.send(vectors.at[1 - move.core], by_core, move.sibling)
-    yield
-    keep.wait()
+def vector_sum_stages(move, clock, vectors, sums, by_core, by_y, by_x, by_near, by_far, out):
+    def go(source, target, device):
+        return move.send(source, target, device), clock.now + 3.0
+
+    copy, due = go(vectors.at[1 - move.core], by_core, move.sibling)
+    yield due
     copy.wait()
-    sums[...] += by_core[...]
-    copy = move.send(sums.at[pl.ds(2, 2)], by_y, move.y_side)
-    yield
+    sums[...] = vectors[move.core] + by_core[...]
+    copy, due = go(sums.at[pl.ds(2, 2)], by_y, move.y_side)
+    yield due
     copy.wait()
     sums[:2] += by_y[...]
-    copy = move.send(sums.at[1], by_x, move.x_side)
-    yield
+    copy, due = go(sums.at[1], by_x, move.x_side)
+    yield due
     copy.wait()
     sums[0] += by_x[...]
-    copy = move.send(sums.at[0], by_near, move.z_near)
-    yield
+    copy, due = go(sums.at[0], by_near, move.z_near)
+    yield due
     copy.wait()
     sums[1] = sums[0] + by_near[...]
-    copy = move.send(sums.at[1], by_far, move.z_far)
-    yield
+    copy, due = go(sums.at[1], by_far, move.z_far)
+    yield due
     copy.wait()
     out[...] = sums[1] + by_far[...]
 
 
-def collect_kernel(groups, *refs):
-    above, below, vectors = refs[:3]
-    grads = refs[3 : 3 + groups]
-    above_out, below_out, vectors_out = refs[3 + groups : 6 + groups]
-    outs = refs[6 + groups : 6 + 2 * groups]
-    buffers = refs[6 + 2 * groups : 6 + 7 * groups]
-    small_buffers = refs[6 + 7 * groups : 12 + 7 * groups]
-    move = Mover(*refs[12 + 7 * groups :])
+def backward_steps(move, plan, score_scale, layers, box, start_group):
+    clock = plan.clock
+    grad, below, source = box["grad"], box["below"], box["source"]
+    branch, normed = box["branch"], box["normed"]
+    upper, fc_in, hid, slope = box["upper"], box["fc_in"], box["hid"], box["slope"]
+    send, got, sums = box["send"], box["got"], box["sums"]
+    half = grad.shape[0]
+    whole = 2 * half
+    tile = 256
+    qkv_width = box["layers"][0]["qkv"].shape[1]
+    att_width = box["layers"][0]["att"].shape[1]
+    wide = hid.shape[1]
+    qkv_part, att_part = pl.ds(0, qkv_width), pl.ds(qkv_width, att_width)
+    loads = {}
+
+    def load(layer, name, target):
+        loads[name] = move.keep(box["layers"][layer][name], target)
+
+    def need(*names):
+        for name in names:
+            if name in loads:
+                loads.pop(name).wait()
+
+    def load_mlp(layer):
+        load(layer, "hid", hid)
+        load(layer, "w3", upper)
+        load(layer, "slope", slope)
+
+    def share_branch():
+        def body(i):
+            rows = at(i, 64)
+            branch[rows, :] = grad[rows, :].astype(brain_type)
+
+        loop(half // 64, body)
+        return move.send(
+            branch.at[pl.ds(0, half)], branch.at[pl.ds(half, half)], move.sibling
+        )
+
+    def weight_grads(kind, layer, left, right, first, width):
+        group = start_group(kind, layer)
+        step = width if width <= 1024 else width // 2
+        for target, side, quarter, link in (
+            ("sent", 0, 1, OVER_Y),
+            ("sent", 1, 3, OVER_X),
+            ("loaded", 0, 0, None),
+            ("loaded", 1, 2, None),
+        ):
+            rows = left[:, pl.ds(quarter * 256, 256)]
+
+            def body(i, target=target, side=side, rows=rows):
+                part = right[:, pl.ds(pl.multiple_of(first + i * step, 128), step)]
+                group[target][side, :, at(i, step)] = tn(rows, part).astype(brain_type)
+
+            loop(width // step, body)
+            if target == "sent":
+                group["go"](side, link)
+            yield 1.0 + width * 0.85e-3
+        group["begin"]()
+
+    def partial_sums(left, first, width, weight, at_column):
+        def body(i):
+            columns = at(i, tile)
+            send[:, columns] = nt(
+                left[pl.ds(half, half), pl.ds(first, width)],
+                weight[columns, pl.ds(at_column, width)],
+            ).astype(brain_type)
+
+        loop(weight.shape[0] // tile, body)
+        return move.send(send, got, move.sibling)
+
+    def whole_sums(left, first, width, weight, at_column, copy):
+        def product(i):
+            columns = at(i, tile)
+            below[:, columns] = nt(
+                left[pl.ds(0, half), pl.ds(first, width)],
+                weight[columns, pl.ds(at_column, width)],
+            )
+
+        loop(weight.shape[0] // tile, product)
+        copy.wait()
+
+    def norm_back(gain, grad_gain, grad_shift):
+        gain_row = vector_row(box["vectors"], gain)
+        sums[...] = jnp.zeros_like(sums)
+
+        def body(i):
+            rows = at(i, 64)
+            unit, scale = center_of(source[rows, :])
+            down = below[rows, :] + got[rows, :].astype(float_type)
+            turn = down * gain_row
+            grad[rows, :] += scale * (
+                turn
+                - jnp.mean(turn, axis=-1, keepdims=True)
+                - unit * jnp.mean(turn * unit, axis=-1, keepdims=True)
+            )
+            sums[0:1, :] += jnp.sum(down * unit, axis=0, keepdims=True)
+            sums[1:2, :] += jnp.sum(down, axis=0, keepdims=True)
+
+        loop(half // 64, body)
+        for row, index in ((0, grad_gain), (1, grad_shift)):
+            for core in range(2):
+                for spot in range(4):
+                    to = spot if core == 0 else (0, 2, 1, 3)[spot]
+                    box["vector_grads"][core, to, index : index + 1, :] = sums[
+                        row : row + 1, pl.ds((core * 4 + spot) * 128, 128)
+                    ]
+
+    def slope_times(first):
+        def body(i):
+            rows, columns = pl.ds(first * half, half), at(i, tile)
+            product = nn(branch[rows, :], upper[:, columns])
+            slope[rows, columns] = (product * slope[rows, columns].astype(float_type)).astype(
+                brain_type
+            )
+
+        loop(wide // tile, body)
+
+    def attention(pair):
+        keys_at, values_at = pl.ds(pair * 384 + 128, 128), pl.ds(pair * 384 + 256, 128)
+        grad_keys, grad_values = box["grad_keys"], box["grad_values"]
+        grad_keys[...] = jnp.zeros_like(grad_keys)
+        grad_values[...] = jnp.zeros_like(grad_values)
+
+        def body(part):
+            rows = at(part, tile)
+            low_lane = lax.broadcasted_iota(jnp.int32, (tile, 128), 1) < 64
+            keys, values = hid[:, keys_at], hid[:, values_at]
+            query = hid[rows, pl.ds(pair * 384, 128)]
+            out_grad = slope[rows, pl.ds(qkv_width + pair * 128, 128)]
+            same = box["seg_col"][:, :1] == box["seg_row"][:, rows]
+            grad_queries = []
+            for head in range(2):
+                mine = low_lane if head == 0 else jnp.logical_not(low_lane)
+                masked = jnp.where(mine, query, jnp.zeros_like(query))
+                masked = masked * jnp.asarray(score_scale, brain_type)
+                grad_masked = jnp.where(mine, out_grad, jnp.zeros_like(out_grad))
+                scores = jnp.where(same, nt(keys, masked), -1e30)
+                weight = jnp.exp(scores - jnp.max(scores, axis=0, keepdims=True))
+                probs = weight * (1.0 / jnp.sum(weight, axis=0, keepdims=True))
+                grad_probs = nt(values, grad_masked)
+                inner = jnp.sum(probs * grad_probs, axis=0, keepdims=True)
+                grad_raw = (probs * (grad_probs - inner)).astype(brain_type)
+                grad_values[...] += nn(probs.astype(brain_type), grad_masked)
+                grad_keys[...] += nn(grad_raw, masked)
+                grad_queries.append(tn(grad_raw, keys))
+            slope[rows, pl.ds(pair * 384, 128)] = (
+                jnp.where(low_lane, grad_queries[0], grad_queries[1]) * score_scale
+            ).astype(brain_type)
+
+        loop(whole // tile, body)
+        slope[:, keys_at] = grad_keys[...].astype(brain_type)
+        slope[:, values_at] = grad_values[...].astype(brain_type)
+
+    load_mlp(layers - 1)
+    load(layers - 1, "n2", normed)
+    load(layers - 1, "w2", fc_in)
+    load(layers - 1, "mid", source)
+    for layer in reversed(range(layers)):
+        sent = share_branch()
+        need("w3", "slope")
+        yield 1.0
+        slope_times(0)
+        yield 4.0
+        sent.wait()
+        need("hid")
+        yield from weight_grads(3, layer, branch, hid, 0, wide)
+        load(layer, "qkv", hid.at[:, qkv_part])
+        load(layer, "att", hid.at[:, att_part])
+        slope_times(1)
+        load(layer, "w0", upper.at[:, qkv_part])
+        load(layer, "w1", upper.at[:, att_part])
+        yield 4.0
+        need("n2")
+        yield from weight_grads(2, layer, normed, slope, 0, wide)
+        load(layer, "n1", normed)
+        need("w2")
+        sent = partial_sums(slope, 0, wide, fc_in, 0)
+        yield 3.5
+        need("mid")
+        whole_sums(slope, 0, wide, fc_in, 0, sent)
+        if layer > 0:
+            load(layer - 1, "w2", fc_in)
+        yield 3.5
+        norm_back(2 * layers + layer, 2 * layers + layer, 3 * layers + layer)
+        load(layer, "x", source)
+        sent = share_branch()
+        need("w1")
+        yield 5.0
+
+        def grad_attended(first):
+            rows = pl.ds(first * half, half)
+            slope[rows, att_part] = nn(branch[rows, :], upper[:, att_part]).astype(brain_type)
+
+        grad_attended(0)
+        sent.wait()
+        grad_attended(1)
+        yield 2.0
+        need("att")
+        yield from weight_grads(1, layer, branch, hid, qkv_width, att_width)
+        need("qkv")
+        for pair in range(qkv_width // 384):
+            attention(pair)
+            yield 9.0
+        need("n1")
+        yield from weight_grads(0, layer, normed, slope, 0, qkv_width)
+        if layer > 0:
+            load(layer - 1, "n2", normed)
+            load(layer - 1, "hid", hid)
+        need("w0")
+        sent = partial_sums(slope, 0, qkv_width, upper, 0)
+        yield 3.0
+        whole_sums(slope, 0, qkv_width, upper, 0, sent)
+        if layer > 0:
+            load(layer - 1, "w3", upper)
+            load(layer - 1, "slope", slope)
+        need("x")
+        yield 3.0
+        norm_back(layer, layer, layers + layer)
+        if layer > 0:
+            load(layer - 1, "mid", source)
+        yield 4.0
+
+    def body(i):
+        rows = at(i, 64)
+        send[rows, :] = grad[rows, :].astype(brain_type)
+
+    loop(half // 64, body)
+
+
+BACK_NAMES = ("n1", "qkv", "att", "mid", "n2", "hid", "slope", "x")
+
+
+def backward_kernel(layers, score_scale, *refs):
+    refs = list(refs)
+
+    def take(count):
+        taken, refs[:count] = refs[:count], []
+        return taken
+
+    kinds = 4
+    groups = kinds * layers
+    block, cotangent, vectors, ids, other_ids_in = take(5)
+    weights = take(groups)
+    saved = [dict(zip(BACK_NAMES, take(8))) for _ in range(layers)]
+    for layer in range(layers):
+        for kind in range(kinds):
+            saved[layer][f"w{kind}"] = weights[kinds * layer + kind]
+    block_out, below_out, vectors_out = take(3)
+    outs = take(groups)
+    box = {"layers": saved}
+    names = ("upper", "fc_in", "hid", "slope", "normed", "branch", "source", "grad", "below")
+    box.update(zip(names, take(9)))
+    names = ("send", "got", "grad_keys", "grad_values", "seg_row", "seg_col", "vectors", "sums")
+    box.update(zip(names, take(8)))
+    own_ids, other_ids, box["vector_grads"] = take(3)
+    small = take(6)
+    buffers = [take(6) for _ in range(kinds)]
+    (credits,) = take(1)
+    move = Mover(*refs)
+    clock = Clock()
+    plan = Plan(clock)
+    copies = [
+        move.keep(cotangent, box["send"]),
+        move.keep(vectors, box["vectors"]),
+        move.keep(ids, own_ids),
+        move.keep(other_ids_in, other_ids),
+    ]
     move.greet()
-    tasks = [
-        collect_stages(move, grads[i], outs[i], *buffers[5 * i : 5 * i + 5]) for i in range(groups)
-    ]
-    for task in tasks:
-        next(task)
-    finish_above = return_tokens(move, above, above_out)
-    finish_below = return_tokens(move, below, below_out)
-    small = vector_sum_stages(move, vectors, vectors_out, *small_buffers)
-    next(small)
-    for tick in range(groups + COLLECT_STEPS - 1):
-        for i in range(groups):
-            if 0 <= tick - i < COLLECT_STEPS:
-                next(tasks[i], None)
-        next(small, None)
-    finish_above()
-    finish_below()
-
-
-def collect_all(tokens, vectors, grads):
-    groups = len(grads)
-    width = tokens[0].shape[1]
-    buffers = []
-    for grad in grads:
-        rows, units = grad.shape[0] // 8, grad.shape[1] // 4
-        for height, lanes in ((2 * rows, 4), (2 * rows, 4), (rows, 4), (rows, 2), (rows, 1)):
-            buffers.append(pltpu.VMEM((2, height, lanes * units), grad.dtype))
-    for shape in ((4, 8, 128), (4, 8, 128), (2, 8, 128), (8, 128), (8, 128), (8, 128)):
-        buffers.append(pltpu.VMEM(shape, vectors.dtype))
-    remote = 9 * groups + 9
+    finish_above = return_tokens(move, block, block_out)
+    for copy in copies:
+        copy.wait()
+    segment_rows(move, own_ids, other_ids, box["seg_row"], box["seg_col"])
+
+    def body(i):
+        rows = at(i, 64)
+        box["grad"][rows, :] = box["send"][rows, :].astype(float_type)
+
+    loop(box["grad"].shape[0] // 64, body)
+    devices = {"x": move.x_side, "y": move.y_side, "far": move.z_far, "near": move.z_near}
+    order = list(devices)
+    running = {}
+
+    def start_group(kind, layer):
+        if kind in running:
+            plan.finish(running.pop(kind))
+        sent, loaded, *got = buffers[kind]
+        first = [None, None]
+
+        def free(name):
+            if layer < layers - 1:
+                pl.semaphore_wait(credits.at[kind * 4 + order.index(name)], 1)
+
+        def release():
+            if layer > 0:
+                for i, name in enumerate(order):
+                    pl.semaphore_signal(
+                        credits.at[kind * 4 + i],
+                        inc=1,
+                        device_id=devices[name],
+                        device_id_type=pl.DeviceIdType.MESH,
+                    )
+
+        def go(side, link):
+            name = "y" if side == 0 else "x"
+            free(name)
+            copy = move.send(sent.at[side], got[0].at[side], devices[name])
+            first[side] = (copy, clock.post(size_of(sent.at[side]), link))
+
+        def begin():
+            task = collect_stages(
+                move, clock, first, loaded, got, outs[kinds * layer + kind], free, release
+            )
+            plan.add(task)
+            running[kind] = task
+
+        return {"sent": sent, "loaded": loaded, "go": go, "begin": begin}
+
+    def compute():
+        yield from backward_steps(move, plan, score_scale, layers, box, start_group)
+        ends.append(return_tokens(move, box["send"], below_out))
+        plan.add(vector_sum_stages(move, clock, box["vector_grads"], *small, vectors_out))
+
+    ends = [finish_above]
+    plan.run(compute(), lambda: True)
+    for finish in ends:
+        finish()
+
+
+def backward_all(block, cotangent, vectors, ids, other_ids, weights, saved, layers, score_scale):
+    tokens, width = cotangent.shape
+    units = [w.shape[1] for w in weights[:4]]
+    count = len(weights)
+    low, high = brain_type, float_type
+    small_vectors = (2, 4, vectors.shape[1], vectors.shape[2])
+    scratch = [((2 * tokens, units[2]), low)] * 4
+    scratch += [((2 * tokens, width), low)] * 2
+    scratch += [((tokens, width), high)] * 3
+    scratch += [((tokens, width), low)] * 2
+    scratch += [((2 * tokens, 128), high)] * 2
+    scratch += [((1, 2 * tokens), high), ((2 * tokens, 128), high)]
+    scratch += [(vectors.shape, high), ((8, width), high)]
+    scratch += [(ids.shape, ids.dtype)] * 2
+    scratch += [(small_vectors, high), (small_vectors[1:], high), (small_vectors[1:], high)]
+    scratch += [((2, *small_vectors[2:]), high)] + [(small_vectors[2:], high)] * 3
+    for wide in units:
+        for rows, columns in ((256, 1), (256, 1), (256, 1), (128, 1), (128, 2), (128, 4)):
+            scratch.append(((2, rows, wide // columns), low))
+    remote = 12 * count + 9 + 4 * layers + 8
     outs = pl.pallas_call(
-        partial(collect_kernel, groups),
-        out_shape=[
-            jax.ShapeDtypeStruct((2, tokens[0].shape[0] // 2, width), tokens[0].dtype)
-            for _ in tokens
-        ]
+        partial(backward_kernel, layers, score_scale),
+        out_shape=[jax.ShapeDtypeStruct((2, tokens // 2, width), low)] * 2
+        + [jax.ShapeDtypeStruct(vectors.shape[1:], high)]
+        + [jax.ShapeDtypeStruct((2, 128, w.shape[1] // 4), low) for w in weights],
+        in_specs=hbm(5 + count + 8 * layers),
+        out_specs=hbm(2) + [pl.BlockSpec(memory_space=pltpu.VMEM)] + hbm(count),
+        scratch_shapes=[pltpu.VMEM(*shape) for shape in scratch]
         + [
-            jax.ShapeDtypeStruct(vectors.shape[2:], vectors.dtype),
-        ]
-        + [
-            jax.ShapeDtypeStruct((2, g.shape[0] // 8, g.shape[1] // 4), g.dtype) for g in grads
-        ],
-        in_specs=hbm(3 + groups),
-        out_specs=hbm(2) + [pl.BlockSpec(memory_space=pltpu.VMEM)] + hbm(groups),
-        scratch_shapes=buffers
-        + [
+            pltpu.SemaphoreType.REGULAR((16,)),
             pltpu.SemaphoreType.DMA((remote,)),
             pltpu.SemaphoreType.DMA((remote,)),
-            pltpu.SemaphoreType.DMA((3 * groups + 5,)),
+            pltpu.SemaphoreType.DMA((8 + 14 * layers + count,)),
         ],
         compiler_params=pltpu.CompilerParams(
-            collective_id=1, has_side_effects=True, vmem_limit_bytes=60 * 1024 * 1024
+            collective_id=1, has_side_effects=True, vmem_limit_bytes=62 * 1024 * 1024
         ),
-        name="collect",
-    )(*tokens, vectors, *grads)
+        name="backward",
+    )(block, cotangent, vectors, ids, other_ids, *weights, *[a for kept in saved for a in kept])
     return outs[:2], outs[2], outs[3:]
 
 
@@ -869,10 +1149,7 @@
     layers = norm1_gain.shape[0]
     head_width = inputs.shape[3] // HEADS
     score_scale = 1.0 / math.sqrt(head_width)
-    place = lax.axis_index("dp")
-    height = lax.axis_index("tensor")
-    core, x_bit, y_bit = place & 1, (place >> 1) & 1, (place >> 2) & 1
-    z_low, z_high = height & 1, (height >> 1) & 1
+    core = lax.axis_index("dp") & 1
 
     def halves(columns):
         wide = columns.shape[1] // 2
@@ -889,7 +1166,7 @@
             halves(w_fc_out[layer].T),
         ]
     vectors = jnp.concatenate([norm1_gain, norm1_shift, norm2_gain, norm2_shift], axis=0)
-    rows, grad, vectors, other_ids, weights, saved = forward_all(
+    grad, vectors, other_ids, block, weights, saved = forward_all(
         inputs[:, 0],
         cotangent[:, 0],
         vectors.astype(float_type),
@@ -898,64 +1175,11 @@
         layers,
         score_scale,
     )
-    below_rows = [rows.astype(float_type)] + [kept[7] for kept in saved]
-    grad = grad.astype(float_type)
-    vectors = vectors.transpose(1, 0, 2).reshape(4 * layers, -1)
-
-    ids = pick(z_low ^ core, segment_ids, other_ids)
-    ids = pick(z_high, ids[0, 0], ids[1, 0])
-    half_len = ids.shape[0] // 2
-    ids = pick(core, ids, jnp.concatenate([ids[half_len:], ids[:half_len]]))
-
-    def whole_tokens(half):
-        return jnp.concatenate([half, swap(half, "dp", CORE)], axis=0)
-
-    def summed(product, left):
-        rows_here = left.shape[0] // 2
-        got = swap(product(left[rows_here:]).astype(brain_type), "dp", CORE)
-        return product(left[:rows_here]) + got.astype(float_type)
-
-    block_output = below_rows[layers]
-
-    totals = [None] * (4 * layers)
-    vector_grads = [None] * (4 * layers)
-    for layer in reversed(range(layers)):
-        normed_one, qkv, attended, mid, normed_two, hidden, slope, _ = saved[layer]
-        rows = below_rows[layer]
-        qkv_w, output_w, fc_in_w, fc_out_w = weights[4 * layer : 4 * layer + 4]
-        gain_one, shift_one, gain_two, shift_two = (vectors[i * layers + layer] for i in range(4))
-        branch = whole_tokens(grad.astype(brain_type))
-        totals[4 * layer + 3] = tn_low(branch, hidden)
-        grad_pre = (nn(branch, fc_out_w) * slope.astype(float_type)).astype(brain_type)
-        totals[4 * layer + 2] = tn_low(normed_two, grad_pre)
-        grad_normed = summed(lambda left: nt(left, fc_in_w), grad_pre)
-        below, vector_grads[2 * layers + layer], vector_grads[3 * layers + layer] = normed_back(
-            mid, gain_two, grad_normed
-        )
-        grad = grad + below
-        branch = whole_tokens(grad.astype(brain_type))
-        totals[4 * layer + 1] = tn_low(branch, attended)
-        grad_attended = nn(branch, output_w).astype(brain_type)
-        grad_qkv = attend_back(qkv, grad_attended, ids, score_scale)
-        totals[4 * layer] = tn_low(normed_one, grad_qkv)
-        grad_normed = summed(lambda left: nt(left, qkv_w), grad_qkv)
-        below, vector_grads[layer], vector_grads[layers + layer] = normed_back(
-            rows, gain_one, grad_normed
-        )
-        grad = grad + below
-    vector_grads = jnp.stack(vector_grads).reshape(4 * layers, 2, 4, -1)
-    second = vector_grads[:, 1]
-    second = jnp.stack([second[:, i] for i in (0, 2, 1, 3)], axis=1)
-    vector_grads = jnp.stack([vector_grads[:, 0], second])
-    order = [4 * layer + kind for layer in reversed(range(layers)) for kind in (3, 2, 1, 0)]
-    block_output, vector_grads, outs = collect_all(
-        (block_output.astype(brain_type), grad.astype(brain_type)),
-        vector_grads.transpose(0, 2, 1, 3),
-        [totals[i] for i in order],
+    tokens, vector_grads, outs = backward_all(
+        block, grad, vectors, segment_ids, other_ids, weights, saved, layers, score_scale
     )
+    block_output, input_grad = (part.astype(float_type) for part in tokens)
     outs = [(pick(core, out[0], out[1]), pick(core, out[1], out[0])) for out in outs]
-    outs = [outs[order.index(i)] for i in range(4 * layers)]
-    block_output, input_grad = (tokens.astype(float_type) for tokens in block_output)
 
     def joined(kind, columns=None):
         per_layer = []

time: 831 us -> 620 us (0.75)
  Pallas kernels: 683 us -> 590 us
  matrix products: 80.7 us -> 0 us
  other arithmetic: 30.3 us -> 17.4 us
  local copies, waits for them, and re-layouts: 17 us -> 7.76 us
    dot_general x20 -> x0, matrix products: 80.7 us -> none  [the longest x8 39.8 us: tn(): lax.dot_general(left, right, (((0,), (0,)), ((), ())), preferred_element_...]
    pallas_call x3 -> x1, Pallas kernels: 381 us -> 305 us  [backward_all(): pl.pallas_call(partial(backward_kernel, layers, score_scale), out_shape=[...]
    pallas_call x1, Pallas kernels: 302 us -> 285 us  [forward_all(): pl.pallas_call(partial(forward_kernel, groups, layers, score_scale), out_...]
    convert_element_type x5 -> x0, other arithmetic: 8.82 us -> none  [the longest x1 3.29 us: per_chip(): grad.astype(brain_type)]
  transfers between devices with their start and end apart: 8 -> 0, of which waited for: 3 -> 0; matrix products, arithmetic and copies ran while one was open for 6% -> 0% of each run, Pallas kernels for 0% -> 0%
where the time goes in v3:
time: 620 us; the launch traced here: 617 us
  Pallas kernels  590 us (95%)
  other arithmetic  17.4 us (3%)
  local copies, waits for them, and re-layouts  7.76 us (1%)
    pallas_call x1, Pallas kernels, backward_all(): pl.pallas_call(partial(backward_kernel, layers, score_scale), out_shape=[...  305 us
    pallas_call x1, Pallas kernels, forward_all(): pl.pallas_call(partial(forward_kernel, groups, layers, score_scale), out_...  285 us

profile of v3, /device:TPU:0, one launch (start us, length us, event | category | flops | bytes accessed | tf_op | source)
XLA Modules:
  0.0 616.5 jit_solution(5972061322024531325)
XLA Ops:
  0.7 1.4 maximum_convert_fusion.4.refs_2_
  2.1 0.9 slice_bitcast_fusion.4
  3.0 0.9 slice_bitcast_fusion.3
  3.9 0.9 slice_bitcast_fusion.2
  4.8 0.7 pad_maximum_fusion.3.refs_13_
  6.1 0.7 pad_maximum_fusion.1.refs_5_
  6.8 0.7 pad_maximum_fusion.refs_4_
  7.5 0.9 fusion.1
  9.9 0.7 broadcast_select_fusion.2
  10.6 0.7 broadcast_select_fusion.6
  11.5 0.7 broadcast_select_fusion
  12.4 0.7 broadcast_select_fusion.4
  13.1 284.9 %forward.1 = (bf16[512,1024]{1,0:T(8,128)(2,1)}, bf16[512,1024]{1,0:T(8,128)(2,1)}, f32[8,8,128]{2,1,0:T(8,128)}, s32[2,1,1024]{2,1,0:T(1,128)}, bf16[512,1024]{...) custom-call(bf16[2,256,1024]{2,1,0:T(8,128)(2,1)} %bitcast.104, ...), custom_call_target="tpu_custom_call" | custom-call | tf_op jit(solution)/shard_map/forward/pallas_call | solution.py:632
  298.0 305.2 %backward.1 = (bf16[2,256,1024]{2,1,0:T(8,128)(2,1)}, bf16[2,256,1024]{2,1,0:T(8,128)(2,1)}, f32[8,128]{1,0:T(8,128)}, bf16[2,128,384]{2,1,0:T(8,128)(2,1)}, bf1...) custom-call(bf16[512,1024]{1,0:T(8,128)(2,1)} %get-tuple-element.51., ...), custom_call_target="tpu_custom_call" | custom-call | tf_op jit(solution)/shard_map/backward/pallas_call | solution.py:1112
  603.3 1.4 fusion.6
  604.7 0.8 select_bitcast_fusion.13
  605.6 0.8 copy.31
  606.4 1.1 select_bitcast_fusion.9
  607.7 0.7 maximum_convert_fusion.1
  608.4 0.7 maximum_convert_fusion.2
  609.1 0.7 maximum_convert_fusion.3
  610.2 1.3 copy.32
  611.5 1.0 maximum_convert_fusion
  612.5 3.7 bitcast_convert_fusion
  (49 shorter events, 3.0 us)
Async XLA Ops:
  0.6 10.7 %copy-start.2 = (bf16[2,1024,128]{2,1,0:T(8,128)(2,1)S(1)}, bf16[2,1024,128]{2,1,0:T(8,128)(2,1)}, u32[]{:S(2)}) copy-start(bf16[2,1024,128]{2,1,0:T(8,128)(2,1)} %param.24) | copy-start | bytes 1572868
  0.7 9.2 %copy-start.1 = (bf16[2,128,1024]{2,1,0:T(8,128)(2,1)S(1)}, bf16[2,128,1024]{2,1,0:T(8,128)(2,1)}, u32[]{:S(2)}) copy-start(bf16[2,128,1024]{2,1,0:T(8,128)(2,1)} %param.23) | copy-start | bytes 1572868
  603.2 6.6 %copy-start.5 = (bf16[2,128,512]{2,1,0:T(8,128)(2,1)S(1)}, bf16[2,128,512]{2,1,0:T(8,128)(2,1)}, u32[]{:S(2)}) copy-start(bf16[2,128,512]{2,1,0:T(8,128)(2,1)} %get-tuple-element.86) | copy-start | bytes 786436
  603.2 6.6 %copy-start.6 = (bf16[2,128,512]{2,1,0:T(8,128)(2,1)S(1)}, bf16[2,128,512]{2,1,0:T(8,128)(2,1)}, u32[]{:S(2)}) copy-start(bf16[2,128,512]{2,1,0:T(8,128)(2,1)} %get-tuple-element.87) | copy-start | bytes 786436
  603.3 6.7 %copy-start.3 = (bf16[2,128,512]{2,1,0:T(8,128)(2,1)S(1)}, bf16[2,128,512]{2,1,0:T(8,128)(2,1)}, u32[]{:S(2)}) copy-start(bf16[2,128,512]{2,1,0:T(8,128)(2,1)} %get-tuple-element.88) | copy-start | bytes 786436
  603.3 6.7 %copy-start.4 = (bf16[2,128,512]{2,1,0:T(8,128)(2,1)S(1)}, bf16[2,128,512]{2,1,0:T(8,128)(2,1)}, u32[]{:S(2)}) copy-start(bf16[2,128,512]{2,1,0:T(8,128)(2,1)} %get-tuple-element.89) | copy-start | bytes 786436
  610.0 2.5 copy-start

commit v4 on v3

--- a/solution.py
+++ b/solution.py
@@ -12,10 +12,6 @@
 HEADS = 16
 float_type = jnp.float32
 brain_type = jnp.bfloat16
-
-
-def pick(flag, when_zero, when_one):
-    return jnp.where(flag == 0, when_zero, when_one)
 
 
 def nt(left, right):
@@ -51,7 +47,9 @@
         self.x_side = {"dp": self.place + 2 - 4 * self.x_bit}
         self.y_side = {"dp": self.place + 4 - 8 * self.y_bit}
         self.z_near = {"tensor": self.height + 1 - 2 * self.z_low}
-        self.z_far = {"tensor": self.height + 2 - 4 * self.z_high}
+        self.z_across = {"tensor": 3 - self.height}
+        self.inner = self.z_low != self.z_high
+        self.outer = jnp.logical_not(self.inner)
 
     def make(self, source, target, device, send_index, recv_index):
         return pltpu.make_async_remote_copy(
@@ -181,8 +179,9 @@
 
 
 class Clock:
-    def __init__(self):
+    def __init__(self, latency):
         self.now = 0.0
+        self.latency = latency
         self.free = {}
 
     def post(self, size, links):
@@ -191,13 +190,16 @@
             begin = max(self.free.get(link, 0.0), self.now)
             self.free[link] = begin + share * size * PER_BYTE
             end = max(end, self.free[link])
-        return end + LATENCY
-
-
-PER_BYTE = 2.0 / 88e3
-LATENCY = 1.5
+        return end + self.latency
+
+
+PER_BYTE = 2.0 / 84e3
+LATENCY, SLACK = 2.0, 6.0
+BACKLOG = 4.0
+Z_BACKLOG = 8.0
+TOKENS_AT = 8.0
 OVER_X, OVER_Y = (("x", 1.0),), (("y", 1.0),)
-OVER_NEAR, OVER_FAR = (("z_out", 1.0),), (("z_out", 1.0), ("z_mid", 2.0))
+OVER_NEAR, OVER_MID = (("z_out", 1.0),), (("z_mid", 1.0),)
 OVER_CORE = (("core", 0.1),)
 
 
@@ -242,12 +244,13 @@
     return math.prod(ref.shape) * jnp.dtype(ref.dtype).itemsize
 
 
-def spread_group(move, plan, mine, other, whole, onward, complete):
+def spread_group(move, plan, pieces, whole, rank, plane_first, onward, complete):
     clock = plan.clock
-    rows, units = mine.shape
+    rows = whole.shape[0] // 8
+    units = whole.shape[1] // 4
     half = whole.shape[0] // 2
     own = pl.ds(pl.multiple_of(move.core * half, half), rows)
-    done, planes = [], []
+    done, planes, swapped, kept = [], [], [], []
 
     def part(first, spot, lane, lanes):
         return whole.at[pl.ds(first * half + spot * rows, rows), pl.ds(lane * units, lanes * units)]
@@ -260,12 +263,16 @@
 
     x_way, y_way = (move.x_side, OVER_X), (move.y_side, OVER_Y)
 
-    def plane(lane, lanes):
-        one = go(0, 0, lane, lanes, 1, lane, *x_way)
-        two = go(1, 0, lane, lanes, 1, lane, *y_way)
-        last = [go(0, 0, lane, lanes, 2, lane, *y_way), go(1, 0, lane, lanes, 2, lane, *x_way)]
-
+    def backlog(*links):
+        return max(clock.free.get(link, 0.0) for link in links) - clock.now
+
+    def plane(lane, lanes, arrived):
         def relay():
+            while backlog("x", "y") > BACKLOG:
+                yield clock.now + backlog("x", "y") - BACKLOG + 0.01 * rank
+            one = go(0, 0, lane, lanes, 1, lane, *x_way)
+            two = go(1, 0, lane, lanes, 1, lane, *y_way)
+            last = [go(0, 0, lane, lanes, 2, lane, *y_way), go(1, 0, lane, lanes, 2, lane, *x_way)]
             yield one[1]
             one[0].wait_recv()
             last.append(go(0, 1, lane, lanes, 3, lane, *y_way))
@@ -276,34 +283,123 @@
             for copy, _ in last:
                 copy.wait_recv()
             planes.append(lane)
-            if len(planes) == 3:
-                for copy in done:
-                    copy.wait_send()
-                complete()
+            arrived()
 
         plan.add(relay())
 
-    def stages():
+    def line(block, parts, after_near):
+        size = parts * size_of(block(0, 0))
+        base = move.remote
+        move.remote += 4 * parts
+
+        def cross(i, lane, to_lane):
+            index = base + 4 * i + (0 if lane == 0 else 1)
+            return move.make(block(i, lane), block(i, to_lane), move.z_across, index, index)
+
+        def hand_on(i, lane, to_lane):
+            index = base + 4 * i
+            to_index = index + (0 if to_lane == 3 else 1)
+            return move.make(block(i, lane), block(i, to_lane), move.z_near, index + lane, to_index)
+
+        def sent_across(lane, to_lane):
+            @pl.when(move.inner)
+            def _():
+                for i in range(parts):
+                    cross(i, lane, to_lane).start()
+
+            return clock.post(size, OVER_MID)
+
+        def handed(lane, to_lane):
+            @pl.when(move.inner)
+            def _():
+                for i in range(parts):
+                    cross(i, 0 if lane == 3 else 1, lane).wait_recv()
+                    hand_on(i, lane, to_lane).start()
+
+            return clock.post(size, OVER_NEAR)
+
+        near = []
+        for i in range(parts):
+            near.append(move.send(block(i, 0), block(i, 1), move.z_near))
+        done.extend(near)
+        near_due = clock.post(size, OVER_NEAR)
+        first_due = sent_across(0, 3)
+        if not plane_first:
+            plane(0, 1, arrived)
+            onward()
+        yield near_due
+        for copy in near:
+            copy.wait_recv()
+        second_due = sent_across(1, 2)
+        after_near()
+        yield first_due
+        handed(3, 2)
+        yield second_due
+        last_due = handed(2, 3)
+        yield last_due
+
+        @pl.when(move.outer)
+        def _():
+            for i in range(parts):
+                hand_on(i, 3, 2).wait_recv()
+                hand_on(i, 2, 3).wait_recv()
+
+        @pl.when(move.inner)
+        def _():
+            for i in range(parts):
+                cross(i, 0, 3).wait_send()
+                cross(i, 1, 2).wait_send()
+                hand_on(i, 3, 2).wait_send()
+                hand_on(i, 2, 3).wait_send()
+
+    def finish():
+        for copy in done:
+            copy.wait_send()
+        complete()
+
+    def arrived():
+        if len(planes) == 3:
+            finish()
+
+    def start():
         yield clock.now
-        swapped.wait()
-        kept.wait()
-        near = [go(i, 0, 0, 1, 0, 1, move.z_near, OVER_NEAR) for i in range(2)]
-        far = [go(i, 0, 0, 1, 0, 2, move.z_far, OVER_FAR) for i in range(2)]
-        plane(0, 1)
-        yield near[1][1]
-        for copy, _ in near:
-            copy.wait_recv()
-        far += [go(i, 0, 1, 1, 0, 3, move.z_far, OVER_FAR) for i in range(2)]
-        plane(1, 1)
+        while backlog("z_mid", "z_out") > Z_BACKLOG:
+            yield clock.now + backlog("z_mid", "z_out") - Z_BACKLOG
+        for copy in swapped + kept:
+            copy.wait()
+
+    def over_line_first():
+        yield from start()
+
+        def after_near():
+            plane(1, 1, arrived)
+
+        yield from line(lambda i, lane: part(i, 0, lane, 1), 2, after_near)
+        plane(2, 2, arrived)
+
+    def over_plane_first():
+        yield from start()
+
+        def along():
+            yield clock.now
+            yield from line(
+                lambda i, lane: whole.at[pl.ds(0, 2 * half), pl.ds(lane * units, units)],
+                1,
+                lambda: None,
+            )
+            finish()
+
+        plane(0, 1, lambda: plan.add(along()))
         onward()
-        yield far[3][1]
-        for copy, _ in far:
-            copy.wait_recv()
-        plane(2, 2)
-
-    swapped = move.send(other, whole.at[own, pl.ds(0, units)], move.sibling)
-    kept = move.keep(mine, whole.at[own, pl.ds(0, units)])
-    return stages()
+
+    at_column = 0
+    for mine, other in pieces:
+        width = mine.shape[1]
+        target = whole.at[own, pl.ds(at_column, width)]
+        swapped.append(move.send(other, target, move.sibling))
+        kept.append(move.keep(mine, target))
+        at_column += width
+    return over_plane_first() if plane_first else over_line_first()
 
 
 def vector_stages(move, clock, vectors, out):
@@ -518,7 +614,7 @@
         return taken
 
     inputs, cotangent, vectors, ids = take(4)
-    pieces = take(2 * groups)
+    raw = take(6)
     rows_out, grad_out, vectors_out, ids_out, block_out = take(5)
     wholes = take(groups)
     names = ("n1", "qkv", "att", "mid", "n2", "hid", "slope", "x")
@@ -531,11 +627,9 @@
     box["send"], box["got"], box["low"], box["vectors"] = take(4)
     own_ids, other_ids, box["seg_row"], box["seg_col"] = take(4)
     move = Mover(*refs)
-    clock = Clock()
+    clock = Clock(LATENCY)
     plan = Plan(clock)
     move.greet()
-    finish_rows = fetch_tokens(move, inputs, rows_out)
-    clock.post(size_of(inputs), OVER_FAR)
     clock.now = 2.0
     loads, complete = {}, set()
     state = {"need": None, "begun": False, "loaded": -1, "used": 0}
@@ -555,13 +649,22 @@
         complete.add(group)
         prefetch()
 
+    def halves(ref, layer):
+        wide = ref.shape[2] // 2
+        return tuple(
+            ref.at[layer, :, pl.ds(pl.multiple_of(side * wide, 128), wide)]
+            for side in (move.core, 1 - move.core)
+        )
+
+    kinds = (raw[:3], raw[3:4], raw[4:5], raw[5:6])
     tasks = [
         spread_group(
             move,
             plan,
-            pieces[2 * i],
-            pieces[2 * i + 1],
+            [halves(ref, i // 4) for ref in kinds[i % 4]],
             wholes[i],
+            i,
+            i % 4 == 1,
             partial(spread_next, i + 1),
             partial(completed, i),
         )
@@ -584,7 +687,10 @@
     ends = []
 
     def prepare():
-        yield 35.0
+        yield TOKENS_AT
+        finish_rows = fetch_tokens(move, inputs, rows_out)
+        clock.post(size_of(inputs), OVER_MID)
+        yield TOKENS_AT + 33.0
         ids_copy.wait()
         ids_here.wait()
         ends.append(move.keep(other_ids, ids_out).wait)
@@ -600,7 +706,8 @@
 
         loop(box["x"].shape[0] // 64, body)
         state["begun"] = True
-        yield 80.0
+        yield 100.0
+        clock.post(size_of(inputs), OVER_MID)
         ends.append(fetch_tokens(move, cotangent, grad_out))
 
     plan.add(prepare())
@@ -613,12 +720,12 @@
         finish()
 
 
-def forward_all(inputs, cotangent, vectors, ids, pieces, layers, score_scale):
-    groups = len(pieces)
+def forward_all(inputs, cotangent, vectors, ids, raw, layers, score_scale):
+    groups = 4 * layers
     tokens, width = 2 * inputs.shape[1], inputs.shape[2]
-    units = [p.shape[1] for p, _ in pieces[:4]]
-    flat = [block for piece in pieces for block in piece]
-    remote = 27 * groups + 16 + 4 * layers
+    units = [w.shape[2] // 2 for w in raw]
+    units = [sum(units[:3])] + units[3:]
+    remote = 33 * groups + 16 + 4 * layers
     kept = [
         ((2 * tokens, width), brain_type),
         ((2 * tokens, 4 * units[0]), brain_type),
@@ -638,12 +745,12 @@
             jax.ShapeDtypeStruct(ids.shape, ids.dtype),
             jax.ShapeDtypeStruct((tokens, width), brain_type),
         ]
-        + [jax.ShapeDtypeStruct((8 * p.shape[0], 4 * p.shape[1]), p.dtype) for p, _ in pieces]
+        + [jax.ShapeDtypeStruct((width, 4 * u), brain_type) for _ in range(layers) for u in units]
         + [jax.ShapeDtypeStruct(*shape) for _ in range(layers) for shape in kept],
-        in_specs=hbm(4 + 2 * groups),
+        in_specs=hbm(10),
         out_specs=hbm(5 + groups + 8 * layers),
         scratch_shapes=[pltpu.VMEM(*shape) for shape in kept]
-        + [pltpu.VMEM((8 * p.shape[0], 4 * p.shape[1]), p.dtype) for p, _ in pieces[:4]]
+        + [pltpu.VMEM((width, 4 * u), brain_type) for u in units]
         + [
             pltpu.VMEM((tokens, width), brain_type),
             pltpu.VMEM((tokens, width), brain_type),
@@ -655,19 +762,34 @@
             pltpu.VMEM((2 * tokens, 128), float_type),
             pltpu.SemaphoreType.DMA((remote,)),
             pltpu.SemaphoreType.DMA((remote,)),
-            pltpu.SemaphoreType.DMA((2 * groups + 10 + 8 * layers,)),
+            pltpu.SemaphoreType.DMA((2 * groups + 10 + 12 * layers,)),
         ],
         compiler_params=pltpu.CompilerParams(
             collective_id=0, has_side_effects=True, vmem_limit_bytes=60 * 1024 * 1024
         ),
         name="forward",
-    )(inputs, cotangent, vectors, ids, *flat)
+    )(inputs, cotangent, vectors, ids, *raw)
     saved = [outs[5 + groups + 8 * i : 13 + groups + 8 * i] for i in range(layers)]
     return outs[1], outs[2], outs[3], outs[4], outs[5 : 5 + groups], saved
 
 
+def hand_out(move, clock, loaded, out, units):
+    n = units // len(out)
+    rows = pl.ds(0, loaded.shape[1] // 2)
+    lanes = pl.ds(pl.multiple_of(move.core * n, 128), n)
+    copies = []
+    for i, target in enumerate(out):
+        columns = pl.ds(i * n, n)
+        there = loaded.at[1 - move.core, rows, columns]
+        copies.append(move.send(there, target.at[:, lanes], move.sibling))
+        copies.append(move.keep(loaded.at[move.core, rows, columns], target.at[:, lanes]))
+    yield clock.post(units * 512, OVER_CORE) + 1.0
+    for copy in copies:
+        copy.wait()
+
+
 def collect_stages(move, clock, first, loaded, got, out, free, release):
-    first_got, second_got, far_got, near_got = got
+    first_got, second_got, far_got, cross_got, near_got = got
     rows, units = loaded.shape[1] // 2, loaded.shape[2] // 4
     sides = ((move.x_side, OVER_X), (move.y_side, OVER_Y))
     done = [copy for copy, _ in first]
@@ -692,45 +814,87 @@
         first[i][0].wait_recv()
         total(loaded.at[i], first_got.at[i], 2 * rows, 4 * units)
         second.append(go(loaded.at[i, pl.ds(rows, rows)], second_got.at[i], *sides[i]))
-    far = []
-    free("far")
+    free("near")
+    free("across")
+    base = move.remote
+    move.remote += 6
+    outer_lanes = pl.ds(2 * units, 2 * units)
+
+    def far(i):
+        source = loaded.at[i, pl.ds(0, rows), outer_lanes]
+        return move.make(source, far_got.at[i], move.z_near, base + i, base + i)
+
+    def cross(i):
+        source = loaded.at[i, pl.ds(0, rows), outer_lanes]
+        return move.make(source, cross_got.at[i], move.z_across, base + 2 + i, base + 2 + i)
+
+    def near(i):
+        source = loaded.at[i, pl.ds(0, rows), pl.ds(units, units)]
+        return move.make(source, near_got.at[i], move.z_near, base + 4 + i, base + 4 + i)
+
+    def lanes_total(i, source, pairs):
+        def body(step):
+            rows_here = at(step, 32)
+            for lane, to_lane in pairs:
+                span = (rows_here, pl.ds(to_lane * units, units))
+                loaded[(i, *span)] = (
+                    loaded[(i, *span)].astype(float_type)
+                    + source[i, rows_here, pl.ds(lane * units, units)].astype(float_type)
+                ).astype(brain_type)
+
+        loop(rows // 32, body)
+
+    far_due = []
     for i in range(2):
         yield second[i][1]
         second[i][0].wait_recv()
         total(loaded.at[i], second_got.at[i], rows, 4 * units)
-        far.append(
-            go(
-                loaded.at[i, pl.ds(0, rows), pl.ds(2 * units, 2 * units)],
-                far_got.at[i],
-                move.z_far,
-                OVER_FAR,
-            )
-        )
-    near = []
-    free("near")
+
+        @pl.when(move.outer)
+        def _():
+            far(i).start()
+            near(i).start()
+
+        far_due.append(clock.post(size_of(far_got.at[i]), OVER_NEAR))
+    cross_due = []
     for i in range(2):
-        yield far[i][1]
-        far[i][0].wait_recv()
-        total(loaded.at[i], far_got.at[i], rows, 2 * units)
-        near.append(
-            go(
-                loaded.at[i, pl.ds(0, rows), pl.ds(units, units)],
-                near_got.at[i],
-                move.z_near,
-                OVER_NEAR,
-            )
-        )
-    yield max(near[0][1], near[1][1])
+        yield far_due[i]
+
+        @pl.when(move.inner)
+        def _():
+            far(i).wait_recv()
+            lanes_total(i, far_got, ((0, 3), (1, 2)))
+            cross(i).start()
+
+        cross_due.append(clock.post(size_of(far_got.at[i]), OVER_MID))
+    near_due = []
     for i in range(2):
-        near[i][0].wait_recv()
-        total(loaded.at[i], near_got.at[i], rows, units)
+        yield cross_due[i]
+
+        @pl.when(move.inner)
+        def _():
+            cross(i).wait_recv()
+            lanes_total(i, cross_got, ((0, 1), (1, 0)))
+            near(i).start()
+
+        near_due.append(clock.post(size_of(near_got.at[i]), OVER_NEAR))
+    yield max(near_due)
+    for i in range(2):
+        near(i).wait()
+        lanes_total(i, near_got, ((0, 0),))
+
+    @pl.when(move.outer)
+    def _():
+        for i in range(2):
+            far(i).wait_send()
+
+    @pl.when(move.inner)
+    def _():
+        for i in range(2):
+            cross(i).wait_send()
+
     release()
-    ready = pl.ds(0, rows), pl.ds(0, units)
-    last, due = go(loaded.at[(1 - move.core, *ready)], out.at[1], move.sibling, OVER_CORE)
-    stay = move.keep(loaded.at[(move.core, *ready)], out.at[0])
-    yield due + 1.0
-    last.wait_recv()
-    stay.wait()
+    yield from hand_out(move, clock, loaded, out, units)
     for copy in done:
         copy.wait_send()
 
@@ -755,7 +919,7 @@
     yield due
     copy.wait()
     sums[1] = sums[0] + by_near[...]
-    copy, due = go(sums.at[1], by_far, move.z_far)
+    copy, due = go(sums.at[1], by_far, move.z_across)
     yield due
     copy.wait()
     out[...] = sums[1] + by_far[...]
@@ -1009,7 +1173,7 @@
         for kind in range(kinds):
             saved[layer][f"w{kind}"] = weights[kinds * layer + kind]
     block_out, below_out, vectors_out = take(3)
-    outs = take(groups)
+    outs = take(6)
     box = {"layers": saved}
     names = ("upper", "fc_in", "hid", "slope", "normed", "branch", "source", "grad", "below")
     box.update(zip(names, take(9)))
@@ -1017,10 +1181,10 @@
     box.update(zip(names, take(8)))
     own_ids, other_ids, box["vector_grads"] = take(3)
     small = take(6)
-    buffers = [take(6) for _ in range(kinds)]
+    buffers = [take(7) for _ in range(kinds)]
     (credits,) = take(1)
     move = Mover(*refs)
-    clock = Clock()
+    clock = Clock(SLACK)
     plan = Plan(clock)
     copies = [
         move.keep(cotangent, box["send"]),
@@ -1039,7 +1203,12 @@
         box["grad"][rows, :] = box["send"][rows, :].astype(float_type)
 
     loop(box["grad"].shape[0] // 64, body)
-    devices = {"x": move.x_side, "y": move.y_side, "far": move.z_far, "near": move.z_near}
+    devices = {
+        "x": move.x_side,
+        "y": move.y_side,
+        "across": move.z_across,
+        "near": move.z_near,
+    }
     order = list(devices)
     running = {}
 
@@ -1063,6 +1232,10 @@
                         device_id_type=pl.DeviceIdType.MESH,
                     )
 
+        out = [
+            ref.at[layer] for ref in (outs[:3], outs[3:4], outs[4:5], outs[5:6])[kind]
+        ]
+
         def go(side, link):
             name = "y" if side == 0 else "x"
             free(name)
@@ -1070,9 +1243,7 @@
             first[side] = (copy, clock.post(size_of(sent.at[side]), link))
 
         def begin():
-            task = collect_stages(
-                move, clock, first, loaded, got, outs[kinds * layer + kind], free, release
-            )
+            task = collect_stages(move, clock, first, loaded, got, out, free, release)
             plan.add(task)
             running[kind] = task
 
@@ -1106,22 +1277,23 @@
     scratch += [(small_vectors, high), (small_vectors[1:], high), (small_vectors[1:], high)]
     scratch += [((2, *small_vectors[2:]), high)] + [(small_vectors[2:], high)] * 3
     for wide in units:
-        for rows, columns in ((256, 1), (256, 1), (256, 1), (128, 1), (128, 2), (128, 4)):
+        for rows, columns in ((256, 1), (256, 1), (256, 1), (128, 1), (128, 2), (128, 2), (128, 4)):
             scratch.append(((2, rows, wide // columns), low))
-    remote = 12 * count + 9 + 4 * layers + 8
+    remote = 16 * count + 9 + 4 * layers + 8
     outs = pl.pallas_call(
         partial(backward_kernel, layers, score_scale),
         out_shape=[jax.ShapeDtypeStruct((2, tokens // 2, width), low)] * 2
         + [jax.ShapeDtypeStruct(vectors.shape[1:], high)]
-        + [jax.ShapeDtypeStruct((2, 128, w.shape[1] // 4), low) for w in weights],
+        + [jax.ShapeDtypeStruct((layers, 128, units[0] // 6), low)] * 3
+        + [jax.ShapeDtypeStruct((layers, 128, w // 2), low) for w in units[1:]],
         in_specs=hbm(5 + count + 8 * layers),
-        out_specs=hbm(2) + [pl.BlockSpec(memory_space=pltpu.VMEM)] + hbm(count),
+        out_specs=hbm(2) + [pl.BlockSpec(memory_space=pltpu.VMEM)] + hbm(6),
         scratch_shapes=[pltpu.VMEM(*shape) for shape in scratch]
         + [
             pltpu.SemaphoreType.REGULAR((16,)),
             pltpu.SemaphoreType.DMA((remote,)),
             pltpu.SemaphoreType.DMA((remote,)),
-            pltpu.SemaphoreType.DMA((8 + 14 * layers + count,)),
+            pltpu.SemaphoreType.DMA((8 + 14 * layers + 2 * count,)),
         ],
         compiler_params=pltpu.CompilerParams(
             collective_id=1, has_side_effects=True, vmem_limit_bytes=62 * 1024 * 1024
@@ -1149,29 +1321,13 @@
     layers = norm1_gain.shape[0]
     head_width = inputs.shape[3] // HEADS
     score_scale = 1.0 / math.sqrt(head_width)
-    core = lax.axis_index("dp") & 1
-
-    def halves(columns):
-        wide = columns.shape[1] // 2
-        low, high = columns[:, :wide], columns[:, wide:]
-        return pick(core, low, high), pick(core, high, low)
-
-    pieces = []
-    for layer in range(layers):
-        both = [halves(w[layer]) for w in (w_query, w_key, w_value)]
-        pieces += [
-            tuple(jnp.concatenate([b[side] for b in both], axis=1) for side in range(2)),
-            halves(w_output[layer].T),
-            halves(w_fc_in[layer]),
-            halves(w_fc_out[layer].T),
-        ]
     vectors = jnp.concatenate([norm1_gain, norm1_shift, norm2_gain, norm2_shift], axis=0)
     grad, vectors, other_ids, block, weights, saved = forward_all(
         inputs[:, 0],
         cotangent[:, 0],
         vectors.astype(float_type),
         segment_ids,
-        pieces,
+        (w_query, w_key, w_value, w_output.mT, w_fc_in, w_fc_out.mT),
         layers,
         score_scale,
     )
@@ -1179,23 +1335,8 @@
         block, grad, vectors, segment_ids, other_ids, weights, saved, layers, score_scale
     )
     block_output, input_grad = (part.astype(float_type) for part in tokens)
-    outs = [(pick(core, out[0], out[1]), pick(core, out[1], out[0])) for out in outs]
-
-    def joined(kind, columns=None):
-        per_layer = []
-        for layer in range(layers):
-            low, high = outs[4 * layer + kind]
-            if columns is not None:
-                low, high = low[:, columns], high[:, columns]
-            per_layer.append(jnp.concatenate([low, high], axis=1))
-        return jnp.stack(per_layer)
-
-    width = w_query.shape[2] // 2
-    grad_query, grad_key, grad_value = (joined(0, slice(i * width, (i + 1) * width)) for i in range(3))
-    grad_output = joined(1).transpose(0, 2, 1)
-    grad_fc_in = joined(2)
-    grad_fc_out = joined(3).transpose(0, 2, 1)
-
+    grad_query, grad_key, grad_value, grad_output, grad_fc_in, grad_fc_out = outs
+    grad_output, grad_fc_out = grad_output.mT, grad_fc_out.mT
     gain_one, shift_one, gain_two, shift_two = (
         vector_grads[i * layers : (i + 1) * layers] for i in range(4)
     )

time: 620 us -> 570 us (0.919)
  Pallas kernels: 590 us -> 542 us
    pallas_call x1, Pallas kernels: 285 us -> 260 us  [forward_all(): pl.pallas_call(partial(forward_kernel, groups, layers, score_scale), out_...]
    pallas_call x1, Pallas kernels: 305 us -> 282 us  [backward_all(): pl.pallas_call(partial(backward_kernel, layers, score_scale), out_shape=[...]
where the time goes in v4:
time: 570 us; the launch traced here: 563 us
  Pallas kernels  542 us (95%)
  other arithmetic  13 us (2%)
  local copies, waits for them, and re-layouts  7.26 us (1%)
    pallas_call x1, Pallas kernels, backward_all(): pl.pallas_call(partial(backward_kernel, layers, score_scale), out_shape=[...  282 us
    pallas_call x1, Pallas kernels, forward_all(): pl.pallas_call(partial(forward_kernel, groups, layers, score_scale), out_...  260 us

profile of v4, /device:TPU:0, one launch (start us, length us, event | category | flops | bytes accessed | tf_op | source)
XLA Modules:
  0.0 563.2 jit_solution(10132473856840770130)
XLA Ops:
  0.6 1.3 maximum_convert_fusion.refs_2_
  2.0 1.7 copy.25
  3.6 2.0 copy.26
  5.7 260.4 %forward.1 = (bf16[512,1024]{1,0:T(8,128)(2,1)}, bf16[512,1024]{1,0:T(8,128)(2,1)}, f32[8,8,128]{2,1,0:T(8,128)}, s32[2,1,1024]{2,1,0:T(1,128)}, bf16[512,1024]{...) custom-call(bf16[2,256,1024]{2,1,0:T(8,128)(2,1)} %bitcast.21, ...), custom_call_target="tpu_custom_call" | custom-call | tf_op jit(solution)/shard_map/forward/pallas_call | solution.py:739
  266.1 281.7 %backward.1 = (bf16[2,256,1024]{2,1,0:T(8,128)(2,1)}, bf16[2,256,1024]{2,1,0:T(8,128)(2,1)}, f32[8,128]{1,0:T(8,128)}, bf16[2,128,256]{2,1,0:T(8,128)(2,1)}, bf1...) custom-call(bf16[512,1024]{1,0:T(8,128)(2,1)} %get-tuple-element.49., ...), custom_call_target="tpu_custom_call" | custom-call | tf_op jit(solution)/shard_map/backward/pallas_call | solution.py:1283
  547.8 1.4 fusion
  549.2 1.6 convert_element_type.30
  550.8 1.6 convert_element_type.31
  552.4 1.6 convert_element_type.32
  554.1 0.0 copy-start
  554.1 0.0 copy-start.1
  554.1 1.1 convert_bitcast_fusion.1
  555.1 0.8 copy.29
  556.0 2.1 convert_element_type.35
  558.1 1.1 convert_bitcast_fusion
  559.2 1.3 copy.30
  560.6 0.0 copy-done
  560.6 0.0 copy-done.1
  560.6 2.5 bitcast_convert_fusion
Async XLA Ops:
  554.1 6.5 %copy-start = (bf16[2,256,1024]{2,1,0:T(8,128)(2,1)S(1)}, bf16[2,256,1024]{2,1,0:T(8,128)(2,1)}, u32[]{:S(2)}) copy-start(bf16[2,256,1024]{2,1,0:T(8,128)(2,1)} %get-tuple-element.77) | copy-start | bytes 3145732
  554.1 6.5 %copy-start.1 = (bf16[2,256,1024]{2,1,0:T(8,128)(2,1)S(1)}, bf16[2,256,1024]{2,1,0:T(8,128)(2,1)}, u32[]{:S(2)}) copy-start(bf16[2,256,1024]{2,1,0:T(8,128)(2,1)} %get-tuple-element.78) | copy-start | bytes 3145732

commit v5 on v4

--- a/solution.py
+++ b/solution.py
@@ -195,9 +195,10 @@
 
 PER_BYTE = 2.0 / 84e3
 LATENCY, SLACK = 2.0, 6.0
-BACKLOG = 4.0
+BACKLOG = 8.0
 Z_BACKLOG = 8.0
-TOKENS_AT = 8.0
+TOKENS_AT = 12.0
+SCALE = 1.3
 OVER_X, OVER_Y = (("x", 1.0),), (("y", 1.0),)
 OVER_NEAR, OVER_MID = (("z_out", 1.0),), (("z_mid", 1.0),)
 OVER_CORE = (("core", 0.1),)
@@ -225,7 +226,7 @@
         while any(task is other for _, other in self.tasks):
             self.step()
 
-    def run(self, compute, ready):
+    def run(self, compute, ready, scale=1.0):
         over = False
         while self.tasks or not over:
             if self.due() <= self.clock.now:
@@ -235,7 +236,7 @@
                 if cost is None:
                     over = True
                 else:
-                    self.clock.now += cost
+                    self.clock.now += scale * cost
             elif self.tasks:
                 self.step()
 
@@ -715,7 +716,7 @@
     def ready():
         return state["begun"] and (state["need"] is None or state["need"] in loads)
 
-    plan.run(forward_steps(move, score_scale, layers, box), ready)
+    plan.run(forward_steps(move, score_scale, layers, box), ready, SCALE)
     for finish in ends:
         finish()
 

time: 570 us -> 565 us (level)
  no operation moved by 1% of the time
where the time goes in v5:
time: 565 us; the launch traced here: 560 us
  Pallas kernels  538 us (95%)
  other arithmetic  13 us (2%)
  local copies, waits for them, and re-layouts  7.26 us (1%)
    pallas_call x1, Pallas kernels, backward_all(): pl.pallas_call(partial(backward_kernel, layers, score_scale), out_shape=[...  282 us
    pallas_call x1, Pallas kernels, forward_all(): pl.pallas_call(partial(forward_kernel, groups, layers, score_scale), out_...  256 us

profile of v5, /device:TPU:0, one launch (start us, length us, event | category | flops | bytes accessed | tf_op | source)
XLA Modules:
  0.0 559.5 jit_solution(16760187565775137672)
XLA Ops:
  0.6 1.3 maximum_convert_fusion.refs_2_
  2.0 1.7 copy.25
  3.6 2.0 copy.26
  5.7 256.2 %forward.1 = (bf16[512,1024]{1,0:T(8,128)(2,1)}, bf16[512,1024]{1,0:T(8,128)(2,1)}, f32[8,8,128]{2,1,0:T(8,128)}, s32[2,1,1024]{2,1,0:T(1,128)}, bf16[512,1024]{...) custom-call(bf16[2,256,1024]{2,1,0:T(8,128)(2,1)} %bitcast.21, ...), custom_call_target="tpu_custom_call" | custom-call | tf_op jit(solution)/shard_map/forward/pallas_call | solution.py:740
  261.9 282.2 %backward.1 = (bf16[2,256,1024]{2,1,0:T(8,128)(2,1)}, bf16[2,256,1024]{2,1,0:T(8,128)(2,1)}, f32[8,128]{1,0:T(8,128)}, bf16[2,128,256]{2,1,0:T(8,128)(2,1)}, bf1...) custom-call(bf16[512,1024]{1,0:T(8,128)(2,1)} %get-tuple-element.49., ...), custom_call_target="tpu_custom_call" | custom-call | tf_op jit(solution)/shard_map/backward/pallas_call | solution.py:1284
  544.1 1.4 fusion
  545.5 1.6 convert_element_type.30
  547.1 1.6 convert_element_type.31
  548.7 1.6 convert_element_type.32
  550.4 0.0 copy-start
  550.4 0.0 copy-start.1
  550.4 1.1 convert_bitcast_fusion.1
  551.4 0.8 copy.29
  552.3 2.1 convert_element_type.35
  554.4 1.1 convert_bitcast_fusion
  555.6 1.3 copy.30
  556.9 0.0 copy-done
  556.9 0.0 copy-done.1
  556.9 2.5 bitcast_convert_fusion
Async XLA Ops:
  550.4 6.5 %copy-start = (bf16[2,256,1024]{2,1,0:T(8,128)(2,1)S(1)}, bf16[2,256,1024]{2,1,0:T(8,128)(2,1)}, u32[]{:S(2)}) copy-start(bf16[2,256,1024]{2,1,0:T(8,128)(2,1)} %get-tuple-element.77) | copy-start | bytes 3145732
  550.4 6.5 %copy-start.1 = (bf16[2,256,1024]{2,1,0:T(8,128)(2,1)S(1)}, bf16[2,256,1024]{2,1,0:T(8,128)(2,1)}, u32[]{:S(2)}) copy-start(bf16[2,256,1024]{2,1,0:T(8,128)(2,1)} %get-tuple-element.78) | copy-start | bytes 3145732
